TPU v7x, 32 devices: a whole 2x2x4 slice. The times are simulated.
32 devices in a mesh: row: 4 (over x, core), col: 8 (over z, y).
Axes of the slice: x: 2, y: 2, z: 4, core: 2. Of those that a mesh axis runs over, the one named last changes fastest.
Arguments:
- strain: bfloat16 [32, 192000], P(('row', 'col')), may hold values from -500 to 500
- seg_offsets: int32 [32], replicated, may hold values from 0 to 186000, as said below
- band_bins: int32 [512], replicated, may hold values from 60 to 1083, as said below
Outputs:
- stacked: float32 [32, 4, 8, 2, 512], P('row', None, 'col')
Inputs may be any that keep to these rules, and one draw needn't show every extreme that they name: `seg_offsets`: segment 0 starts the record and the last segment ends it; each other segment s starts between s * 6000 - 6000 // 2 and s * 6000. `band_bins`: strictly increasing.
All inputs are finite; a program needn't handle non-finite values.
Results may differ from a plain program's by a relative error of at most 0.0064.
Values may be sent and summed in bfloat16 or wider, within the bound.
No kernel may reach another device: no remote copies, remote signals or barrier semaphores. Data moves between devices by JAX's collectives and lax.ppermute only.
A program may use at most 192 MiB of HBM per device.

v0:
```python
import math

import jax
import jax.numpy as jnp
from jax import lax
from jax.sharding import PartitionSpec as P

F = 512
SEGLEN = 6000
SEG = 32
NSUB = 5
TAPER = 32
SMOOTH = 64


def build_tables(band_bins):
    inner_len = SEGLEN // NSUB
    inner = jnp.arange(inner_len, dtype=jnp.int32)
    phase = inner[:, None] * band_bins[None, :] % SEGLEN
    angle = phase.astype(jnp.float32) * (2.0 * math.pi / SEGLEN)
    table = jnp.concatenate([jnp.cos(angle), -jnp.sin(angle)], axis=1).astype(jnp.bfloat16)
    outer = jnp.arange(NSUB, dtype=jnp.int32)
    outer_phase = outer[:, None] * (band_bins[None, :] * inner_len) % SEGLEN
    outer_angle = outer_phase.astype(jnp.float32) * (2.0 * math.pi / SEGLEN)
    twist_re = jnp.cos(outer_angle)
    twist_im = -jnp.sin(outer_angle)
    samples = jnp.arange(SEGLEN, dtype=jnp.float32)
    window = 0.5 - 0.5 * jnp.cos(samples * (2.0 * math.pi / SEGLEN))
    freq = jnp.arange(F, dtype=jnp.float32) + 0.5
    reach = jnp.minimum(jnp.minimum(freq, F - freq) / TAPER, 1.0)
    band_taper = jnp.square(jnp.sin(0.5 * math.pi * reach))
    lower = jnp.clip(jnp.arange(F, dtype=jnp.int32) - SMOOTH // 2, 0, F - SMOOTH)
    source = jnp.arange(F, dtype=jnp.int32)
    inside = (source[:, None] >= lower[None, :]) & (source[:, None] < lower[None, :] + SMOOTH)
    average = inside.astype(jnp.float32) / SMOOTH
    return (table, twist_re, twist_im, window, band_taper, average)


def taper_segments(records, seg_offsets, window):

    def one_segment(begin):
        return lax.dynamic_slice_in_dim(records, begin, SEGLEN, 1)

    segments = jax.vmap(one_segment)(seg_offsets)
    return (segments.astype(jnp.float32) * window).astype(jnp.bfloat16)


def spectra_of(tapered, tables):
    table, twist_re, twist_im, window, band_taper, average = tables
    count = tapered.shape[1]
    inner_len = SEGLEN // NSUB
    total_rows = SEG * count
    flattened = tapered.reshape(total_rows, NSUB, inner_len)
    spec_re = jnp.zeros((total_rows, F), jnp.float32)
    spec_im = jnp.zeros((total_rows, F), jnp.float32)
    for block in range(NSUB):
        part = jnp.dot(flattened[:, block, :], table, preferred_element_type=jnp.float32)
        part_re = part[:, :F]
        part_im = part[:, F:]
        spec_re = spec_re + part_re * twist_re[block] - part_im * twist_im[block]
        spec_im = spec_im + part_re * twist_im[block] + part_im * twist_re[block]
    power = spec_re * spec_re + spec_im * spec_im
    smooth = jnp.dot(power, average, precision=lax.Precision.HIGHEST)
    scale = band_taper * lax.rsqrt(smooth + 1e-06)
    whitened = jnp.concatenate([spec_re * scale, spec_im * scale], axis=1).astype(jnp.bfloat16)
    return whitened.reshape(SEG, count, 2 * F)


def segment_share(energy, channels):
    weights = 1.0 / (energy / (channels * SEGLEN) + 1e-06)
    return weights / jnp.sum(weights)


def cross_spectra(row_side, col_side, share):
    seg_count = row_side.shape[0]
    left_rows = row_side.shape[1]
    right_rows = col_side.shape[1]
    width = row_side.shape[2] // 2
    step_len = math.gcd(seg_count, 4)
    turns = seg_count // step_len

    def one_turn(turn, totals):
        real_sum, imag_sum = totals
        begin = turn * step_len
        left = lax.dynamic_slice_in_dim(row_side, begin, step_len, 0)
        right = lax.dynamic_slice_in_dim(col_side, begin, step_len, 0)
        weights = lax.dynamic_slice_in_dim(share, begin, step_len, 0)[:, None, None]
        left_re = left[:, :, :width].astype(jnp.float32) * weights
        left_im = left[:, :, width:].astype(jnp.float32) * weights
        right_re = right[:, :, :width].astype(jnp.float32)
        right_im = right[:, :, width:].astype(jnp.float32)
        real_term = (
            left_re[:, :, None, :] * right_re[:, None, :, :]
            + left_im[:, :, None, :] * right_im[:, None, :, :]
        )
        imag_term = (
            left_im[:, :, None, :] * right_re[:, None, :, :]
            - left_re[:, :, None, :] * right_im[:, None, :, :]
        )
        return (real_sum + jnp.sum(real_term, axis=0), imag_sum + jnp.sum(imag_term, axis=0))

    zeros = jnp.zeros((left_rows, right_rows, width), jnp.float32)
    real_sum, imag_sum = lax.fori_loop(0, turns, one_turn, (zeros, zeros))
    return jnp.stack([real_sum, imag_sum], axis=2)


def per_device(strain, seg_offsets, band_bins):
    tables = build_tables(band_bins)
    channels = lax.axis_size("row") * lax.axis_size("col")
    own_tapered = taper_segments(strain, seg_offsets, tables[3])
    local_energy = jnp.sum(jnp.square(own_tapered.astype(jnp.float32)), axis=(1, 2))
    energy = lax.psum(local_energy, ("row", "col"))
    share = segment_share(energy, channels)
    own_spectra = spectra_of(own_tapered, tables)
    row_side = lax.all_gather(own_spectra, "col", axis=1, tiled=True)
    col_side = lax.all_gather(own_spectra, "row", axis=1, tiled=True)
    stacked = cross_spectra(row_side, col_side, share)
    return stacked[:, :, None]


def solution(mesh):
    placed = (P(("row", "col"), None), P(), P())
    return jax.shard_map(
        per_device,
        mesh=mesh,
        in_specs=placed,
        out_specs=P("row", None, "col", None, None),
        check_vma=False,
    )
```

profile of v0, /device:TPU:0, one launch (start us, length us, event | category | flops | bytes accessed | tf_op | source)
XLA Modules:
  0.0 177.8 jit_solution(4520081052556448161)
XLA Ops:
  0.7 71.2 %while.17 = (s32[]{:T(128)}, bf16[1,192000]{1,0:T(2,128)(2,1)}, s32[32,2]{0,1:T(2,128)S(1)}, bf16[32,1,6000]{2,1,0:T(2,128)(2,1)S(1)}, s32[]{:T(128)}) while((s32[]{:T(128)}, bf16[1,192000]{1,0:T(2,128)(2,1)}, s32[32,2]{0,1:T(2,128)S(1)}, bf16[32,1,6000]{2,1,0:T(2,128)(2,1)S(1)}, s32[]{:T(128)}) %tuple.84), condition=%wide.while_cond, body=%wide.while_body.sunk | while | flops 2 | bytes 36161 | solution.py:42
  1.3 1.5 bitcast_dynamic-update-slice_fusion.2
  3.6 1.5 bitcast_dynamic-update-slice_fusion.2
  5.8 1.5 bitcast_dynamic-update-slice_fusion.2
  8.0 1.5 bitcast_dynamic-update-slice_fusion.2
  10.2 1.5 bitcast_dynamic-update-slice_fusion.2
  12.5 1.5 bitcast_dynamic-update-slice_fusion.2
  14.7 1.5 bitcast_dynamic-update-slice_fusion.2
  16.9 1.5 bitcast_dynamic-update-slice_fusion.2
  19.2 1.5 bitcast_dynamic-update-slice_fusion.2
  21.4 1.5 bitcast_dynamic-update-slice_fusion.2
  23.6 1.5 bitcast_dynamic-update-slice_fusion.2
  25.8 1.5 bitcast_dynamic-update-slice_fusion.2
  28.1 1.5 bitcast_dynamic-update-slice_fusion.2
  30.3 1.5 bitcast_dynamic-update-slice_fusion.2
  32.5 1.5 bitcast_dynamic-update-slice_fusion.2
  34.7 1.5 bitcast_dynamic-update-slice_fusion.2
  37.0 1.5 bitcast_dynamic-update-slice_fusion.2
  39.2 1.5 bitcast_dynamic-update-slice_fusion.2
  41.4 1.5 bitcast_dynamic-update-slice_fusion.2
  43.6 1.5 bitcast_dynamic-update-slice_fusion.2
  45.9 1.5 bitcast_dynamic-update-slice_fusion.2
  48.1 1.5 bitcast_dynamic-update-slice_fusion.2
  50.3 1.5 bitcast_dynamic-update-slice_fusion.2
  54.8 1.5 bitcast_dynamic-update-slice_fusion.2
  59.2 1.5 bitcast_dynamic-update-slice_fusion.2
  72.0 4.8 %fusion.13 = (f32[32]{0:T(128)S(1)}, f32[32,6000]{1,0:T(8,128)S(1)}) fusion(bf16[32,1,6000]{2,1,0:T(2,128)(2,1)S(1)} %get-tuple-element.124, f32[6000]{0:T(1024)S(1)} %multiply_subtract_fusion.2), kind=kLoop, calls=%fused_computation.37 | loop fusion | flops 1151968 | bytes 1176128 | tf_op jit(solution)/shard_map/reduce_sum | solution.py:111
  78.4 10.4 %cosine_convert_fusion = (bf16[1200,512]{1,0:T(8,128)(2,1)S(1)}, bf16[1200,512]{1,0:T(8,128)(2,1)S(1)}) fusion(s32[512]{0:T(512)S(1)} %copy-done), kind=kLoop, calls=%fused_computation.19 | loop fusion | flops 7372800 | bytes 2459648 | tf_op jit(solution)/shard_map/convert.5
  92.6 33.0 %all_gather.6 = bf16[32,8,1024]{2,0,1:T(8,128)(2,1)S(1)} all-gather(bf16[32,1,1024]{2,0,1:T(8,128)(2,1)S(1)} %pad_maximum_fusion.1), channel_id=1, replica_groups=mesh['row'=4,'col'=8] {'col'}, dimensions={1}, use_global_device_ids=true | all-gather | bytes 589824 | tf_op jit(solution)/shard_map/all_gather | solution.py:115
  125.6 5.8 %all_gather.7 = bf16[32,4,1024]{2,0,1:T(8,128)(2,1)S(1)} all-gather(bf16[32,1,1024]{2,0,1:T(8,128)(2,1)S(1)} %pad_maximum_fusion.1), channel_id=1, replica_groups=mesh['row'=4,'col'=8] {'row'}, dimensions={1}, use_global_device_ids=true | all-gather | bytes 327680 | tf_op jit(solution)/shard_map/all_gather | solution.py:116
  131.4 39.7 %psum.7 = f32[32]{0:T(128)S(1)} all-reduce(f32[32]{0:T(128)S(1)} %get-tuple-element.172), channel_id=1, replica_groups=mesh['row'=4,'col'=8] {'row','col'}, use_global_device_ids=true, to_apply=%region_1.2 | all-reduce | flops 32 | bytes 256 | tf_op jit(solution)/shard_map/psum | solution.py:112
  172.4 4.5 %while.18 = (s32[]{:T(128)}, f32[8,4,512]{2,0,1:T(8,128)S(1)}, f32[8,4,512]{2,0,1:T(8,128)S(1)}, bf16[32,8,1024]{2,0,1:T(8,128)(2,1)S(1)}, f32[32]{0:T(128)S(1)}...) while((s32[]{:T(128)}, f32[8,4,512]{2,0,1:T(8,128)S(1)}, ...), condition=%wide.region_6.7_spmd.clone, body=%wide.region_3.6_spmd.clone.sunk | while | flops 638984 | bytes 1212661 | solution.py:103
  (164 shorter events, 44.5 us)
Async XLA Ops:
  77.7 0.7 copy-start
where the time goes:
time: 180 us; the launch traced here: 178 us
  blocking collectives  78.5 us (44%)
  local copies, waits for them, and re-layouts  74.4 us (41%)
  other arithmetic  20.1 us (11%)
  matrix products  3.63 us (2%)
    gather x96, local copies, waits for them, and re-layouts  70.7 us
    psum x1, blocking collectives, per_device(): energy = lax.psum(local_energy, ('row', 'col'))  39.7 us
    all_gather x1, blocking collectives, per_device(): row_side = lax.all_gather(own_spectra, 'col', axis=1, tiled=True)  33 us
    another operation x1, other arithmetic  10.4 us
    all_gather x1, blocking collectives, per_device(): col_side = lax.all_gather(own_spectra, 'row', axis=1, tiled=True)  5.77 us
    reduce_sum x1, other arithmetic, per_device(): jnp.sum(jnp.square(own_tapered.astype(jnp.float32)), axis=(1, 2))  4.82 us

commit v1 on v0

v1 whole, which is shorter than its diff:
```python
import functools
import math

import jax
import jax.numpy as jnp
import numpy as np
from jax import lax
from jax.experimental import pallas as pl
from jax.experimental.pallas import tpu as pltpu
from jax.sharding import PartitionSpec as P

SEGLEN = 6000
TAPER = 32
SMOOTH = 64
EPS = 1e-06
LANES = 128
DEPTH = 256
EDGE = 16


def window_constants(rows):
    position = np.arange(rows * DEPTH, dtype=np.float64).reshape(rows, DEPTH)
    angle = 2.0 * math.pi / SEGLEN * position
    both = np.concatenate([0.5 * np.cos(angle), 0.5 * np.sin(angle)], axis=0)
    return both.astype(np.float32)


def ramp_constant(width):
    freq = np.arange(width, dtype=np.float64) + 0.5
    reach = np.minimum(np.minimum(freq, width - freq) / TAPER, 1.0)
    return np.square(np.sin(0.5 * math.pi * reach)).astype(np.float32)[None, :]


def transform_kernel(
    count, rows, width, offsets, strain, bins, trig, ramp, spectra, energy,
    record, shift, tapered, parts, table, waves,
):
    samples = strain.shape[1]
    chunk = LANES * 8 * 8
    begin = 0
    while begin < samples:
        size = min(chunk, samples - begin)
        part = strain[:, begin : begin + size].astype(jnp.float32)
        record[begin // LANES : (begin + size) // LANES, :] = part.reshape(size // LANES, LANES)
        begin += size
    tail = record.shape[0] - samples // LANES
    record[samples // LANES :, :] = jnp.zeros((tail, LANES), jnp.float32)

    mult_row = lax.broadcasted_iota(jnp.int32, (2 * EDGE + rows, 1), 0)
    mult = jnp.where(
        mult_row < EDGE,
        mult_row,
        jnp.where(mult_row < 2 * EDGE, (mult_row - EDGE) * EDGE, (mult_row - 2 * EDGE) * DEPTH),
    ).astype(jnp.float32)
    phase = mult * bins[...].reshape(1, width).astype(jnp.float32)
    turns = jnp.floor(phase * (1.0 / SEGLEN) + 0.5)
    angle = (phase - turns * SEGLEN) * (2.0 * math.pi / SEGLEN)
    waves[0] = jnp.cos(angle)
    waves[1] = jnp.sin(angle)
    tiles = width // LANES
    low_cos = waves[0, 0:EDGE, :]
    low_sin = waves[1, 0:EDGE, :]
    for high in range(DEPTH // EDGE):
        at = EDGE + high
        high_cos = waves[0, at : at + 1, :]
        high_sin = waves[1, at : at + 1, :]
        real = high_cos * low_cos - high_sin * low_sin
        imag = -(high_sin * low_cos + high_cos * low_sin)
        for tile in range(tiles):
            cut = slice(tile * LANES, (tile + 1) * LANES)
            to = 2 * tile * LANES
            here = slice(high * EDGE, (high + 1) * EDGE)
            table[here, to : to + LANES] = real[:, cut].astype(jnp.bfloat16)
            table[here, to + LANES : to + 2 * LANES] = imag[:, cut].astype(jnp.bfloat16)

    for s in range(count):
        inside = (offsets[s] & (LANES - 1)).astype(jnp.float32)
        shift[0, s : s + 1, :] = jnp.full((1, LANES), inside, jnp.float32)
    turn = shift[0] * (2.0 * math.pi / SEGLEN)
    shift[1] = jnp.cos(turn)
    shift[2] = jnp.sin(turn)
    place = (
        lax.broadcasted_iota(jnp.int32, (8, LANES), 0) * DEPTH
        + lax.broadcasted_iota(jnp.int32, (8, LANES), 1)
    ).astype(jnp.float32)
    for s in range(count):
        first = offsets[s] // LANES
        moved = place - shift[0, s : s + 1, :]
        turn_cos = shift[1, s : s + 1, :]
        turn_sin = shift[2, s : s + 1, :]
        total = jnp.zeros((8, LANES), jnp.float32)
        for group in range(rows // 8):
            for half in range(DEPTH // LANES):
                block = record[pl.ds(first + half + 16 * group, 8, stride=2), :]
                lanes = slice(half * LANES, (half + 1) * LANES)
                wave_cos = trig[group * 8 : group * 8 + 8, lanes]
                wave_sin = trig[rows + group * 8 : rows + group * 8 + 8, lanes]
                window = 0.5 - (wave_cos * turn_cos + wave_sin * turn_sin)
                value = block * window
                sample = group * 8 * DEPTH + half * LANES
                if group == 0 and half == 0:
                    value = jnp.where(moved > -0.5, value, 0.0)
                if (group + 1) * 8 * DEPTH > SEGLEN - DEPTH:
                    value = jnp.where(moved < SEGLEN - sample - 0.5, value, 0.0)
                value = value.astype(jnp.bfloat16).astype(jnp.float32)
                total = total + value * value
                tapered[half, pl.ds(s + group * 8 * count, 8, stride=count), :] = value
        energy[s : s + 1, :] = jnp.sum(total, axis=0, keepdims=True)

    left = jnp.concatenate(
        [tapered[half].astype(jnp.bfloat16) for half in range(DEPTH // LANES)], axis=1
    )
    for tile in range(tiles):
        cut = slice(tile * LANES, (tile + 1) * LANES)
        to = 2 * tile * LANES
        product = jnp.dot(left, table[:, to : to + 2 * LANES], preferred_element_type=jnp.float32)
        real = jnp.zeros((count, LANES), jnp.float32)
        imag = jnp.zeros((count, LANES), jnp.float32)
        for r in range(rows):
            part = product[r * count : (r + 1) * count, :]
            twist_re = waves[0, 2 * EDGE + r : 2 * EDGE + r + 1, cut]
            twist_im = -waves[1, 2 * EDGE + r : 2 * EDGE + r + 1, cut]
            part_re, part_im = part[:, :LANES], part[:, LANES:]
            real = real + (part_re * twist_re - part_im * twist_im)
            imag = imag + (part_re * twist_im + part_im * twist_re)
        parts[0, :, cut] = real
        parts[1, :, cut] = imag
    real, imag = parts[0], parts[1]
    summed = real * real + imag * imag
    reach = 1
    while reach < SMOOTH:
        summed = summed + pltpu.roll(summed, width - reach, 1)
        reach *= 2
    lane = lax.broadcasted_iota(jnp.int32, (count, width), 1)
    middle = pltpu.roll(summed, SMOOTH // 2, 1)
    middle = jnp.where(lane < SMOOTH // 2, summed[:, 0:1], middle)
    last = width - SMOOTH
    middle = jnp.where(lane >= last + SMOOTH // 2, summed[:, last : last + 1], middle)
    scale = ramp[...] * lax.rsqrt(middle * (1.0 / SMOOTH) + EPS)
    spectra[:, 0:width] = (real * scale).astype(jnp.bfloat16)
    spectra[:, width:] = (imag * scale).astype(jnp.bfloat16)


def transform(strain, offsets, bins):
    count, width = offsets.shape[0], bins.shape[0]
    samples = strain.shape[1]
    rows = -(-(SEGLEN + LANES - 1) // DEPTH)
    lines = -(-(samples // LANES + 2) // 8) * 8
    vmem = pl.BlockSpec(memory_space=pltpu.VMEM)
    return pl.pallas_call(
        functools.partial(transform_kernel, count, rows, width),
        out_shape=[
            jax.ShapeDtypeStruct((count, 2 * width), jnp.bfloat16),
            jax.ShapeDtypeStruct((count, LANES), jnp.float32),
        ],
        in_specs=[pl.BlockSpec(memory_space=pltpu.SMEM)] + [vmem] * 4,
        out_specs=[vmem, vmem],
        scratch_shapes=[
            pltpu.VMEM((lines, LANES), jnp.float32),
            pltpu.VMEM((3, count, LANES), jnp.float32),
            pltpu.VMEM((DEPTH // LANES, rows * count, LANES), jnp.float32),
            pltpu.VMEM((2, count, width), jnp.float32),
            pltpu.VMEM((DEPTH, 2 * width), jnp.bfloat16),
            pltpu.VMEM((2, 2 * EDGE + rows, width), jnp.float32),
        ],
        compiler_params=pltpu.CompilerParams(vmem_limit_bytes=40 << 20),
        name="transform",
    )(offsets, strain, bins, window_constants(rows), ramp_constant(width))


def cross_kernel(left_count, right_count, places, share, *refs):
    left, right = refs[:left_count], refs[left_count : left_count + right_count]
    out = refs[-1]
    count = share.shape[0]
    width = left[0].shape[1] // 2
    for tile in range(width // LANES):
        cut = slice(tile * LANES, (tile + 1) * LANES)
        cut_im = slice(width + tile * LANES, width + (tile + 1) * LANES)
        rights = [
            (ref[:, cut].astype(jnp.float32), ref[:, cut_im].astype(jnp.float32)) for ref in right
        ]
        for i, ref in enumerate(left):
            left_re = ref[:, cut].astype(jnp.float32) * share[...]
            left_im = ref[:, cut_im].astype(jnp.float32) * share[...]
            for j, (right_re, right_im) in enumerate(rights):
                real = left_re * right_re + left_im * right_im
                imag = left_im * right_re - left_re * right_im
                at = places[i], places[left_count + j]
                out[at[0], at[1], 0, 0:1, cut] = jnp.sum(real, axis=0, keepdims=True)
                out[at[0], at[1], 0, 1:2, cut] = jnp.sum(imag, axis=0, keepdims=True)


def cross(places, share, left, right):
    width = left[0].shape[1] // 2
    vmem = pl.BlockSpec(memory_space=pltpu.VMEM)
    return pl.pallas_call(
        functools.partial(cross_kernel, len(left), len(right)),
        out_shape=jax.ShapeDtypeStruct((len(left), len(right), 1, 2, width), jnp.float32),
        in_specs=[pl.BlockSpec(memory_space=pltpu.SMEM)] + [vmem] * (1 + len(left) + len(right)),
        out_specs=vmem,
        compiler_params=pltpu.CompilerParams(vmem_limit_bytes=40 << 20),
        name="cross",
    )(places, share, *left, *right)


def partners(size):
    if size & (size - 1) == 0:
        return [lambda p, k=k: p ^ k for k in range(size)]
    return [lambda p, k=k: (p - k) % size for k in range(size)]


def exchange(x, axis, size):
    out = []
    for source in partners(size)[1:]:
        pairs = [(source(p), p) for p in range(size)]
        out.append(lax.ppermute(x, axis, pairs))
    return out


def per_device(strain, offsets, bins):
    row_size, col_size = lax.axis_size("row"), lax.axis_size("col")
    spectra, partial = transform(strain, offsets, bins)
    own = jnp.sum(partial, axis=1)
    energy = lax.psum(own, ("row", "col"))
    weight = 1.0 / (energy / (row_size * col_size * SEGLEN) + EPS)
    share = weight / jnp.sum(weight)
    share = jnp.broadcast_to(share[:, None], (share.shape[0], LANES))
    row, col = lax.axis_index("row"), lax.axis_index("col")
    left = [spectra] + exchange(spectra, "col", col_size)
    right = [spectra] + exchange(spectra, "row", row_size)
    places = jnp.stack(
        [f(col) for f in partners(col_size)] + [f(row) for f in partners(row_size)]
    ).astype(jnp.int32)
    return cross(places, share, left, right)


def solution(mesh):
    placed = (P(("row", "col"), None), P(), P())
    return jax.shard_map(
        per_device,
        mesh=mesh,
        in_specs=placed,
        out_specs=P("row", None, "col", None, None),
        check_vma=False,
    )
```

time: 180 us -> 69.1 us (0.38); the launches traced: 178 us -> 68.8 us
  local copies, waits for them, and re-layouts: 74.4 us -> 4.1 us
  blocking collectives: 78.5 us -> 38.9 us
  other arithmetic: 20.1 us -> 1.37 us
  starting transfers between devices: 0 us -> 16.5 us
  Pallas kernels: 0 us -> 5.17 us
  matrix products: 3.63 us -> 0 us
  waiting for transfers between devices: 0 us -> 2.69 us
    gather x96 -> x0, local copies, waits for them, and re-layouts: 70.7 us -> none
    all_gather x2 -> x0, blocking collectives: 38.8 us -> none  [the longest x1 33 us: per_device(): row_side = lax.all_gather(own_spectra, 'col', axis=1, tiled=True)]
    ppermute x0 -> x10, starting transfers between devices: none -> 16.5 us  [exchange(): out.append(lax.ppermute(x, axis, pairs))]
    another operation x1 -> x0, other arithmetic: 10.4 us -> none
    reduce_sum x10 -> x2, other arithmetic: 5.98 us -> 0.72 us  [the longest x1 0.61 us: per_device(): share = weight / jnp.sum(weight)]
    pallas_call x0 -> x2, Pallas kernels: none -> 5.17 us  [the longest x1 3.15 us: transform(): pl.pallas_call(functools.partial(transform_kernel, count, rows, width), o...]
    unnamed x2 -> x10, local copies, waits for them, and re-layouts: 0.07 us -> 3.94 us
    dot_general x6 -> x0, matrix products: 3.63 us -> none  [the longest x5 2.63 us: spectra_of(): jnp.dot(flattened[:, block, :], table, preferred_element_type=jnp.float32)]
  transfers between devices with their start and end apart: 0 -> 10, of which waited for: 0 -> 4; matrix products, arithmetic and copies ran while one was open for 0% -> 2% of each run, Pallas kernels for 0% -> 0%
where the time goes in v1:
time: 69.1 us; the launch traced here: 68.8 us
  blocking collectives  38.9 us (56%)
  starting transfers between devices  16.5 us (24%)
  Pallas kernels  5.17 us (7%)
  local copies, waits for them, and re-layouts  4.1 us (6%)
  waiting for transfers between devices  2.69 us (4%)
  other arithmetic  1.37 us (2%)
    psum x1, blocking collectives, per_device(): energy = lax.psum(own, ('row', 'col'))  38.9 us
    ppermute x10, starting transfers between devices, exchange(): out.append(lax.ppermute(x, axis, pairs))  16.5 us
    unnamed x10, local copies, waits for them, and re-layouts  3.94 us
    pallas_call x1, Pallas kernels, transform(): pl.pallas_call(functools.partial(transform_kernel, count, rows, width), o...  3.15 us
    ppermute x10, waiting for transfers between devices, exchange(): out.append(lax.ppermute(x, axis, pairs))  2.69 us
    pallas_call x1, Pallas kernels, cross(): pl.pallas_call(functools.partial(cross_kernel, len(left), len(right)), ou...  2.03 us
  transfers between devices with their start and end apart: 10, of which 4 were waited for; matrix products, arithmetic and copies ran while one was open for 2% of the time, Pallas kernels for 0%

profile of v1, /device:TPU:0, one launch (start us, length us, event | category | flops | bytes accessed | tf_op | source)
XLA Modules:
  0.0 68.8 jit_solution(7057680973888792163)
XLA Ops:
  0.0 0.7 copy-done.3
  0.7 1.1 %copy-done = bf16[1,192000]{1,0:T(2,128)(2,1)S(1)} copy-done((bf16[1,192000]{1,0:T(2,128)(2,1)S(1)}, bf16[1,192000]{1,0:T(2,128)(2,1)}, u32[]{:S(2)}) %copy-start) | copy-done | bytes 384024
  1.8 0.8 %copy-done.1 = f32[48,256]{1,0:T(8,128)S(1)} copy-done((f32[48,256]{1,0:T(8,128)S(1)}, f32[48,256]{1,0:T(8,128)}, u32[]{:S(2)}) %copy-start.1) | copy-done | bytes 49176
  2.6 0.7 copy-done.2
  3.3 0.7 copy-done.4
  3.9 3.1 %transform.1 = (bf16[32,1024]{1,0:T(8,128)(2,1)S(1)}, f32[32,128]{1,0:T(8,128)S(1)}) custom-call(s32[32]{0:T(128)S(1)} %copy-done.4, bf16[1,192000]{1,0:T(2,128)(2,1)S(1)} %copy-done, s32[512]{0:T(512)S(1)} %copy-done.2, f32[48,256]{1,0:T(8,128)S(1)} %copy-done.1, f32[1,512]{1,0:T(1,128)S(1)} %copy-done.3), custom_call_target="tpu_custom_call" | custom-call | tf_op jit(solution)/shard_map/transform/pallas_call | solution.py:150
  7.1 2.4 %collective-permute-start.9 = (bf16[32,1024]{1,0:T(8,128)(2,1)S(1)}, bf16[32,1024]{1,0:T(8,128)(2,1)S(1)}, u32[]{:S(2)}, u32[]{:S(2)}) collective-permute-start(bf16[32,1024]{1,0:T(8,128)(2,1)S(1)} %get-tuple-element.8.refs_0_.refs_8_), channel_id=1, source_target_pairs={{24,0},{16,8},{8,16},{0,24},{25,1},{17,9},{9,17},{1,25},{26,2},{18... | collective-permute-start | bytes 196616 | tf_op jit(solution)/shard_map/ppermute | solution.py:216
  9.5 0.6 collective-permute-start.8
  10.2 0.0 collective-permute-start.7
  10.2 4.8 %collective-permute-start.6 = (bf16[32,1024]{1,0:T(8,128)(2,1)S(1)}, bf16[32,1024]{1,0:T(8,128)(2,1)S(1)}, u32[]{:S(2)}, u32[]{:S(2)}) collective-permute-start(bf16[32,1024]{1,0:T(8,128)(2,1)S(1)} %get-tuple-element.8.refs_0_.refs_8_), channel_id=1, source_target_pairs={{7,0},{6,1},{5,2},{4,3},{3,4},{2,5},{1,6},{0,7},{15,8},{14,9},{13,... | collective-permute-start | bytes 196616 | tf_op jit(solution)/shard_map/ppermute | solution.py:216
  15.0 0.1 reduce_sum.18
  15.1 0.3 collective-permute-start.5
  15.4 38.9 %psum.7 = f32[32]{0:T(128)S(1)} all-reduce(f32[32]{0:T(128)S(1)} %reduce_sum.18), channel_id=1, replica_groups=mesh['row'=4,'col'=8] {'row','col'}, use_global_device_ids=true, to_apply=%region_1.0 | all-reduce | flops 32 | bytes 256 | tf_op jit(solution)/shard_map/psum | solution.py:224
  54.3 0.6 divide_reduce_fusion
  54.9 0.0 collective-permute-done.9.refs_11_
  54.9 4.7 %collective-permute-start.4 = (bf16[32,1024]{1,0:T(8,128)(2,1)S(1)}, bf16[32,1024]{1,0:T(8,128)(2,1)S(1)}, u32[]{:S(2)}, u32[]{:S(2)}) collective-permute-start(bf16[32,1024]{1,0:T(8,128)(2,1)S(1)} %get-tuple-element.8.refs_0_.refs_8_), channel_id=1, source_target_pairs={{5,0},{4,1},{7,2},{6,3},{1,4},{0,5},{3,6},{2,7},{13,8},{12,9},{15,... | collective-permute-start | bytes 196616 | tf_op jit(solution)/shard_map/ppermute | solution.py:216
  59.6 0.0 collective-permute-done.8.refs_10_
  59.6 0.0 collective-permute-start.3
  59.6 1.3 %collective-permute-start.2 = (bf16[32,1024]{1,0:T(8,128)(2,1)S(1)}, bf16[32,1024]{1,0:T(8,128)(2,1)S(1)}, u32[]{:S(2)}, u32[]{:S(2)}) collective-permute-start(bf16[32,1024]{1,0:T(8,128)(2,1)S(1)} %get-tuple-element.8.refs_0_.refs_8_), channel_id=1, source_target_pairs={{3,0},{2,1},{1,2},{0,3},{7,4},{6,5},{5,6},{4,7},{11,8},{10,9},{9,1... | collective-permute-start | bytes 196616 | tf_op jit(solution)/shard_map/ppermute | solution.py:216
  60.9 0.0 collective-permute-done.6.refs_7_
  60.9 0.9 %collective-permute-start.1 = (bf16[32,1024]{1,0:T(8,128)(2,1)S(1)}, bf16[32,1024]{1,0:T(8,128)(2,1)S(1)}, u32[]{:S(2)}, u32[]{:S(2)}) collective-permute-start(bf16[32,1024]{1,0:T(8,128)(2,1)S(1)} %get-tuple-element.8.refs_0_.refs_8_), channel_id=1, source_target_pairs={{2,0},{3,1},{0,2},{1,3},{6,4},{7,5},{4,6},{5,7},{10,8},{11,9},{8,1... | collective-permute-start | bytes 196616 | tf_op jit(solution)/shard_map/ppermute | solution.py:216
  61.8 0.0 collective-permute-done.5.refs_6_
  61.8 1.5 %collective-permute-start = (bf16[32,1024]{1,0:T(8,128)(2,1)S(1)}, bf16[32,1024]{1,0:T(8,128)(2,1)S(1)}, u32[]{:S(2)}, u32[]{:S(2)}) collective-permute-start(bf16[32,1024]{1,0:T(8,128)(2,1)S(1)} %get-tuple-element.8.refs_0_.refs_8_), channel_id=1, source_target_pairs={{1,0},{0,1},{3,2},{2,3},{5,4},{4,5},{7,6},{6,7},{9,8},{8,9},{11,10... | collective-permute-start | bytes 196616 | tf_op jit(solution)/shard_map/ppermute | solution.py:216
  63.2 0.7 multiply_divide_fusion
  63.9 0.1 stack.51.places
  64.0 0.5 collective-permute-done.4.refs_5_
  64.5 1.2 %collective-permute-done.3.refs_4_ = bf16[32,1024]{1,0:T(8,128)(2,1)S(1)} collective-permute-done((bf16[32,1024]{1,0:T(8,128)(2,1)S(1)}, bf16[32,1024]{1,0:T(8,128)(2,1)S(1)}, u32[]{:S(2)}, u32[]{:S(2)}) %collective-permute-start.3) | collective-permute-done | bytes 65568 | tf_op jit(solution)/shard_map/ppermute | solution.py:216
  65.7 0.9 %collective-permute-done.2.refs_3_ = bf16[32,1024]{1,0:T(8,128)(2,1)S(1)} collective-permute-done((bf16[32,1024]{1,0:T(8,128)(2,1)S(1)}, bf16[32,1024]{1,0:T(8,128)(2,1)S(1)}, u32[]{:S(2)}, u32[]{:S(2)}) %collective-permute-start.2) | collective-permute-done | bytes 65568 | tf_op jit(solution)/shard_map/ppermute | solution.py:216
  66.6 0.0 collective-permute-done.1.refs_2_
  66.6 0.1 collective-permute-done.refs_1_
  66.7 0.1 broadcast_in_dim.2.share
  66.7 2.0 %cross.1 = f32[8,4,1,2,512]{4,3,2,1,0:T(2,128)} custom-call(s32[12]{0:T(128)S(1)} %stack.51.places, f32[32,128]{1,0:T(8,128)S(1)} %broadcast_in_dim.2.share, bf16[32,1024]{1,0:T(8,128)(2,1)S(1)} %get-tuple-element.8.refs_0_.refs_8_, bf16[32,1024]{1,0:T(8,128)(2,1)S(1)} %collective-permute-done.refs_1_, bf16[32,1024]{1,0:T(8,128)(2,1)S(1)} %collective-permute-done.1.refs_2_, ...), custom_call_target="tpu_custom_call" | custom-call | tf_op jit(solution)/shard_map/cross/pallas_call | solution.py:196
  (6 shorter events, 0.0 us)
Async XLA Ops:
  0.0 0.7 copy-start.3
  0.7 1.1 %copy-start = (bf16[1,192000]{1,0:T(2,128)(2,1)S(1)}, bf16[1,192000]{1,0:T(2,128)(2,1)}, u32[]{:S(2)}) copy-start(bf16[1,192000]{1,0:T(2,128)(2,1)} %strain.1) | copy-start | bytes 1152004
  1.8 0.8 %copy-start.1 = (f32[48,256]{1,0:T(8,128)S(1)}, f32[48,256]{1,0:T(8,128)}, u32[]{:S(2)}) copy-start(f32[48,256]{1,0:T(8,128)} %constant.35.clone.trig) | copy-start | bytes 147460
  2.6 0.7 copy-start.2
  3.3 0.7 copy-start.4
  7.1 47.8 %collective-permute-start.9 = (bf16[32,1024]{1,0:T(8,128)(2,1)S(1)}, bf16[32,1024]{1,0:T(8,128)(2,1)S(1)}, u32[]{:S(2)}, u32[]{:S(2)}) collective-permute-start(bf16[32,1024]{1,0:T(8,128)(2,1)S(1)} %get-tuple-element.8.refs_0_.refs_8_), channel_id=1, source_target_pairs={{24,0},{16,8},{8,16},{0,24},{25,1},{17,9},{9,17},{1,25},{26,2},{18... | collective-permute-start | bytes 196616 | tf_op jit(solution)/shard_map/ppermute | solution.py:216
  9.5 50.0 %collective-permute-start.8 = (bf16[32,1024]{1,0:T(8,128)(2,1)S(1)}, bf16[32,1024]{1,0:T(8,128)(2,1)S(1)}, u32[]{:S(2)}, u32[]{:S(2)}) collective-permute-start(bf16[32,1024]{1,0:T(8,128)(2,1)S(1)} %get-tuple-element.8.refs_0_.refs_8_), channel_id=1, source_target_pairs={{16,0},{24,8},{0,16},{8,24},{17,1},{25,9},{1,17},{9,25},{18,2},{26... | collective-permute-start | bytes 196616 | tf_op jit(solution)/shard_map/ppermute | solution.py:216
  10.2 49.4 %collective-permute-start.7 = (bf16[32,1024]{1,0:T(8,128)(2,1)S(1)}, bf16[32,1024]{1,0:T(8,128)(2,1)S(1)}, u32[]{:S(2)}, u32[]{:S(2)}) collective-permute-start(bf16[32,1024]{1,0:T(8,128)(2,1)S(1)} %get-tuple-element.8.refs_0_.refs_8_), channel_id=1, source_target_pairs={{8,0},{0,8},{24,16},{16,24},{9,1},{1,9},{25,17},{17,25},{10,2},{2,... | collective-permute-start | bytes 196616 | tf_op jit(solution)/shard_map/ppermute | solution.py:216
  10.2 50.7 %collective-permute-start.6 = (bf16[32,1024]{1,0:T(8,128)(2,1)S(1)}, bf16[32,1024]{1,0:T(8,128)(2,1)S(1)}, u32[]{:S(2)}, u32[]{:S(2)}) collective-permute-start(bf16[32,1024]{1,0:T(8,128)(2,1)S(1)} %get-tuple-element.8.refs_0_.refs_8_), channel_id=1, source_target_pairs={{7,0},{6,1},{5,2},{4,3},{3,4},{2,5},{1,6},{0,7},{15,8},{14,9},{13,... | collective-permute-start | bytes 196616 | tf_op jit(solution)/shard_map/ppermute | solution.py:216
  15.1 46.6 %collective-permute-start.5 = (bf16[32,1024]{1,0:T(8,128)(2,1)S(1)}, bf16[32,1024]{1,0:T(8,128)(2,1)S(1)}, u32[]{:S(2)}, u32[]{:S(2)}) collective-permute-start(bf16[32,1024]{1,0:T(8,128)(2,1)S(1)} %get-tuple-element.8.refs_0_.refs_8_), channel_id=1, source_target_pairs={{6,0},{7,1},{4,2},{5,3},{2,4},{3,5},{0,6},{1,7},{14,8},{15,9},{12,... | collective-permute-start | bytes 196616 | tf_op jit(solution)/shard_map/ppermute | solution.py:216
  54.9 9.6 %collective-permute-start.4 = (bf16[32,1024]{1,0:T(8,128)(2,1)S(1)}, bf16[32,1024]{1,0:T(8,128)(2,1)S(1)}, u32[]{:S(2)}, u32[]{:S(2)}) collective-permute-start(bf16[32,1024]{1,0:T(8,128)(2,1)S(1)} %get-tuple-element.8.refs_0_.refs_8_), channel_id=1, source_target_pairs={{5,0},{4,1},{7,2},{6,3},{1,4},{0,5},{3,6},{2,7},{13,8},{12,9},{15,... | collective-permute-start | bytes 196616 | tf_op jit(solution)/shard_map/ppermute | solution.py:216
  59.6 6.2 %collective-permute-start.3 = (bf16[32,1024]{1,0:T(8,128)(2,1)S(1)}, bf16[32,1024]{1,0:T(8,128)(2,1)S(1)}, u32[]{:S(2)}, u32[]{:S(2)}) collective-permute-start(bf16[32,1024]{1,0:T(8,128)(2,1)S(1)} %get-tuple-element.8.refs_0_.refs_8_), channel_id=1, source_target_pairs={{4,0},{5,1},{6,2},{7,3},{0,4},{1,5},{2,6},{3,7},{12,8},{13,9},{14,... | collective-permute-start | bytes 196616 | tf_op jit(solution)/shard_map/ppermute | solution.py:216
  59.6 7.0 %collective-permute-start.2 = (bf16[32,1024]{1,0:T(8,128)(2,1)S(1)}, bf16[32,1024]{1,0:T(8,128)(2,1)S(1)}, u32[]{:S(2)}, u32[]{:S(2)}) collective-permute-start(bf16[32,1024]{1,0:T(8,128)(2,1)S(1)} %get-tuple-element.8.refs_0_.refs_8_), channel_id=1, source_target_pairs={{3,0},{2,1},{1,2},{0,3},{7,4},{6,5},{5,6},{4,7},{11,8},{10,9},{9,1... | collective-permute-start | bytes 196616 | tf_op jit(solution)/shard_map/ppermute | solution.py:216
  60.9 5.7 %collective-permute-start.1 = (bf16[32,1024]{1,0:T(8,128)(2,1)S(1)}, bf16[32,1024]{1,0:T(8,128)(2,1)S(1)}, u32[]{:S(2)}, u32[]{:S(2)}) collective-permute-start(bf16[32,1024]{1,0:T(8,128)(2,1)S(1)} %get-tuple-element.8.refs_0_.refs_8_), channel_id=1, source_target_pairs={{2,0},{3,1},{0,2},{1,3},{6,4},{7,5},{4,6},{5,7},{10,8},{11,9},{8,1... | collective-permute-start | bytes 196616 | tf_op jit(solution)/shard_map/ppermute | solution.py:216
  61.8 4.9 %collective-permute-start = (bf16[32,1024]{1,0:T(8,128)(2,1)S(1)}, bf16[32,1024]{1,0:T(8,128)(2,1)S(1)}, u32[]{:S(2)}, u32[]{:S(2)}) collective-permute-start(bf16[32,1024]{1,0:T(8,128)(2,1)S(1)} %get-tuple-element.8.refs_0_.refs_8_), channel_id=1, source_target_pairs={{1,0},{0,1},{3,2},{2,3},{5,4},{4,5},{7,6},{6,7},{9,8},{8,9},{11,10... | collective-permute-start | bytes 196616 | tf_op jit(solution)/shard_map/ppermute | solution.py:216

commit v2 on v1

v2 whole, which is shorter than its diff:
```python
import functools
import math

import jax
import jax.numpy as jnp
import numpy as np
from jax import lax
from jax.experimental import pallas as pl
from jax.experimental.pallas import tpu as pltpu
from jax.sharding import Mesh
from jax.sharding import PartitionSpec as P

SEGLEN = 6000
TAPER = 32
SMOOTH = 64
EPS = 1e-06
LANES = 128
DEPTH = 256
VMEM_LIMIT = 58 << 20
CROSS_VMEM = 16 << 20
EXTRA = 16
PIECES = 3
EDGE = 16


def window_constants(rows):
    position = np.arange(rows * DEPTH, dtype=np.float64).reshape(rows, DEPTH)
    angle = 2.0 * math.pi / SEGLEN * position
    both = np.concatenate([0.5 * np.cos(angle), 0.5 * np.sin(angle)], axis=0)
    return both.astype(np.float32)


def ramp_constant(width):
    freq = np.arange(width, dtype=np.float64) + 0.5
    reach = np.minimum(np.minimum(freq, width - freq) / TAPER, 1.0)
    return np.square(np.sin(0.5 * math.pi * reach)).astype(np.float32)[None, :]


def transform_kernel(
    count, rows, width, offsets_hbm, strain_hbm, bins_hbm, trig_hbm, ramp_hbm, payload,
    offsets, strain, bins, trig, ramp, record, shift, blocks, sums, parts, table, waves, sems,
):
    arrivals = [
        pltpu.make_async_copy(source, target, sems.at[i])
        for i, (source, target) in enumerate(
            [
                (bins_hbm, bins),
                (offsets_hbm, offsets),
                (strain_hbm, strain),
                (trig_hbm, trig),
                (ramp_hbm, ramp),
            ]
        )
    ]
    for copy in arrivals:
        copy.start()

    arrivals[0].wait()
    mult_row = lax.broadcasted_iota(jnp.int32, (2 * EDGE + rows, 1), 0)
    mult = jnp.where(
        mult_row < EDGE,
        mult_row,
        jnp.where(mult_row < 2 * EDGE, (mult_row - EDGE) * EDGE, (mult_row - 2 * EDGE) * DEPTH),
    ).astype(jnp.float32)
    phase = mult * bins[...].reshape(1, width).astype(jnp.float32)
    turns = jnp.floor(phase * (1.0 / SEGLEN) + 0.5)
    angle = (phase - turns * SEGLEN) * (2.0 * math.pi / SEGLEN)
    waves[0] = jnp.cos(angle)
    waves[1] = jnp.sin(angle)
    tiles = width // LANES
    low_cos = waves[0, 0:EDGE, :]
    low_sin = waves[1, 0:EDGE, :]
    for high in range(DEPTH // EDGE):
        at = EDGE + high
        high_cos = waves[0, at : at + 1, :]
        high_sin = waves[1, at : at + 1, :]
        real = high_cos * low_cos - high_sin * low_sin
        imag = -(high_sin * low_cos + high_cos * low_sin)
        for tile in range(tiles):
            cut = slice(tile * LANES, (tile + 1) * LANES)
            to = 2 * tile * LANES
            here = slice(high * EDGE, (high + 1) * EDGE)
            table[here, to : to + LANES] = real[:, cut].astype(jnp.bfloat16)
            table[here, to + LANES : to + 2 * LANES] = imag[:, cut].astype(jnp.bfloat16)
    arrivals[1].wait()
    for s in range(count):
        inside = (offsets[s] & (LANES - 1)).astype(jnp.float32)
        shift[0, s : s + 1, :] = jnp.full((1, LANES), inside, jnp.float32)
    turn = shift[0] * (2.0 * math.pi / SEGLEN)
    shift[1] = jnp.cos(turn)
    shift[2] = jnp.sin(turn)
    for copy in arrivals[2:]:
        copy.wait()
    samples = strain.shape[1]
    chunk = LANES * 8 * 8
    begin = 0
    while begin < samples:
        size = min(chunk, samples - begin)
        part = strain[:, begin : begin + size].astype(jnp.float32)
        record[begin // LANES : (begin + size) // LANES, :] = part.reshape(size // LANES, LANES)
        begin += size
    tail = record.shape[0] - samples // LANES
    record[samples // LANES :, :] = jnp.zeros((tail, LANES), jnp.float32)
    place = (
        lax.broadcasted_iota(jnp.int32, (8, LANES), 0) * DEPTH
        + lax.broadcasted_iota(jnp.int32, (8, LANES), 1)
    ).astype(jnp.float32)
    for s in range(count):
        first = offsets[s] // LANES
        moved = place - shift[0, s : s + 1, :]
        turn_cos = shift[1, s : s + 1, :]
        turn_sin = shift[2, s : s + 1, :]
        total = jnp.zeros((8, LANES), jnp.float32)
        for group in range(rows // 8):
            for half in range(DEPTH // LANES):
                block = record[pl.ds(first + half + 16 * group, 8, stride=2), :]
                lanes = slice(half * LANES, (half + 1) * LANES)
                wave_cos = trig[group * 8 : group * 8 + 8, lanes]
                wave_sin = trig[rows + group * 8 : rows + group * 8 + 8, lanes]
                window = 0.5 - (wave_cos * turn_cos + wave_sin * turn_sin)
                value = block * window
                sample = group * 8 * DEPTH + half * LANES
                if group == 0 and half == 0:
                    value = jnp.where(moved > -0.5, value, 0.0)
                if (group + 1) * 8 * DEPTH > SEGLEN - DEPTH:
                    value = jnp.where(moved < SEGLEN - sample - 0.5, value, 0.0)
                value = value.astype(jnp.bfloat16).astype(jnp.float32)
                total = total + value * value
                blocks[half, pl.ds(s + group * 8 * count, 8, stride=count), :] = value
        sums[s : s + 1, :] = jnp.sum(total, axis=0, keepdims=True)
    tapered = jnp.concatenate(
        [blocks[half].astype(jnp.bfloat16) for half in range(DEPTH // LANES)], axis=1
    )
    lane = lax.broadcasted_iota(jnp.int32, (count, LANES), 1)
    line = lax.broadcasted_iota(jnp.int32, (count, LANES), 0)
    whole = jnp.sum(sums[...], axis=1, keepdims=True)
    rest = jnp.sum(jnp.where(lane == line, whole, 0.0), axis=0, keepdims=True)
    place = lax.broadcasted_iota(jnp.int32, (EXTRA, LANES), 0)
    extra = jnp.zeros((EXTRA, LANES), jnp.float32)
    for i in range(PIECES):
        piece = rest.astype(jnp.bfloat16).astype(jnp.float32)
        extra = jnp.where(place == i, piece, extra)
        rest = rest - piece
    payload[2 * tiles * count :, :] = extra.astype(jnp.bfloat16)

    for tile in range(tiles):
        cut = slice(tile * LANES, (tile + 1) * LANES)
        to = 2 * tile * LANES
        product = jnp.dot(
            tapered, table[:, to : to + 2 * LANES], preferred_element_type=jnp.float32
        )
        real = jnp.zeros((count, LANES), jnp.float32)
        imag = jnp.zeros((count, LANES), jnp.float32)
        for r in range(rows):
            part = product[r * count : (r + 1) * count, :]
            twist_re = waves[0, 2 * EDGE + r : 2 * EDGE + r + 1, cut]
            twist_im = -waves[1, 2 * EDGE + r : 2 * EDGE + r + 1, cut]
            part_re, part_im = part[:, :LANES], part[:, LANES:]
            real = real + (part_re * twist_re - part_im * twist_im)
            imag = imag + (part_re * twist_im + part_im * twist_re)
        parts[0, :, cut] = real
        parts[1, :, cut] = imag
    real, imag = parts[0], parts[1]
    summed = real * real + imag * imag
    reach = 1
    while reach < SMOOTH:
        summed = summed + pltpu.roll(summed, width - reach, 1)
        reach *= 2
    lane = lax.broadcasted_iota(jnp.int32, (count, width), 1)
    middle = pltpu.roll(summed, SMOOTH // 2, 1)
    middle = jnp.where(lane < SMOOTH // 2, summed[:, 0:1], middle)
    last = width - SMOOTH
    middle = jnp.where(lane >= last + SMOOTH // 2, summed[:, last : last + 1], middle)
    scale = ramp[...] * lax.rsqrt(middle * (1.0 / SMOOTH) + EPS)
    real, imag = (real * scale).astype(jnp.bfloat16), (imag * scale).astype(jnp.bfloat16)
    for tile in range(tiles):
        cut = slice(tile * LANES, (tile + 1) * LANES)
        payload[2 * tile * count : (2 * tile + 1) * count, :] = real[:, cut]
        payload[(2 * tile + 1) * count : (2 * tile + 2) * count, :] = imag[:, cut]


def transform(strain, offsets, bins):
    count, width = offsets.shape[0], bins.shape[0]
    samples = strain.shape[1]
    rows = -(-(SEGLEN + LANES - 1) // DEPTH)
    lines = -(-(samples // LANES + 2) // 8) * 8
    trig, ramp = window_constants(rows), ramp_constant(width)
    vmem = pl.BlockSpec(memory_space=pltpu.VMEM)
    hbm = pl.BlockSpec(memory_space=pltpu.HBM)
    return pl.pallas_call(
        functools.partial(transform_kernel, count, rows, width),
        out_shape=jax.ShapeDtypeStruct((2 * width // LANES * count + EXTRA, LANES), jnp.bfloat16),
        in_specs=[hbm] * 5,
        out_specs=vmem,
        scratch_shapes=[
            pltpu.SMEM(offsets.shape, jnp.int32),
            pltpu.VMEM(strain.shape, strain.dtype),
            pltpu.VMEM(bins.shape, jnp.int32),
            pltpu.VMEM(trig.shape, jnp.float32),
            pltpu.VMEM(ramp.shape, jnp.float32),
            pltpu.VMEM((lines, LANES), jnp.float32),
            pltpu.VMEM((3, count, LANES), jnp.float32),
            pltpu.VMEM((DEPTH // LANES, rows * count, LANES), jnp.float32),
            pltpu.VMEM((count, LANES), jnp.float32),
            pltpu.VMEM((2, count, width), jnp.float32),
            pltpu.VMEM((DEPTH, 2 * width), jnp.bfloat16),
            pltpu.VMEM((2, 2 * EDGE + rows, width), jnp.float32),
            pltpu.SemaphoreType.DMA((5,)),
        ],
        compiler_params=pltpu.CompilerParams(vmem_limit_bytes=VMEM_LIMIT),
        cost_estimate=pl.CostEstimate(flops=400 << 20, bytes_accessed=6 << 20, transcendentals=0),
        name="transform",
    )(offsets, strain, bins, trig, ramp)


def energy_of(payload):
    return jnp.sum(payload[-EXTRA:, :].astype(jnp.float32), axis=0, keepdims=True)


def share_of(energy, count, channels):
    lane = lax.broadcasted_iota(jnp.int32, (count, LANES), 1)
    line = lax.broadcasted_iota(jnp.int32, (count, LANES), 0)
    weight = 1.0 / (energy * (1.0 / (channels * SEGLEN)) + EPS)
    weight = jnp.where(lane[0:1] < count, weight, 0.0)
    weight = weight / jnp.sum(weight, axis=1, keepdims=True)
    column = jnp.sum(jnp.where(lane == line, weight, 0.0), axis=1, keepdims=True)
    return jnp.broadcast_to(column, (count, LANES))


def cross_kernel(left_count, right_count, count, channels, places, energy, *refs):
    left, right = refs[:left_count], refs[left_count : left_count + right_count]
    out, block, sems = refs[left_count + right_count :]
    share = share_of(energy[...], count, channels)
    tiles = block.shape[-1] // LANES
    copies = [
        pltpu.make_async_copy(block.at[i], out.at[places[right_count + i]], sems.at[i])
        for i in range(left_count)
    ]
    for i, ref in enumerate(left):
        for tile in range(tiles):
            cut = slice(tile * LANES, (tile + 1) * LANES)
            at_re = slice(2 * tile * count, (2 * tile + 1) * count)
            at_im = slice((2 * tile + 1) * count, (2 * tile + 2) * count)
            left_re = ref[at_re, :].astype(jnp.float32) * share
            left_im = ref[at_im, :].astype(jnp.float32) * share
            for j, other in enumerate(right):
                right_re = other[at_re, :].astype(jnp.float32)
                right_im = other[at_im, :].astype(jnp.float32)
                real = left_re * right_re + left_im * right_im
                imag = left_im * right_re - left_re * right_im
                at = places[j]
                block[i, at, 0, 0:1, cut] = jnp.sum(real, axis=0, keepdims=True)
                block[i, at, 0, 1:2, cut] = jnp.sum(imag, axis=0, keepdims=True)
        copies[i].start()
    for copy in copies:
        copy.wait()


def cross(places, energy, left, right, count, width, channels):
    vmem = pl.BlockSpec(memory_space=pltpu.VMEM)
    arrays = [energy, *left, *right]
    return pl.pallas_call(
        functools.partial(cross_kernel, len(left), len(right), count, channels),
        out_shape=jax.ShapeDtypeStruct((len(left), len(right), 1, 2, width), jnp.float32),
        in_specs=[pl.BlockSpec(memory_space=pltpu.SMEM)] + [vmem] * len(arrays),
        out_specs=pl.BlockSpec(memory_space=pltpu.HBM),
        scratch_shapes=[
            pltpu.VMEM((len(left), len(right), 1, 2, width), jnp.float32),
            pltpu.SemaphoreType.DMA((len(left),)),
        ],
        compiler_params=pltpu.CompilerParams(vmem_limit_bytes=CROSS_VMEM),
        cost_estimate=pl.CostEstimate(flops=4 << 20, bytes_accessed=2 << 20, transcendentals=0),
        name="cross",
    )(places, *arrays)


def partners(size):
    if size & (size - 1) == 0:
        return [lambda p, k=k: p ^ k for k in range(size)]
    return [lambda p, k=k: (p - k) % size for k in range(size)]


def fetch(x, axis, size, step):
    source = partners(size)[step]
    return lax.ppermute(x, axis, [(source(p), p) for p in range(size)])


def fetch_all(x, axis, size):
    return [fetch(x, axis, size, step) for step in range(size - 1, 0, -1)][::-1]


def per_device(row_size, col_size, strain, offsets, bins):
    axes = ("x", "c", "z", "y")
    x_size, c_size, z_size, y_size = (lax.axis_size(a) for a in axes)
    channels = row_size * col_size
    own = transform(strain, offsets, bins)

    column = [own] + fetch_all(own, "z", z_size)
    right = [own] + fetch_all(own, "x", x_size)
    other = fetch_all(own, "y", y_size)
    near = functools.reduce(jnp.add, [energy_of(w) for w in column])
    column, right, other, near = lax.optimization_barrier((column, right, other, near))

    forward = [fetch(w, "y", y_size, step) for w in column[1:] for step in range(1, y_size)]
    far = []
    for i in range(1, x_size):
        for j in range(y_size):
            pairs = [
                (partners(x_size)[i](x) * y_size + partners(y_size)[j](y), x * y_size + y)
                for x in range(x_size)
                for y in range(y_size)
            ]
            far.append(lax.ppermute(near, ("x", "y"), pairs))
    forward, far, near = lax.optimization_barrier((forward, far, near))
    energy = functools.reduce(jnp.add, [energy_of(w) for w in other + forward], near)
    energy = functools.reduce(jnp.add, far, energy)

    energy = functools.reduce(jnp.add, fetch_all(energy, "c", c_size), energy)
    right = right + [fetch(w, "c", c_size, step) for step in range(1, c_size) for w in right]
    x, c, z, y = (lax.axis_index(a) for a in axes)
    across = [f(x) * c_size + g(c) for g in partners(c_size) for f in partners(x_size)]
    up = [f(z) * y_size + y for f in partners(z_size)]
    up = up + [z * y_size + g(y) for g in partners(y_size)[1:]]
    up = up + [f(z) * y_size + g(y) for f in partners(z_size)[1:] for g in partners(y_size)[1:]]
    places = jnp.stack(across + up).astype(jnp.int32)
    left = column + other + forward
    return cross(places, energy, left, right, offsets.shape[0], bins.shape[0], channels)


def factors(size):
    return (size // 2, 2) if size % 2 == 0 else (size, 1)


def solution(mesh):
    row_size, col_size = mesh.shape["row"], mesh.shape["col"]
    shape = factors(row_size) + factors(col_size)
    fine = Mesh(mesh.devices.reshape(shape), ("x", "c", "z", "y"))
    return jax.shard_map(
        functools.partial(per_device, row_size, col_size),
        mesh=fine,
        in_specs=(P(("x", "c", "z", "y"), None), P(), P()),
        out_specs=P(("x", "c"), None, ("z", "y"), None, None),
        check_vma=False,
    )
```

time: 69.1 us -> 30.3 us (0.44)
  blocking collectives: 38.9 us -> 0 us
  waiting for transfers between devices: 2.69 us -> 8.38 us
  local copies, waits for them, and re-layouts: 4.1 us -> 0.1 us
  starting transfers between devices: 16.5 us -> 15.1 us
  other arithmetic: 1.37 us -> 0.16 us
  Pallas kernels: 5.17 us -> 6.34 us
    psum x1 -> x0, blocking collectives: 38.9 us -> none  [per_device(): energy = lax.psum(own, ('row', 'col'))]
    ppermute x10 -> x13, waiting for transfers between devices: 2.69 us -> 8.38 us  [the longest x11 8.38 us: fetch(): return lax.ppermute(x, axis, [(source(p), p) for p in range(size)])]
    unnamed x10 -> x2, local copies, waits for them, and re-layouts: 3.94 us -> 0.01 us
    ppermute x10 -> x13, starting transfers between devices: 16.5 us -> 15.1 us  [the longest x11 13.1 us: fetch(): return lax.ppermute(x, axis, [(source(p), p) for p in range(size)])]
    pallas_call x1, Pallas kernels: 3.15 us -> 4.01 us  [transform(): pl.pallas_call(functools.partial(transform_kernel, count, rows, width), o...]
  transfers between devices with their start and end apart: 10 -> 13, of which waited for: 4 -> 6; matrix products, arithmetic and copies ran while one was open for 2% -> 1% of each run, Pallas kernels for 0% -> 0%
where the time goes in v2:
time: 30.3 us; the launch traced here: 30.2 us
  starting transfers between devices  15.1 us (50%)
  waiting for transfers between devices  8.38 us (28%)
  Pallas kernels  6.34 us (21%)
    ppermute x11, starting transfers between devices, fetch(): return lax.ppermute(x, axis, [(source(p), p) for p in range(size)])  13.1 us
    ppermute x11, waiting for transfers between devices, fetch(): return lax.ppermute(x, axis, [(source(p), p) for p in range(size)])  8.38 us
    pallas_call x1, Pallas kernels, transform(): pl.pallas_call(functools.partial(transform_kernel, count, rows, width), o...  4.01 us
    pallas_call x1, Pallas kernels, cross(): pl.pallas_call(functools.partial(cross_kernel, len(left), len(right), cou...  2.32 us
    ppermute x2, starting transfers between devices, per_device(): far.append(lax.ppermute(near, ('x', 'y'), pairs))  2.04 us
  transfers between devices with their start and end apart: 13, of which 6 were waited for; matrix products, arithmetic and copies ran while one was open for 1% of the time, Pallas kernels for 0%

profile of v2, /device:TPU:0, one launch (start us, length us, event | category | flops | bytes accessed | tf_op | source)
XLA Modules:
  0.0 30.2 jit_solution(16218119811312100366)
XLA Ops:
  0.0 4.0 %transform.1.refs_0_.refs_8_ = bf16[272,128]{1,0:T(8,128)(2,1)} custom-call(s32[32]{0:T(128)} %offsets_hbm.1, bf16[1,192000]{1,0:T(2,128)(2,1)} %strain_hbm.1, s32[512]{0:T(512)} %bins_hbm.1, f32[48,256]{1,0:T(8,128)} %constant.27.clone.trig_hbm, f32[1,512]{1,0:T(1,128)} %constant.28.clone.ramp_hbm), custom_call_target="tpu_custom_call" | custom-call | flops 419430400 | bytes 6291456 | tf_op jit(solution)/shard_map/transform/pallas_call | solution.py:190
  4.0 0.0 copy-start
  4.0 3.0 %collective-permute-start.4 = (bf16[272,128]{1,0:T(8,128)(2,1)}, bf16[272,128]{1,0:T(8,128)(2,1)S(1)}, u32[]{:S(2)}, u32[]{:S(2)}) collective-permute-start(bf16[272,128]{1,0:T(8,128)(2,1)} %transform.1.refs_0_.refs_8_), channel_id=1, source_target_pairs={{1,0},{0,1},{3,2},{2,3},{5,4},{4,5},{7,6},{6,7},{9,8},{8,9},{11,10... | collective-permute-start | bytes 208904 | tf_op jit(solution)/shard_map/ppermute | solution.py:285
  7.1 1.5 %collective-permute-start.3 = (bf16[272,128]{1,0:T(8,128)(2,1)}, bf16[272,128]{1,0:T(8,128)(2,1)S(1)}, u32[]{:S(2)}, u32[]{:S(2)}) collective-permute-start(bf16[272,128]{1,0:T(8,128)(2,1)} %transform.1.refs_0_.refs_8_), channel_id=1, source_target_pairs={{16,0},{0,16},{17,1},{1,17},{18,2},{2,18},{19,3},{3,19},{20,4},{4,... | collective-permute-start | bytes 208904 | tf_op jit(solution)/shard_map/ppermute | solution.py:285
  8.6 3.6 %collective-permute-start.2 = (bf16[272,128]{1,0:T(8,128)(2,1)}, bf16[272,128]{1,0:T(8,128)(2,1)S(1)}, u32[]{:S(2)}, u32[]{:S(2)}) collective-permute-start(bf16[272,128]{1,0:T(8,128)(2,1)} %transform.1.refs_0_.refs_8_), channel_id=1, source_target_pairs={{6,0},{4,2},{2,4},{0,6},{7,1},{5,3},{3,5},{1,7},{14,8},{12,10},{10... | collective-permute-start | bytes 208904 | tf_op jit(solution)/shard_map/ppermute | solution.py:285
  12.2 0.0 collective-permute-start.1
  12.2 0.8 %collective-permute-start = (bf16[272,128]{1,0:T(8,128)(2,1)}, bf16[272,128]{1,0:T(8,128)(2,1)S(1)}, u32[]{:S(2)}, u32[]{:S(2)}) collective-permute-start(bf16[272,128]{1,0:T(8,128)(2,1)} %transform.1.refs_0_.refs_8_), channel_id=1, source_target_pairs={{2,0},{0,2},{6,4},{4,6},{3,1},{1,3},{7,5},{5,7},{10,8},{8,10},{14,... | collective-permute-start | bytes 208904 | tf_op jit(solution)/shard_map/ppermute | solution.py:285
  12.9 0.0 copy-done
  13.0 2.5 %collective-permute-done.2.refs_3_ = bf16[272,128]{1,0:T(8,128)(2,1)S(1)} collective-permute-done((bf16[272,128]{1,0:T(8,128)(2,1)}, bf16[272,128]{1,0:T(8,128)(2,1)S(1)}, u32[]{:S(2)}, u32[]{:S(2)}) %collective-permute-start.2) | collective-permute-done | bytes 69664 | tf_op jit(solution)/shard_map/ppermute | solution.py:285
  15.5 2.4 %collective-permute-done.1.refs_2_ = bf16[272,128]{1,0:T(8,128)(2,1)S(1)} collective-permute-done((bf16[272,128]{1,0:T(8,128)(2,1)}, bf16[272,128]{1,0:T(8,128)(2,1)S(1)}, u32[]{:S(2)}, u32[]{:S(2)}) %collective-permute-start.1) | collective-permute-done | bytes 69664 | tf_op jit(solution)/shard_map/ppermute | solution.py:285
  17.9 0.0 collective-permute-done.refs_1_
  18.0 0.0 collective-permute-done.4.refs_4_
  18.0 0.0 collective-permute-done.3.refs_9_
  18.0 0.6 %collective-permute-start.9 = (f32[1,128]{1,0:T(1,128)S(1)}, f32[1,128]{1,0:T(1,128)S(1)}, u32[]{:S(2)}, u32[]{:S(2)}) collective-permute-start(f32[1,128]{1,0:T(1,128)S(1)} %add_bitcast_fusion), channel_id=1, source_target_pairs={{17,0},{16,1},{1,16},{0,17},{19,2},{18,3},{3,18},{2,19},{21,4},{20... | collective-permute-start | bytes 1544 | tf_op jit(solution)/shard_map/ppermute | solution.py:313
  18.6 1.5 %collective-permute-start.8 = (f32[1,128]{1,0:T(1,128)S(1)}, f32[1,128]{1,0:T(1,128)S(1)}, u32[]{:S(2)}, u32[]{:S(2)}) collective-permute-start(f32[1,128]{1,0:T(1,128)S(1)} %add_bitcast_fusion), channel_id=1, source_target_pairs={{16,0},{17,1},{0,16},{1,17},{18,2},{19,3},{2,18},{3,19},{20,4},{21... | collective-permute-start | bytes 1544 | tf_op jit(solution)/shard_map/ppermute | solution.py:313
  20.0 1.5 %collective-permute-start.5 = (bf16[272,128]{1,0:T(8,128)(2,1)S(1)}, bf16[272,128]{1,0:T(8,128)(2,1)S(1)}, u32[]{:S(2)}, u32[]{:S(2)}) collective-permute-start(bf16[272,128]{1,0:T(8,128)(2,1)S(1)} %collective-permute-done.refs_1_), channel_id=1, source_target_pairs={{1,0},{0,1},{3,2},{2,3},{5,4},{4,5},{7,6},{6,7},{9,8},{8,9},{11,10... | collective-permute-start | bytes 208904 | tf_op jit(solution)/shard_map/ppermute | solution.py:285
  21.5 0.5 %collective-permute-start.6 = (bf16[272,128]{1,0:T(8,128)(2,1)S(1)}, bf16[272,128]{1,0:T(8,128)(2,1)S(1)}, u32[]{:S(2)}, u32[]{:S(2)}) collective-permute-start(bf16[272,128]{1,0:T(8,128)(2,1)S(1)} %collective-permute-done.1.refs_2_), channel_id=1, source_target_pairs={{1,0},{0,1},{3,2},{2,3},{5,4},{4,5},{7,6},{6,7},{9,8},{8,9},{11,10... | collective-permute-start | bytes 208904 | tf_op jit(solution)/shard_map/ppermute | solution.py:285
  22.0 1.5 %collective-permute-start.7 = (bf16[272,128]{1,0:T(8,128)(2,1)S(1)}, bf16[272,128]{1,0:T(8,128)(2,1)S(1)}, u32[]{:S(2)}, u32[]{:S(2)}) collective-permute-start(bf16[272,128]{1,0:T(8,128)(2,1)S(1)} %collective-permute-done.2.refs_3_), channel_id=1, source_target_pairs={{1,0},{0,1},{3,2},{2,3},{5,4},{4,5},{7,6},{6,7},{9,8},{8,9},{11,10... | collective-permute-start | bytes 208904 | tf_op jit(solution)/shard_map/ppermute | solution.py:285
  23.6 0.0 collective-permute-done.9
  23.6 0.1 collective-permute-start.11
  23.7 0.0 collective-permute-done.8
  23.7 0.5 %collective-permute-start.12 = (bf16[272,128]{1,0:T(8,128)(2,1)S(1)}, bf16[272,128]{1,0:T(8,128)(2,1)S(1)}, u32[]{:S(2)}, u32[]{:S(2)}) collective-permute-start(bf16[272,128]{1,0:T(8,128)(2,1)S(1)} %collective-permute-done.3.refs_9_), channel_id=1, source_target_pairs={{8,0},{0,8},{9,1},{1,9},{10,2},{2,10},{11,3},{3,11},{12,4},{4,12},... | collective-permute-start | bytes 208904 | tf_op jit(solution)/shard_map/ppermute | solution.py:285
  24.2 0.7 %collective-permute-done.5.refs_5_ = bf16[272,128]{1,0:T(8,128)(2,1)S(1)} collective-permute-done((bf16[272,128]{1,0:T(8,128)(2,1)S(1)}, bf16[272,128]{1,0:T(8,128)(2,1)S(1)}, u32[]{:S(2)}, u32[]{:S(2)}) %collective-permute-start.5) | collective-permute-done | bytes 69664 | tf_op jit(solution)/shard_map/ppermute | solution.py:285
  24.9 1.0 %collective-permute-done.6.refs_6_ = bf16[272,128]{1,0:T(8,128)(2,1)S(1)} collective-permute-done((bf16[272,128]{1,0:T(8,128)(2,1)S(1)}, bf16[272,128]{1,0:T(8,128)(2,1)S(1)}, u32[]{:S(2)}, u32[]{:S(2)}) %collective-permute-start.6) | collective-permute-done | bytes 69664 | tf_op jit(solution)/shard_map/ppermute | solution.py:285
  25.8 0.7 %collective-permute-done.7.refs_7_ = bf16[272,128]{1,0:T(8,128)(2,1)S(1)} collective-permute-done((bf16[272,128]{1,0:T(8,128)(2,1)S(1)}, bf16[272,128]{1,0:T(8,128)(2,1)S(1)}, u32[]{:S(2)}, u32[]{:S(2)}) %collective-permute-start.7) | collective-permute-done | bytes 69664 | tf_op jit(solution)/shard_map/ppermute | solution.py:285
  26.6 0.1 collective-permute-start.10
  26.7 0.1 stack.51.places
  26.8 1.0 %collective-permute-done.10 = f32[1,128]{1,0:T(1,128)S(1)} collective-permute-done((f32[1,128]{1,0:T(1,128)S(1)}, f32[1,128]{1,0:T(1,128)S(1)}, u32[]{:S(2)}, u32[]{:S(2)}) %collective-permute-start.10) | collective-permute-done | bytes 544 | tf_op jit(solution)/shard_map/ppermute | solution.py:285
  27.8 0.0 collective-permute-done.11.refs_10_
  27.8 0.0 collective-permute-done.12.refs_11_
  27.8 2.3 %cross.1 = f32[8,4,1,2,512]{4,3,2,1,0:T(2,128)} custom-call(s32[12]{0:T(128)S(1)} %stack.51.places, f32[1,128]{1,0:T(1,128)S(1)} %add.117.energy, bf16[272,128]{1,0:T(8,128)(2,1)S(1)} %copy-done, bf16[272,128]{1,0:T(8,128)(2,1)S(1)} %collective-permute-done.refs_1_, bf16[272,128]{1,0:T(8,128)(2,1)S(1)} %collective-permute-done.1.refs_2_, ...), custom_call_target="tpu_custom_call" | custom-call | flops 4194304 | bytes 2097152 | tf_op jit(solution)/shard_map/cross/pallas_call | solution.py:262
  (10 shorter events, 0.2 us)
Async XLA Ops:
  4.0 8.9 %copy-start = (bf16[272,128]{1,0:T(8,128)(2,1)S(1)}, bf16[272,128]{1,0:T(8,128)(2,1)}, u32[]{:S(2)}) copy-start(bf16[272,128]{1,0:T(8,128)(2,1)} %transform.1.refs_0_.refs_8_) | copy-start | bytes 208900
  4.0 13.9 %collective-permute-start.4 = (bf16[272,128]{1,0:T(8,128)(2,1)}, bf16[272,128]{1,0:T(8,128)(2,1)S(1)}, u32[]{:S(2)}, u32[]{:S(2)}) collective-permute-start(bf16[272,128]{1,0:T(8,128)(2,1)} %transform.1.refs_0_.refs_8_), channel_id=1, source_target_pairs={{1,0},{0,1},{3,2},{2,3},{5,4},{4,5},{7,6},{6,7},{9,8},{8,9},{11,10... | collective-permute-start | bytes 208904 | tf_op jit(solution)/shard_map/ppermute | solution.py:285
  7.1 10.9 %collective-permute-start.3 = (bf16[272,128]{1,0:T(8,128)(2,1)}, bf16[272,128]{1,0:T(8,128)(2,1)S(1)}, u32[]{:S(2)}, u32[]{:S(2)}) collective-permute-start(bf16[272,128]{1,0:T(8,128)(2,1)} %transform.1.refs_0_.refs_8_), channel_id=1, source_target_pairs={{16,0},{0,16},{17,1},{1,17},{18,2},{2,18},{19,3},{3,19},{20,4},{4,... | collective-permute-start | bytes 208904 | tf_op jit(solution)/shard_map/ppermute | solution.py:285
  8.6 6.9 %collective-permute-start.2 = (bf16[272,128]{1,0:T(8,128)(2,1)}, bf16[272,128]{1,0:T(8,128)(2,1)S(1)}, u32[]{:S(2)}, u32[]{:S(2)}) collective-permute-start(bf16[272,128]{1,0:T(8,128)(2,1)} %transform.1.refs_0_.refs_8_), channel_id=1, source_target_pairs={{6,0},{4,2},{2,4},{0,6},{7,1},{5,3},{3,5},{1,7},{14,8},{12,10},{10... | collective-permute-start | bytes 208904 | tf_op jit(solution)/shard_map/ppermute | solution.py:285
  12.2 5.7 %collective-permute-start.1 = (bf16[272,128]{1,0:T(8,128)(2,1)}, bf16[272,128]{1,0:T(8,128)(2,1)S(1)}, u32[]{:S(2)}, u32[]{:S(2)}) collective-permute-start(bf16[272,128]{1,0:T(8,128)(2,1)} %transform.1.refs_0_.refs_8_), channel_id=1, source_target_pairs={{4,0},{6,2},{0,4},{2,6},{5,1},{7,3},{1,5},{3,7},{12,8},{14,10},{8,... | collective-permute-start | bytes 208904 | tf_op jit(solution)/shard_map/ppermute | solution.py:285
  12.2 5.8 %collective-permute-start = (bf16[272,128]{1,0:T(8,128)(2,1)}, bf16[272,128]{1,0:T(8,128)(2,1)S(1)}, u32[]{:S(2)}, u32[]{:S(2)}) collective-permute-start(bf16[272,128]{1,0:T(8,128)(2,1)} %transform.1.refs_0_.refs_8_), channel_id=1, source_target_pairs={{2,0},{0,2},{6,4},{4,6},{3,1},{1,3},{7,5},{5,7},{10,8},{8,10},{14,... | collective-permute-start | bytes 208904 | tf_op jit(solution)/shard_map/ppermute | solution.py:285
  18.0 5.6 %collective-permute-start.9 = (f32[1,128]{1,0:T(1,128)S(1)}, f32[1,128]{1,0:T(1,128)S(1)}, u32[]{:S(2)}, u32[]{:S(2)}) collective-permute-start(f32[1,128]{1,0:T(1,128)S(1)} %add_bitcast_fusion), channel_id=1, source_target_pairs={{17,0},{16,1},{1,16},{0,17},{19,2},{18,3},{3,18},{2,19},{21,4},{20... | collective-permute-start | bytes 1544 | tf_op jit(solution)/shard_map/ppermute | solution.py:313
  18.6 5.1 %collective-permute-start.8 = (f32[1,128]{1,0:T(1,128)S(1)}, f32[1,128]{1,0:T(1,128)S(1)}, u32[]{:S(2)}, u32[]{:S(2)}) collective-permute-start(f32[1,128]{1,0:T(1,128)S(1)} %add_bitcast_fusion), channel_id=1, source_target_pairs={{16,0},{17,1},{0,16},{1,17},{18,2},{19,3},{2,18},{3,19},{20,4},{21... | collective-permute-start | bytes 1544 | tf_op jit(solution)/shard_map/ppermute | solution.py:313
  20.0 4.8 %collective-permute-start.5 = (bf16[272,128]{1,0:T(8,128)(2,1)S(1)}, bf16[272,128]{1,0:T(8,128)(2,1)S(1)}, u32[]{:S(2)}, u32[]{:S(2)}) collective-permute-start(bf16[272,128]{1,0:T(8,128)(2,1)S(1)} %collective-permute-done.refs_1_), channel_id=1, source_target_pairs={{1,0},{0,1},{3,2},{2,3},{5,4},{4,5},{7,6},{6,7},{9,8},{8,9},{11,10... | collective-permute-start | bytes 208904 | tf_op jit(solution)/shard_map/ppermute | solution.py:285
  21.5 4.3 %collective-permute-start.6 = (bf16[272,128]{1,0:T(8,128)(2,1)S(1)}, bf16[272,128]{1,0:T(8,128)(2,1)S(1)}, u32[]{:S(2)}, u32[]{:S(2)}) collective-permute-start(bf16[272,128]{1,0:T(8,128)(2,1)S(1)} %collective-permute-done.1.refs_2_), channel_id=1, source_target_pairs={{1,0},{0,1},{3,2},{2,3},{5,4},{4,5},{7,6},{6,7},{9,8},{8,9},{11,10... | collective-permute-start | bytes 208904 | tf_op jit(solution)/shard_map/ppermute | solution.py:285
  22.0 4.5 %collective-permute-start.7 = (bf16[272,128]{1,0:T(8,128)(2,1)S(1)}, bf16[272,128]{1,0:T(8,128)(2,1)S(1)}, u32[]{:S(2)}, u32[]{:S(2)}) collective-permute-start(bf16[272,128]{1,0:T(8,128)(2,1)S(1)} %collective-permute-done.2.refs_3_), channel_id=1, source_target_pairs={{1,0},{0,1},{3,2},{2,3},{5,4},{4,5},{7,6},{6,7},{9,8},{8,9},{11,10... | collective-permute-start | bytes 208904 | tf_op jit(solution)/shard_map/ppermute | solution.py:285
  23.6 4.3 %collective-permute-start.11 = (bf16[272,128]{1,0:T(8,128)(2,1)S(1)}, bf16[272,128]{1,0:T(8,128)(2,1)S(1)}, u32[]{:S(2)}, u32[]{:S(2)}) collective-permute-start(bf16[272,128]{1,0:T(8,128)(2,1)S(1)} %copy-done), channel_id=1, source_target_pairs={{8,0},{0,8},{9,1},{1,9},{10,2},{2,10},{11,3},{3,11},{12,4},{4,12},... | collective-permute-start | bytes 208904 | tf_op jit(solution)/shard_map/ppermute | solution.py:285
  23.7 4.2 %collective-permute-start.12 = (bf16[272,128]{1,0:T(8,128)(2,1)S(1)}, bf16[272,128]{1,0:T(8,128)(2,1)S(1)}, u32[]{:S(2)}, u32[]{:S(2)}) collective-permute-start(bf16[272,128]{1,0:T(8,128)(2,1)S(1)} %collective-permute-done.3.refs_9_), channel_id=1, source_target_pairs={{8,0},{0,8},{9,1},{1,9},{10,2},{2,10},{11,3},{3,11},{12,4},{4,12},... | collective-permute-start | bytes 208904 | tf_op jit(solution)/shard_map/ppermute | solution.py:285
  26.6 1.2 %collective-permute-start.10 = (f32[1,128]{1,0:T(1,128)S(1)}, f32[1,128]{1,0:T(1,128)S(1)}, u32[]{:S(2)}, u32[]{:S(2)}) collective-permute-start(f32[1,128]{1,0:T(1,128)S(1)} %fusion.1), channel_id=1, source_target_pairs={{8,0},{0,8},{9,1},{1,9},{10,2},{2,10},{11,3},{3,11},{12,4},{4,12},... | collective-permute-start | bytes 1544 | tf_op jit(solution)/shard_map/ppermute | solution.py:285

commit v3 on v2

--- a/solution.py
+++ b/solution.py
@@ -3,7 +3,6 @@
 
 import jax
 import jax.numpy as jnp
-import numpy as np
 from jax import lax
 from jax.experimental import pallas as pl
 from jax.experimental.pallas import tpu as pltpu
@@ -23,54 +22,41 @@
 EDGE = 16
 
 
-def window_constants(rows):
-    position = np.arange(rows * DEPTH, dtype=np.float64).reshape(rows, DEPTH)
-    angle = 2.0 * math.pi / SEGLEN * position
-    both = np.concatenate([0.5 * np.cos(angle), 0.5 * np.sin(angle)], axis=0)
-    return both.astype(np.float32)
-
-
-def ramp_constant(width):
-    freq = np.arange(width, dtype=np.float64) + 0.5
-    reach = np.minimum(np.minimum(freq, width - freq) / TAPER, 1.0)
-    return np.square(np.sin(0.5 * math.pi * reach)).astype(np.float32)[None, :]
+def turns_of(place):
+    return place.astype(jnp.float32) * (2.0 * math.pi / SEGLEN)
 
 
 def transform_kernel(
-    count, rows, width, offsets_hbm, strain_hbm, bins_hbm, trig_hbm, ramp_hbm, payload,
-    offsets, strain, bins, trig, ramp, record, shift, blocks, sums, parts, table, waves, sems,
+    count, rows, width, offsets_hbm, strain_hbm, bins_hbm, payload,
+    offsets, strain, bins, trig, record, shift, blocks, sums, parts, table, waves, sems,
 ):
     arrivals = [
         pltpu.make_async_copy(source, target, sems.at[i])
         for i, (source, target) in enumerate(
-            [
-                (bins_hbm, bins),
-                (offsets_hbm, offsets),
-                (strain_hbm, strain),
-                (trig_hbm, trig),
-                (ramp_hbm, ramp),
-            ]
+            [(bins_hbm, bins), (offsets_hbm, offsets), (strain_hbm, strain)]
         )
     ]
     for copy in arrivals:
         copy.start()
 
     arrivals[0].wait()
-    mult_row = lax.broadcasted_iota(jnp.int32, (2 * EDGE + rows, 1), 0)
+    high_rows = DEPTH // EDGE
+    twist_row = EDGE + high_rows
+    mult_row = lax.broadcasted_iota(jnp.int32, (twist_row + rows, 1), 0)
     mult = jnp.where(
         mult_row < EDGE,
         mult_row,
-        jnp.where(mult_row < 2 * EDGE, (mult_row - EDGE) * EDGE, (mult_row - 2 * EDGE) * DEPTH),
+        jnp.where(mult_row < twist_row, (mult_row - EDGE) * EDGE, (mult_row - twist_row) * DEPTH),
     ).astype(jnp.float32)
     phase = mult * bins[...].reshape(1, width).astype(jnp.float32)
     turns = jnp.floor(phase * (1.0 / SEGLEN) + 0.5)
-    angle = (phase - turns * SEGLEN) * (2.0 * math.pi / SEGLEN)
+    angle = turns_of(phase - turns * SEGLEN)
     waves[0] = jnp.cos(angle)
     waves[1] = jnp.sin(angle)
     tiles = width // LANES
     low_cos = waves[0, 0:EDGE, :]
     low_sin = waves[1, 0:EDGE, :]
-    for high in range(DEPTH // EDGE):
+    for high in range(high_rows):
         at = EDGE + high
         high_cos = waves[0, at : at + 1, :]
         high_sin = waves[1, at : at + 1, :]
@@ -82,11 +68,15 @@
             here = slice(high * EDGE, (high + 1) * EDGE)
             table[here, to : to + LANES] = real[:, cut].astype(jnp.bfloat16)
             table[here, to + LANES : to + 2 * LANES] = imag[:, cut].astype(jnp.bfloat16)
+    line = lax.broadcasted_iota(jnp.int32, (rows, DEPTH), 0)
+    turn = turns_of(line * DEPTH + lax.broadcasted_iota(jnp.int32, (rows, DEPTH), 1))
+    trig[0] = 0.5 * jnp.cos(turn)
+    trig[1] = 0.5 * jnp.sin(turn)
     arrivals[1].wait()
     for s in range(count):
         inside = (offsets[s] & (LANES - 1)).astype(jnp.float32)
         shift[0, s : s + 1, :] = jnp.full((1, LANES), inside, jnp.float32)
-    turn = shift[0] * (2.0 * math.pi / SEGLEN)
+    turn = turns_of(shift[0])
     shift[1] = jnp.cos(turn)
     shift[2] = jnp.sin(turn)
     for copy in arrivals[2:]:
@@ -105,31 +95,31 @@
         lax.broadcasted_iota(jnp.int32, (8, LANES), 0) * DEPTH
         + lax.broadcasted_iota(jnp.int32, (8, LANES), 1)
     ).astype(jnp.float32)
+    steps = DEPTH // LANES
     for s in range(count):
         first = offsets[s] // LANES
         moved = place - shift[0, s : s + 1, :]
         turn_cos = shift[1, s : s + 1, :]
         turn_sin = shift[2, s : s + 1, :]
         total = jnp.zeros((8, LANES), jnp.float32)
-        for group in range(rows // 8):
-            for half in range(DEPTH // LANES):
-                block = record[pl.ds(first + half + 16 * group, 8, stride=2), :]
-                lanes = slice(half * LANES, (half + 1) * LANES)
-                wave_cos = trig[group * 8 : group * 8 + 8, lanes]
-                wave_sin = trig[rows + group * 8 : rows + group * 8 + 8, lanes]
-                window = 0.5 - (wave_cos * turn_cos + wave_sin * turn_sin)
+        for start in range(0, rows, 8):
+            here = slice(start, start + 8)
+            for part in range(steps):
+                lanes = slice(part * LANES, (part + 1) * LANES)
+                block = record[pl.ds(first + part + steps * start, 8, stride=steps), :]
+                window = 0.5 - (trig[0, here, lanes] * turn_cos + trig[1, here, lanes] * turn_sin)
                 value = block * window
-                sample = group * 8 * DEPTH + half * LANES
-                if group == 0 and half == 0:
+                sample = start * DEPTH + part * LANES
+                if sample == 0:
                     value = jnp.where(moved > -0.5, value, 0.0)
-                if (group + 1) * 8 * DEPTH > SEGLEN - DEPTH:
+                if (start + 7) * DEPTH + (part + 1) * LANES > SEGLEN:
                     value = jnp.where(moved < SEGLEN - sample - 0.5, value, 0.0)
                 value = value.astype(jnp.bfloat16).astype(jnp.float32)
                 total = total + value * value
-                blocks[half, pl.ds(s + group * 8 * count, 8, stride=count), :] = value
+                blocks[part, pl.ds(s + start * count, 8, stride=count), :] = value
         sums[s : s + 1, :] = jnp.sum(total, axis=0, keepdims=True)
     tapered = jnp.concatenate(
-        [blocks[half].astype(jnp.bfloat16) for half in range(DEPTH // LANES)], axis=1
+        [blocks[part].astype(jnp.bfloat16) for part in range(steps)], axis=1
     )
     lane = lax.broadcasted_iota(jnp.int32, (count, LANES), 1)
     line = lax.broadcasted_iota(jnp.int32, (count, LANES), 0)
@@ -153,25 +143,28 @@
         imag = jnp.zeros((count, LANES), jnp.float32)
         for r in range(rows):
             part = product[r * count : (r + 1) * count, :]
-            twist_re = waves[0, 2 * EDGE + r : 2 * EDGE + r + 1, cut]
-            twist_im = -waves[1, 2 * EDGE + r : 2 * EDGE + r + 1, cut]
+            twist_re = waves[0, twist_row + r : twist_row + r + 1, cut]
+            twist_im = -waves[1, twist_row + r : twist_row + r + 1, cut]
             part_re, part_im = part[:, :LANES], part[:, LANES:]
             real = real + (part_re * twist_re - part_im * twist_im)
             imag = imag + (part_re * twist_im + part_im * twist_re)
         parts[0, :, cut] = real
         parts[1, :, cut] = imag
     real, imag = parts[0], parts[1]
-    summed = real * real + imag * imag
+    power = real * real + imag * imag
     reach = 1
-    while reach < SMOOTH:
-        summed = summed + pltpu.roll(summed, width - reach, 1)
-        reach *= 2
+    while reach < SMOOTH // 4:
+        power = power + sum(pltpu.roll(power, width - k * reach, 1) for k in range(1, 4))
+        reach *= 4
+    power = sum(pltpu.roll(power, (SMOOTH // 2 - k * reach) % width, 1) for k in range(4))
     lane = lax.broadcasted_iota(jnp.int32, (count, width), 1)
-    middle = pltpu.roll(summed, SMOOTH // 2, 1)
-    middle = jnp.where(lane < SMOOTH // 2, summed[:, 0:1], middle)
-    last = width - SMOOTH
-    middle = jnp.where(lane >= last + SMOOTH // 2, summed[:, last : last + 1], middle)
-    scale = ramp[...] * lax.rsqrt(middle * (1.0 / SMOOTH) + EPS)
+    begin, end = SMOOTH // 2, width - SMOOTH // 2
+    power = jnp.where(lane < begin, power[:, begin : begin + 1], power)
+    power = jnp.where(lane > end, power[:, end : end + 1], power)
+    bin_at = (lax.broadcasted_iota(jnp.int32, (1, width), 1)).astype(jnp.float32) + 0.5
+    rise = jnp.minimum(jnp.minimum(bin_at, width - bin_at) * (1.0 / TAPER), 1.0)
+    ramp = jnp.square(jnp.sin(0.5 * math.pi * rise))
+    scale = ramp * lax.rsqrt(power * (1.0 / SMOOTH) + EPS)
     real, imag = (real * scale).astype(jnp.bfloat16), (imag * scale).astype(jnp.bfloat16)
     for tile in range(tiles):
         cut = slice(tile * LANES, (tile + 1) * LANES)
@@ -182,35 +175,33 @@
 def transform(strain, offsets, bins):
     count, width = offsets.shape[0], bins.shape[0]
     samples = strain.shape[1]
-    rows = -(-(SEGLEN + LANES - 1) // DEPTH)
-    lines = -(-(samples // LANES + 2) // 8) * 8
-    trig, ramp = window_constants(rows), ramp_constant(width)
+    rows = -(-(SEGLEN + LANES - 1) // (8 * DEPTH)) * 8
+    lines = -(-(samples // LANES + DEPTH // LANES) // 8) * 8
     vmem = pl.BlockSpec(memory_space=pltpu.VMEM)
     hbm = pl.BlockSpec(memory_space=pltpu.HBM)
     return pl.pallas_call(
         functools.partial(transform_kernel, count, rows, width),
         out_shape=jax.ShapeDtypeStruct((2 * width // LANES * count + EXTRA, LANES), jnp.bfloat16),
-        in_specs=[hbm] * 5,
+        in_specs=[hbm] * 3,
         out_specs=vmem,
         scratch_shapes=[
             pltpu.SMEM(offsets.shape, jnp.int32),
             pltpu.VMEM(strain.shape, strain.dtype),
             pltpu.VMEM(bins.shape, jnp.int32),
-            pltpu.VMEM(trig.shape, jnp.float32),
-            pltpu.VMEM(ramp.shape, jnp.float32),
+            pltpu.VMEM((2, rows, DEPTH), jnp.float32),
             pltpu.VMEM((lines, LANES), jnp.float32),
             pltpu.VMEM((3, count, LANES), jnp.float32),
             pltpu.VMEM((DEPTH // LANES, rows * count, LANES), jnp.float32),
             pltpu.VMEM((count, LANES), jnp.float32),
             pltpu.VMEM((2, count, width), jnp.float32),
             pltpu.VMEM((DEPTH, 2 * width), jnp.bfloat16),
-            pltpu.VMEM((2, 2 * EDGE + rows, width), jnp.float32),
-            pltpu.SemaphoreType.DMA((5,)),
+            pltpu.VMEM((2, EDGE + DEPTH // EDGE + rows, width), jnp.float32),
+            pltpu.SemaphoreType.DMA((3,)),
         ],
         compiler_params=pltpu.CompilerParams(vmem_limit_bytes=VMEM_LIMIT),
         cost_estimate=pl.CostEstimate(flops=400 << 20, bytes_accessed=6 << 20, transcendentals=0),
         name="transform",
-    )(offsets, strain, bins, trig, ramp)
+    )(offsets, strain, bins)
 
 
 def energy_of(payload):
@@ -296,12 +287,13 @@
     own = transform(strain, offsets, bins)
 
     column = [own] + fetch_all(own, "z", z_size)
-    right = [own] + fetch_all(own, "x", x_size)
+    beside = fetch_all(own, "x", x_size)
     other = fetch_all(own, "y", y_size)
+    soon = [fetch(w, "y", y_size, step) for w in column[3:] for step in range(1, y_size)]
+    other, beside, soon, column = lax.optimization_barrier((other, beside, soon, column))
     near = functools.reduce(jnp.add, [energy_of(w) for w in column])
-    column, right, other, near = lax.optimization_barrier((column, right, other, near))
-
-    forward = [fetch(w, "y", y_size, step) for w in column[1:] for step in range(1, y_size)]
+
+    forward = [fetch(w, "y", y_size, step) for w in column[1:3] for step in range(1, y_size)]
     far = []
     for i in range(1, x_size):
         for j in range(y_size):
@@ -312,10 +304,12 @@
             ]
             far.append(lax.ppermute(near, ("x", "y"), pairs))
     forward, far, near = lax.optimization_barrier((forward, far, near))
+    forward = forward + soon
     energy = functools.reduce(jnp.add, [energy_of(w) for w in other + forward], near)
     energy = functools.reduce(jnp.add, far, energy)
 
     energy = functools.reduce(jnp.add, fetch_all(energy, "c", c_size), energy)
+    right = [own] + beside
     right = right + [fetch(w, "c", c_size, step) for step in range(1, c_size) for w in right]
     x, c, z, y = (lax.axis_index(a) for a in axes)
     across = [f(x) * c_size + g(c) for g in partners(c_size) for f in partners(x_size)]

time: 30.3 us -> 28.9 us (0.954)
  waiting for transfers between devices: 8.38 us -> 7.58 us
  starting transfers between devices: 15.1 us -> 14.5 us
    ppermute x11, waiting for transfers between devices: 8.38 us -> 6.73 us  [fetch(): return lax.ppermute(x, axis, [(source(p), p) for p in range(size)])]
    ppermute x11, starting transfers between devices: 13.1 us -> 12 us  [fetch(): return lax.ppermute(x, axis, [(source(p), p) for p in range(size)])]
    ppermute x2, waiting for transfers between devices: 0.01 us -> 0.85 us  [per_device(): far.append(lax.ppermute(near, ('x', 'y'), pairs))]
    ppermute x2, starting transfers between devices: 2.04 us -> 2.5 us  [per_device(): far.append(lax.ppermute(near, ('x', 'y'), pairs))]
  transfers between devices with their start and end apart: 13 -> 13, of which waited for: 6 -> 7; matrix products, arithmetic and copies ran while one was open for 1% -> 1% of each run, Pallas kernels for 0% -> 0%
where the time goes in v3:
time: 28.9 us; the launch traced here: 28.8 us
  starting transfers between devices  14.5 us (50%)
  waiting for transfers between devices  7.58 us (26%)
  Pallas kernels  6.38 us (22%)
    ppermute x11, starting transfers between devices, fetch(): return lax.ppermute(x, axis, [(source(p), p) for p in range(size)])  12 us
    ppermute x11, waiting for transfers between devices, fetch(): return lax.ppermute(x, axis, [(source(p), p) for p in range(size)])  6.73 us
    pallas_call x1, Pallas kernels, transform(): pl.pallas_call(functools.partial(transform_kernel, count, rows, width), o...  4.06 us
    ppermute x2, starting transfers between devices, per_device(): far.append(lax.ppermute(near, ('x', 'y'), pairs))  2.5 us
    pallas_call x1, Pallas kernels, cross(): pl.pallas_call(functools.partial(cross_kernel, len(left), len(right), cou...  2.32 us
    ppermute x2, waiting for transfers between devices, per_device(): far.append(lax.ppermute(near, ('x', 'y'), pairs))  0.85 us
  transfers between devices with their start and end apart: 13, of which 7 were waited for; matrix products, arithmetic and copies ran while one was open for 1% of the time, Pallas kernels for 0%

profile of v3, /device:TPU:0, one launch (start us, length us, event | category | flops | bytes accessed | tf_op | source)
XLA Modules:
  0.0 28.8 jit_solution(17585473020184180379)
XLA Ops:
  0.0 4.1 %transform.1.refs_0_.refs_8_ = bf16[272,128]{1,0:T(8,128)(2,1)} custom-call(s32[32]{0:T(128)} %offsets_hbm.1, bf16[1,192000]{1,0:T(2,128)(2,1)} %strain_hbm.1, s32[512]{0:T(512)} %bins_hbm.1), custom_call_target="tpu_custom_call" | custom-call | flops 419430400 | bytes 6291456 | tf_op jit(solution)/shard_map/transform/pallas_call | solution.py:182
  4.1 0.0 copy-start
  4.1 5.1 %collective-permute-start.2 = (bf16[272,128]{1,0:T(8,128)(2,1)}, bf16[272,128]{1,0:T(8,128)(2,1)S(1)}, u32[]{:S(2)}, u32[]{:S(2)}) collective-permute-start(bf16[272,128]{1,0:T(8,128)(2,1)} %transform.1.refs_0_.refs_8_), channel_id=1, source_target_pairs={{6,0},{4,2},{2,4},{0,6},{7,1},{5,3},{3,5},{1,7},{14,8},{12,10},{10... | collective-permute-start | bytes 208904 | tf_op jit(solution)/shard_map/ppermute | solution.py:276
  9.2 0.0 collective-permute-start.5
  9.2 0.6 %collective-permute-start.4 = (bf16[272,128]{1,0:T(8,128)(2,1)}, bf16[272,128]{1,0:T(8,128)(2,1)S(1)}, u32[]{:S(2)}, u32[]{:S(2)}) collective-permute-start(bf16[272,128]{1,0:T(8,128)(2,1)} %transform.1.refs_0_.refs_8_), channel_id=1, source_target_pairs={{2,0},{0,2},{6,4},{4,6},{3,1},{1,3},{7,5},{5,7},{10,8},{8,10},{14,... | collective-permute-start | bytes 208904 | tf_op jit(solution)/shard_map/ppermute | solution.py:276
  9.8 1.6 %collective-permute-start.1 = (bf16[272,128]{1,0:T(8,128)(2,1)}, bf16[272,128]{1,0:T(8,128)(2,1)S(1)}, u32[]{:S(2)}, u32[]{:S(2)}) collective-permute-start(bf16[272,128]{1,0:T(8,128)(2,1)} %transform.1.refs_0_.refs_8_), channel_id=1, source_target_pairs={{16,0},{0,16},{17,1},{1,17},{18,2},{2,18},{19,3},{3,19},{20,4},{4,... | collective-permute-start | bytes 208904 | tf_op jit(solution)/shard_map/ppermute | solution.py:276
  11.5 1.5 %collective-permute-start = (bf16[272,128]{1,0:T(8,128)(2,1)}, bf16[272,128]{1,0:T(8,128)(2,1)S(1)}, u32[]{:S(2)}, u32[]{:S(2)}) collective-permute-start(bf16[272,128]{1,0:T(8,128)(2,1)} %transform.1.refs_0_.refs_8_), channel_id=1, source_target_pairs={{1,0},{0,1},{3,2},{2,3},{5,4},{4,5},{7,6},{6,7},{9,8},{8,9},{11,10... | collective-permute-start | bytes 208904 | tf_op jit(solution)/shard_map/ppermute | solution.py:276
  13.0 0.0 collective-permute-done.2.refs_3_
  13.0 1.0 %collective-permute-start.3 = (bf16[272,128]{1,0:T(8,128)(2,1)S(1)}, bf16[272,128]{1,0:T(8,128)(2,1)S(1)}, u32[]{:S(2)}, u32[]{:S(2)}) collective-permute-start(bf16[272,128]{1,0:T(8,128)(2,1)S(1)} %collective-permute-done.2.refs_3_), channel_id=1, source_target_pairs={{1,0},{0,1},{3,2},{2,3},{5,4},{4,5},{7,6},{6,7},{9,8},{8,9},{11,10... | collective-permute-start | bytes 208904 | tf_op jit(solution)/shard_map/ppermute | solution.py:276
  14.0 1.3 %collective-permute-done.5.refs_2_ = bf16[272,128]{1,0:T(8,128)(2,1)S(1)} collective-permute-done((bf16[272,128]{1,0:T(8,128)(2,1)}, bf16[272,128]{1,0:T(8,128)(2,1)S(1)}, u32[]{:S(2)}, u32[]{:S(2)}) %collective-permute-start.5) | collective-permute-done | bytes 69664 | tf_op jit(solution)/shard_map/ppermute | solution.py:276
  15.3 0.0 copy-done
  15.3 0.0 collective-permute-start.11
  15.3 0.0 collective-permute-done.4.refs_1_
  15.3 0.0 collective-permute-done.1.refs_9_
  15.3 0.7 %collective-permute-done.refs_4_ = bf16[272,128]{1,0:T(8,128)(2,1)S(1)} collective-permute-done((bf16[272,128]{1,0:T(8,128)(2,1)}, bf16[272,128]{1,0:T(8,128)(2,1)S(1)}, u32[]{:S(2)}, u32[]{:S(2)}) %collective-permute-start) | collective-permute-done | bytes 69664 | tf_op jit(solution)/shard_map/ppermute | solution.py:276
  16.0 1.3 %collective-permute-done.3.refs_7_ = bf16[272,128]{1,0:T(8,128)(2,1)S(1)} collective-permute-done((bf16[272,128]{1,0:T(8,128)(2,1)S(1)}, bf16[272,128]{1,0:T(8,128)(2,1)S(1)}, u32[]{:S(2)}, u32[]{:S(2)}) %collective-permute-start.3) | collective-permute-done | bytes 69664 | tf_op jit(solution)/shard_map/ppermute | solution.py:276
  17.4 1.9 %collective-permute-start.9 = (f32[1,128]{1,0:T(1,128)S(1)}, f32[1,128]{1,0:T(1,128)S(1)}, u32[]{:S(2)}, u32[]{:S(2)}) collective-permute-start(f32[1,128]{1,0:T(1,128)S(1)} %add_bitcast_fusion), channel_id=1, source_target_pairs={{17,0},{16,1},{1,16},{0,17},{19,2},{18,3},{3,18},{2,19},{21,4},{20... | collective-permute-start | bytes 1544 | tf_op jit(solution)/shard_map/ppermute | solution.py:305
  19.3 0.6 %collective-permute-start.8 = (f32[1,128]{1,0:T(1,128)S(1)}, f32[1,128]{1,0:T(1,128)S(1)}, u32[]{:S(2)}, u32[]{:S(2)}) collective-permute-start(f32[1,128]{1,0:T(1,128)S(1)} %add_bitcast_fusion), channel_id=1, source_target_pairs={{16,0},{17,1},{0,16},{1,17},{18,2},{19,3},{2,18},{3,19},{20,4},{21... | collective-permute-start | bytes 1544 | tf_op jit(solution)/shard_map/ppermute | solution.py:305
  19.9 1.1 %collective-permute-start.6 = (bf16[272,128]{1,0:T(8,128)(2,1)S(1)}, bf16[272,128]{1,0:T(8,128)(2,1)S(1)}, u32[]{:S(2)}, u32[]{:S(2)}) collective-permute-start(bf16[272,128]{1,0:T(8,128)(2,1)S(1)} %collective-permute-done.4.refs_1_), channel_id=1, source_target_pairs={{1,0},{0,1},{3,2},{2,3},{5,4},{4,5},{7,6},{6,7},{9,8},{8,9},{11,10... | collective-permute-start | bytes 208904 | tf_op jit(solution)/shard_map/ppermute | solution.py:276
  20.9 1.0 %collective-permute-start.7 = (bf16[272,128]{1,0:T(8,128)(2,1)S(1)}, bf16[272,128]{1,0:T(8,128)(2,1)S(1)}, u32[]{:S(2)}, u32[]{:S(2)}) collective-permute-start(bf16[272,128]{1,0:T(8,128)(2,1)S(1)} %collective-permute-done.5.refs_2_), channel_id=1, source_target_pairs={{1,0},{0,1},{3,2},{2,3},{5,4},{4,5},{7,6},{6,7},{9,8},{8,9},{11,10... | collective-permute-start | bytes 208904 | tf_op jit(solution)/shard_map/ppermute | solution.py:276
  21.9 0.0 collective-permute-done.9
  21.9 0.1 collective-permute-start.12
  22.0 0.8 %collective-permute-done.8 = f32[1,128]{1,0:T(1,128)S(1)} collective-permute-done((f32[1,128]{1,0:T(1,128)S(1)}, f32[1,128]{1,0:T(1,128)S(1)}, u32[]{:S(2)}, u32[]{:S(2)}) %collective-permute-start.8) | collective-permute-done | bytes 544 | tf_op jit(solution)/shard_map/ppermute | solution.py:305
  22.8 1.3 %collective-permute-done.6.refs_5_ = bf16[272,128]{1,0:T(8,128)(2,1)S(1)} collective-permute-done((bf16[272,128]{1,0:T(8,128)(2,1)S(1)}, bf16[272,128]{1,0:T(8,128)(2,1)S(1)}, u32[]{:S(2)}, u32[]{:S(2)}) %collective-permute-start.6) | collective-permute-done | bytes 69664 | tf_op jit(solution)/shard_map/ppermute | solution.py:276
  24.2 1.1 %collective-permute-done.7.refs_6_ = bf16[272,128]{1,0:T(8,128)(2,1)S(1)} collective-permute-done((bf16[272,128]{1,0:T(8,128)(2,1)S(1)}, bf16[272,128]{1,0:T(8,128)(2,1)S(1)}, u32[]{:S(2)}, u32[]{:S(2)}) %collective-permute-start.7) | collective-permute-done | bytes 69664 | tf_op jit(solution)/shard_map/ppermute | solution.py:276
  25.3 0.1 collective-permute-start.10
  25.3 0.1 stack.51.places
  25.4 1.0 %collective-permute-done.10 = f32[1,128]{1,0:T(1,128)S(1)} collective-permute-done((f32[1,128]{1,0:T(1,128)S(1)}, f32[1,128]{1,0:T(1,128)S(1)}, u32[]{:S(2)}, u32[]{:S(2)}) %collective-permute-start.10) | collective-permute-done | bytes 544 | tf_op jit(solution)/shard_map/ppermute | solution.py:276
  26.5 0.0 collective-permute-done.11.refs_10_
  26.5 0.0 collective-permute-done.12.refs_11_
  26.5 2.3 %cross.1 = f32[8,4,1,2,512]{4,3,2,1,0:T(2,128)} custom-call(s32[12]{0:T(128)S(1)} %stack.51.places, f32[1,128]{1,0:T(1,128)S(1)} %add.117.energy, bf16[272,128]{1,0:T(8,128)(2,1)S(1)} %copy-done, bf16[272,128]{1,0:T(8,128)(2,1)S(1)} %collective-permute-done.4.refs_1_, bf16[272,128]{1,0:T(8,128)(2,1)S(1)} %collective-permute-done.5.refs_2_, ...), custom_call_target="tpu_custom_call" | custom-call | flops 4194304 | bytes 2097152 | tf_op jit(solution)/shard_map/cross/pallas_call | solution.py:253
  (8 shorter events, 0.1 us)
Async XLA Ops:
  4.1 11.2 %copy-start = (bf16[272,128]{1,0:T(8,128)(2,1)S(1)}, bf16[272,128]{1,0:T(8,128)(2,1)}, u32[]{:S(2)}) copy-start(bf16[272,128]{1,0:T(8,128)(2,1)} %transform.1.refs_0_.refs_8_) | copy-start | bytes 208900
  4.1 8.9 %collective-permute-start.2 = (bf16[272,128]{1,0:T(8,128)(2,1)}, bf16[272,128]{1,0:T(8,128)(2,1)S(1)}, u32[]{:S(2)}, u32[]{:S(2)}) collective-permute-start(bf16[272,128]{1,0:T(8,128)(2,1)} %transform.1.refs_0_.refs_8_), channel_id=1, source_target_pairs={{6,0},{4,2},{2,4},{0,6},{7,1},{5,3},{3,5},{1,7},{14,8},{12,10},{10... | collective-permute-start | bytes 208904 | tf_op jit(solution)/shard_map/ppermute | solution.py:276
  9.2 6.1 %collective-permute-start.5 = (bf16[272,128]{1,0:T(8,128)(2,1)}, bf16[272,128]{1,0:T(8,128)(2,1)S(1)}, u32[]{:S(2)}, u32[]{:S(2)}) collective-permute-start(bf16[272,128]{1,0:T(8,128)(2,1)} %transform.1.refs_0_.refs_8_), channel_id=1, source_target_pairs={{4,0},{6,2},{0,4},{2,6},{5,1},{7,3},{1,5},{3,7},{12,8},{14,10},{8,... | collective-permute-start | bytes 208904 | tf_op jit(solution)/shard_map/ppermute | solution.py:276
  9.2 6.1 %collective-permute-start.4 = (bf16[272,128]{1,0:T(8,128)(2,1)}, bf16[272,128]{1,0:T(8,128)(2,1)S(1)}, u32[]{:S(2)}, u32[]{:S(2)}) collective-permute-start(bf16[272,128]{1,0:T(8,128)(2,1)} %transform.1.refs_0_.refs_8_), channel_id=1, source_target_pairs={{2,0},{0,2},{6,4},{4,6},{3,1},{1,3},{7,5},{5,7},{10,8},{8,10},{14,... | collective-permute-start | bytes 208904 | tf_op jit(solution)/shard_map/ppermute | solution.py:276
  9.8 5.5 %collective-permute-start.1 = (bf16[272,128]{1,0:T(8,128)(2,1)}, bf16[272,128]{1,0:T(8,128)(2,1)S(1)}, u32[]{:S(2)}, u32[]{:S(2)}) collective-permute-start(bf16[272,128]{1,0:T(8,128)(2,1)} %transform.1.refs_0_.refs_8_), channel_id=1, source_target_pairs={{16,0},{0,16},{17,1},{1,17},{18,2},{2,18},{19,3},{3,19},{20,4},{4,... | collective-permute-start | bytes 208904 | tf_op jit(solution)/shard_map/ppermute | solution.py:276
  11.5 4.5 %collective-permute-start = (bf16[272,128]{1,0:T(8,128)(2,1)}, bf16[272,128]{1,0:T(8,128)(2,1)S(1)}, u32[]{:S(2)}, u32[]{:S(2)}) collective-permute-start(bf16[272,128]{1,0:T(8,128)(2,1)} %transform.1.refs_0_.refs_8_), channel_id=1, source_target_pairs={{1,0},{0,1},{3,2},{2,3},{5,4},{4,5},{7,6},{6,7},{9,8},{8,9},{11,10... | collective-permute-start | bytes 208904 | tf_op jit(solution)/shard_map/ppermute | solution.py:276
  13.0 4.3 %collective-permute-start.3 = (bf16[272,128]{1,0:T(8,128)(2,1)S(1)}, bf16[272,128]{1,0:T(8,128)(2,1)S(1)}, u32[]{:S(2)}, u32[]{:S(2)}) collective-permute-start(bf16[272,128]{1,0:T(8,128)(2,1)S(1)} %collective-permute-done.2.refs_3_), channel_id=1, source_target_pairs={{1,0},{0,1},{3,2},{2,3},{5,4},{4,5},{7,6},{6,7},{9,8},{8,9},{11,10... | collective-permute-start | bytes 208904 | tf_op jit(solution)/shard_map/ppermute | solution.py:276
  15.3 11.1 %collective-permute-start.11 = (bf16[272,128]{1,0:T(8,128)(2,1)S(1)}, bf16[272,128]{1,0:T(8,128)(2,1)S(1)}, u32[]{:S(2)}, u32[]{:S(2)}) collective-permute-start(bf16[272,128]{1,0:T(8,128)(2,1)S(1)} %copy-done), channel_id=1, source_target_pairs={{8,0},{0,8},{9,1},{1,9},{10,2},{2,10},{11,3},{3,11},{12,4},{4,12},... | collective-permute-start | bytes 208904 | tf_op jit(solution)/shard_map/ppermute | solution.py:276
  17.4 4.5 %collective-permute-start.9 = (f32[1,128]{1,0:T(1,128)S(1)}, f32[1,128]{1,0:T(1,128)S(1)}, u32[]{:S(2)}, u32[]{:S(2)}) collective-permute-start(f32[1,128]{1,0:T(1,128)S(1)} %add_bitcast_fusion), channel_id=1, source_target_pairs={{17,0},{16,1},{1,16},{0,17},{19,2},{18,3},{3,18},{2,19},{21,4},{20... | collective-permute-start | bytes 1544 | tf_op jit(solution)/shard_map/ppermute | solution.py:305
  19.3 3.5 %collective-permute-start.8 = (f32[1,128]{1,0:T(1,128)S(1)}, f32[1,128]{1,0:T(1,128)S(1)}, u32[]{:S(2)}, u32[]{:S(2)}) collective-permute-start(f32[1,128]{1,0:T(1,128)S(1)} %add_bitcast_fusion), channel_id=1, source_target_pairs={{16,0},{17,1},{0,16},{1,17},{18,2},{19,3},{2,18},{3,19},{20,4},{21... | collective-permute-start | bytes 1544 | tf_op jit(solution)/shard_map/ppermute | solution.py:305
  19.9 4.3 %collective-permute-start.6 = (bf16[272,128]{1,0:T(8,128)(2,1)S(1)}, bf16[272,128]{1,0:T(8,128)(2,1)S(1)}, u32[]{:S(2)}, u32[]{:S(2)}) collective-permute-start(bf16[272,128]{1,0:T(8,128)(2,1)S(1)} %collective-permute-done.4.refs_1_), channel_id=1, source_target_pairs={{1,0},{0,1},{3,2},{2,3},{5,4},{4,5},{7,6},{6,7},{9,8},{8,9},{11,10... | collective-permute-start | bytes 208904 | tf_op jit(solution)/shard_map/ppermute | solution.py:276
  20.9 4.3 %collective-permute-start.7 = (bf16[272,128]{1,0:T(8,128)(2,1)S(1)}, bf16[272,128]{1,0:T(8,128)(2,1)S(1)}, u32[]{:S(2)}, u32[]{:S(2)}) collective-permute-start(bf16[272,128]{1,0:T(8,128)(2,1)S(1)} %collective-permute-done.5.refs_2_), channel_id=1, source_target_pairs={{1,0},{0,1},{3,2},{2,3},{5,4},{4,5},{7,6},{6,7},{9,8},{8,9},{11,10... | collective-permute-start | bytes 208904 | tf_op jit(solution)/shard_map/ppermute | solution.py:276
  21.9 4.6 %collective-permute-start.12 = (bf16[272,128]{1,0:T(8,128)(2,1)S(1)}, bf16[272,128]{1,0:T(8,128)(2,1)S(1)}, u32[]{:S(2)}, u32[]{:S(2)}) collective-permute-start(bf16[272,128]{1,0:T(8,128)(2,1)S(1)} %collective-permute-done.1.refs_9_), channel_id=1, source_target_pairs={{8,0},{0,8},{9,1},{1,9},{10,2},{2,10},{11,3},{3,11},{12,4},{4,12},... | collective-permute-start | bytes 208904 | tf_op jit(solution)/shard_map/ppermute | solution.py:276
  25.3 1.2 %collective-permute-start.10 = (f32[1,128]{1,0:T(1,128)S(1)}, f32[1,128]{1,0:T(1,128)S(1)}, u32[]{:S(2)}, u32[]{:S(2)}) collective-permute-start(f32[1,128]{1,0:T(1,128)S(1)} %fusion.1), channel_id=1, source_target_pairs={{8,0},{0,8},{9,1},{1,9},{10,2},{2,10},{11,3},{3,11},{12,4},{4,12},... | collective-permute-start | bytes 1544 | tf_op jit(solution)/shard_map/ppermute | solution.py:276

commit v4 on v3

--- a/solution.py
+++ b/solution.py
@@ -17,6 +17,7 @@
 DEPTH = 256
 VMEM_LIMIT = 58 << 20
 CROSS_VMEM = 16 << 20
+PRODUCT_BYTES = 8 << 20
 EXTRA = 16
 PIECES = 3
 EDGE = 16
@@ -28,7 +29,7 @@
 
 def transform_kernel(
     count, rows, width, offsets_hbm, strain_hbm, bins_hbm, payload,
-    offsets, strain, bins, trig, record, shift, blocks, sums, parts, table, waves, sems,
+    offsets, strain, bins, trig, ramp, record, shift, blocks, sums, table, waves, sems,
 ):
     arrivals = [
         pltpu.make_async_copy(source, target, sems.at[i])
@@ -38,6 +39,14 @@
     ]
     for copy in arrivals:
         copy.start()
+
+    line = lax.broadcasted_iota(jnp.int32, (rows, DEPTH), 0)
+    turn = turns_of(line * DEPTH + lax.broadcasted_iota(jnp.int32, (rows, DEPTH), 1))
+    trig[0] = 0.5 * jnp.cos(turn)
+    trig[1] = 0.5 * jnp.sin(turn)
+    bin_at = lax.broadcasted_iota(jnp.int32, (1, width), 1).astype(jnp.float32) + 0.5
+    rise = jnp.minimum(jnp.minimum(bin_at, width - bin_at) * (1.0 / TAPER), 1.0)
+    ramp[...] = jnp.square(jnp.sin(0.5 * math.pi * rise))
 
     arrivals[0].wait()
     high_rows = DEPTH // EDGE
@@ -68,10 +77,6 @@
             here = slice(high * EDGE, (high + 1) * EDGE)
             table[here, to : to + LANES] = real[:, cut].astype(jnp.bfloat16)
             table[here, to + LANES : to + 2 * LANES] = imag[:, cut].astype(jnp.bfloat16)
-    line = lax.broadcasted_iota(jnp.int32, (rows, DEPTH), 0)
-    turn = turns_of(line * DEPTH + lax.broadcasted_iota(jnp.int32, (rows, DEPTH), 1))
-    trig[0] = 0.5 * jnp.cos(turn)
-    trig[1] = 0.5 * jnp.sin(turn)
     arrivals[1].wait()
     for s in range(count):
         inside = (offsets[s] & (LANES - 1)).astype(jnp.float32)
@@ -121,18 +126,44 @@
     tapered = jnp.concatenate(
         [blocks[part].astype(jnp.bfloat16) for part in range(steps)], axis=1
     )
-    lane = lax.broadcasted_iota(jnp.int32, (count, LANES), 1)
-    line = lax.broadcasted_iota(jnp.int32, (count, LANES), 0)
-    whole = jnp.sum(sums[...], axis=1, keepdims=True)
-    rest = jnp.sum(jnp.where(lane == line, whole, 0.0), axis=0, keepdims=True)
-    place = lax.broadcasted_iota(jnp.int32, (EXTRA, LANES), 0)
-    extra = jnp.zeros((EXTRA, LANES), jnp.float32)
-    for i in range(PIECES):
-        piece = rest.astype(jnp.bfloat16).astype(jnp.float32)
-        extra = jnp.where(place == i, piece, extra)
-        rest = rest - piece
-    payload[2 * tiles * count :, :] = extra.astype(jnp.bfloat16)
-
+
+    def window_sums(tile):
+        above = powers[min(tile + 1, tiles - 1)]
+        sums = jnp.concatenate([powers[tile], above], axis=1)
+        reach = 1
+        while reach < SMOOTH:
+            sums = sums + sum(pltpu.roll(sums, 2 * LANES - k * reach, 1) for k in range(1, 4))
+            reach *= 4
+        return pltpu.roll(sums[:, :LANES], SMOOTH // 2, 1)
+
+    def whiten(tile):
+        windows.append(window_sums(tile))
+        lane = lax.broadcasted_iota(jnp.int32, (count, LANES), 1)
+        begin, end = SMOOTH // 2, LANES - SMOOTH // 2
+        under = windows[tile][:, begin : begin + 1] if tile == 0 else windows[tile - 1]
+        power = jnp.where(lane < begin, under, windows[tile])
+        if tile == tiles - 1:
+            power = jnp.where(lane > end, power[:, end : end + 1], power)
+        cut = slice(tile * LANES, (tile + 1) * LANES)
+        scale = ramp[:, cut] * lax.rsqrt(power * (1.0 / SMOOTH) + EPS)
+        real, imag = spectra[tile]
+        at = 2 * tile * count
+        payload[at : at + count, :] = (real * scale).astype(jnp.bfloat16)
+        payload[at + count : at + 2 * count, :] = (imag * scale).astype(jnp.bfloat16)
+
+    def write_energy():
+        lane = lax.broadcasted_iota(jnp.int32, (count, LANES), 1)
+        line = lax.broadcasted_iota(jnp.int32, (count, LANES), 0)
+        whole = jnp.sum(sums[...], axis=1, keepdims=True)
+        rest = jnp.sum(jnp.where(lane == line, whole, 0.0), axis=0, keepdims=True)
+        place = lax.broadcasted_iota(jnp.int32, (EXTRA, LANES), 0)
+        extra = jnp.zeros((EXTRA, LANES), jnp.float32)
+        for i in range(PIECES):
+            piece = rest.astype(jnp.bfloat16).astype(jnp.float32)
+            extra = jnp.where(place == i, piece, extra)
+            rest = rest - piece
+        payload[2 * tiles * count :, :] = extra.astype(jnp.bfloat16)
+    spectra, powers, windows = [], [], []
     for tile in range(tiles):
         cut = slice(tile * LANES, (tile + 1) * LANES)
         to = 2 * tile * LANES
@@ -148,28 +179,13 @@
             part_re, part_im = part[:, :LANES], part[:, LANES:]
             real = real + (part_re * twist_re - part_im * twist_im)
             imag = imag + (part_re * twist_im + part_im * twist_re)
-        parts[0, :, cut] = real
-        parts[1, :, cut] = imag
-    real, imag = parts[0], parts[1]
-    power = real * real + imag * imag
-    reach = 1
-    while reach < SMOOTH // 4:
-        power = power + sum(pltpu.roll(power, width - k * reach, 1) for k in range(1, 4))
-        reach *= 4
-    power = sum(pltpu.roll(power, (SMOOTH // 2 - k * reach) % width, 1) for k in range(4))
-    lane = lax.broadcasted_iota(jnp.int32, (count, width), 1)
-    begin, end = SMOOTH // 2, width - SMOOTH // 2
-    power = jnp.where(lane < begin, power[:, begin : begin + 1], power)
-    power = jnp.where(lane > end, power[:, end : end + 1], power)
-    bin_at = (lax.broadcasted_iota(jnp.int32, (1, width), 1)).astype(jnp.float32) + 0.5
-    rise = jnp.minimum(jnp.minimum(bin_at, width - bin_at) * (1.0 / TAPER), 1.0)
-    ramp = jnp.square(jnp.sin(0.5 * math.pi * rise))
-    scale = ramp * lax.rsqrt(power * (1.0 / SMOOTH) + EPS)
-    real, imag = (real * scale).astype(jnp.bfloat16), (imag * scale).astype(jnp.bfloat16)
-    for tile in range(tiles):
-        cut = slice(tile * LANES, (tile + 1) * LANES)
-        payload[2 * tile * count : (2 * tile + 1) * count, :] = real[:, cut]
-        payload[(2 * tile + 1) * count : (2 * tile + 2) * count, :] = imag[:, cut]
+        spectra.append((real, imag))
+        powers.append(real * real + imag * imag)
+        if tile == 0:
+            write_energy()
+        else:
+            whiten(tile - 1)
+    whiten(tiles - 1)
 
 
 def transform(strain, offsets, bins):
@@ -189,11 +205,11 @@
             pltpu.VMEM(strain.shape, strain.dtype),
             pltpu.VMEM(bins.shape, jnp.int32),
             pltpu.VMEM((2, rows, DEPTH), jnp.float32),
+            pltpu.VMEM((1, width), jnp.float32),
             pltpu.VMEM((lines, LANES), jnp.float32),
             pltpu.VMEM((3, count, LANES), jnp.float32),
             pltpu.VMEM((DEPTH // LANES, rows * count, LANES), jnp.float32),
             pltpu.VMEM((count, LANES), jnp.float32),
-            pltpu.VMEM((2, count, width), jnp.float32),
             pltpu.VMEM((DEPTH, 2 * width), jnp.bfloat16),
             pltpu.VMEM((2, EDGE + DEPTH // EDGE + rows, width), jnp.float32),
             pltpu.SemaphoreType.DMA((3,)),
@@ -208,61 +224,171 @@
     return jnp.sum(payload[-EXTRA:, :].astype(jnp.float32), axis=0, keepdims=True)
 
 
-def share_of(energy, count, channels):
+def weights_of(energy, count, channels):
     lane = lax.broadcasted_iota(jnp.int32, (count, LANES), 1)
     line = lax.broadcasted_iota(jnp.int32, (count, LANES), 0)
     weight = 1.0 / (energy * (1.0 / (channels * SEGLEN)) + EPS)
     weight = jnp.where(lane[0:1] < count, weight, 0.0)
-    weight = weight / jnp.sum(weight, axis=1, keepdims=True)
+    scale = 1.0 / jnp.sum(weight, axis=1, keepdims=True)
     column = jnp.sum(jnp.where(lane == line, weight, 0.0), axis=1, keepdims=True)
-    return jnp.broadcast_to(column, (count, LANES))
-
-
-def cross_kernel(left_count, right_count, count, channels, places, energy, *refs):
+    return jnp.broadcast_to(column, (count, LANES)), scale
+
+
+AXES = ("x", "c", "z", "y")
+
+
+def places_here():
+    x_size, c_size, z_size, y_size = (lax.axis_size(a) for a in AXES)
+    x, c, z, y = (lax.axis_index(a) for a in AXES)
+    across = [f(x) * c_size + g(c) for g in partners(c_size) for f in partners(x_size)]
+    up = [f(z) * y_size + y for f in partners(z_size)]
+    up = up + [z * y_size + g(y) for g in partners(y_size)[1:]]
+    up = up + [f(z) * y_size + g(y) for f in partners(z_size)[1:] for g in partners(y_size)[1:]]
+    return up, across
+
+
+def cross_kernel(left_count, right_count, count, channels, energy, *refs):
     left, right = refs[:left_count], refs[left_count : left_count + right_count]
     out, block, sems = refs[left_count + right_count :]
-    share = share_of(energy[...], count, channels)
-    tiles = block.shape[-1] // LANES
-    copies = [
-        pltpu.make_async_copy(block.at[i], out.at[places[right_count + i]], sems.at[i])
-        for i in range(left_count)
-    ]
-    for i, ref in enumerate(left):
-        for tile in range(tiles):
-            cut = slice(tile * LANES, (tile + 1) * LANES)
-            at_re = slice(2 * tile * count, (2 * tile + 1) * count)
-            at_im = slice((2 * tile + 1) * count, (2 * tile + 2) * count)
+    weight, scale = weights_of(energy[...], count, channels)
+    share = weight * scale
+    up, across = places_here()
+    copies = []
+    for tile in range(block.shape[-1] // LANES):
+        cut = slice(tile * LANES, (tile + 1) * LANES)
+        at_re = slice(2 * tile * count, (2 * tile + 1) * count)
+        at_im = slice((2 * tile + 1) * count, (2 * tile + 2) * count)
+        rights = [
+            (ref[at_re, :].astype(jnp.float32), ref[at_im, :].astype(jnp.float32)) for ref in right
+        ]
+        for i, ref in enumerate(left):
             left_re = ref[at_re, :].astype(jnp.float32) * share
             left_im = ref[at_im, :].astype(jnp.float32) * share
-            for j, other in enumerate(right):
-                right_re = other[at_re, :].astype(jnp.float32)
-                right_im = other[at_im, :].astype(jnp.float32)
+            for j, (right_re, right_im) in enumerate(rights):
                 real = left_re * right_re + left_im * right_im
                 imag = left_im * right_re - left_re * right_im
-                at = places[j]
-                block[i, at, 0, 0:1, cut] = jnp.sum(real, axis=0, keepdims=True)
-                block[i, at, 0, 1:2, cut] = jnp.sum(imag, axis=0, keepdims=True)
-        copies[i].start()
+                at = up[i], across[j]
+                block[at[0], at[1], 0, 0:1, cut] = jnp.sum(real, axis=0, keepdims=True)
+                block[at[0], at[1], 0, 1:2, cut] = jnp.sum(imag, axis=0, keepdims=True)
+        part = (slice(None),) * 4 + (cut,)
+        copies.append(pltpu.make_async_copy(block.at[part], out.at[part], sems.at[tile]))
+        copies[-1].start()
     for copy in copies:
         copy.wait()
 
 
-def cross(places, energy, left, right, count, width, channels):
+def cross(energy, left, right, count, width, channels):
     vmem = pl.BlockSpec(memory_space=pltpu.VMEM)
     arrays = [energy, *left, *right]
     return pl.pallas_call(
         functools.partial(cross_kernel, len(left), len(right), count, channels),
         out_shape=jax.ShapeDtypeStruct((len(left), len(right), 1, 2, width), jnp.float32),
-        in_specs=[pl.BlockSpec(memory_space=pltpu.SMEM)] + [vmem] * len(arrays),
+        in_specs=[vmem] * len(arrays),
         out_specs=pl.BlockSpec(memory_space=pltpu.HBM),
         scratch_shapes=[
             pltpu.VMEM((len(left), len(right), 1, 2, width), jnp.float32),
-            pltpu.SemaphoreType.DMA((len(left),)),
+            pltpu.SemaphoreType.DMA((width // LANES,)),
         ],
         compiler_params=pltpu.CompilerParams(vmem_limit_bytes=CROSS_VMEM),
         cost_estimate=pl.CostEstimate(flops=4 << 20, bytes_accessed=2 << 20, transcendentals=0),
         name="cross",
-    )(places, *arrays)
+    )(*arrays)
+
+
+def product_kernel(left_count, right_count, count, *refs):
+    left, right = refs[:left_count], refs[left_count : left_count + right_count]
+    products = refs[-1]
+    for tile in range(products.shape[1] // 2):
+        at_re = slice(2 * tile * count, (2 * tile + 1) * count)
+        at_im = slice((2 * tile + 1) * count, (2 * tile + 2) * count)
+        rights = [
+            (ref[at_re, :].astype(jnp.float32), ref[at_im, :].astype(jnp.float32)) for ref in right
+        ]
+        for i, ref in enumerate(left):
+            left_re = ref[at_re, :].astype(jnp.float32)
+            left_im = ref[at_im, :].astype(jnp.float32)
+            for j, (right_re, right_im) in enumerate(rights):
+                pair = i * right_count + j
+                products[pair, 2 * tile] = left_re * right_re + left_im * right_im
+                products[pair, 2 * tile + 1] = left_im * right_re - left_re * right_im
+
+
+def pair_products(left, right, count, width):
+    pairs = len(left) * len(right)
+    vmem = pl.BlockSpec(memory_space=pltpu.VMEM)
+    return pl.pallas_call(
+        functools.partial(product_kernel, len(left), len(right), count),
+        out_shape=jax.ShapeDtypeStruct((pairs, 2 * width // LANES, count, LANES), jnp.float32),
+        in_specs=[vmem] * (len(left) + len(right)),
+        out_specs=vmem,
+        compiler_params=pltpu.CompilerParams(vmem_limit_bytes=CROSS_VMEM),
+        cost_estimate=pl.CostEstimate(flops=4 << 20, bytes_accessed=2 << 20, transcendentals=0),
+        name="pair_products",
+    )(*left, *right)
+
+
+def sublane_sums(values):
+    row = lax.broadcasted_iota(jnp.int32, (8, LANES), 0)
+    for bit in (4, 2, 1):
+        low = (row & bit) == 0
+        packed = []
+        for q in range(bit):
+            a, b = values[q], values[q + bit]
+            theirs = jnp.where(low, b, a)
+            down = pltpu.roll(theirs, bit, 0)
+            if bit < 4:
+                down = jnp.where(low, pltpu.roll(theirs, 8 - bit, 0), down)
+            packed.append(jnp.where(low, a, b) + down)
+        values = packed
+    return values[0]
+
+
+def stack_kernel(left_count, right_count, channels, energy, products, out, block, sems):
+    count = products.shape[2]
+    weight, scale = weights_of(energy[...], count, channels)
+    up, across = places_here()
+    copies = []
+    for tile in range(block.shape[-1] // LANES):
+        cut = slice(tile * LANES, (tile + 1) * LANES)
+        for i in range(left_count):
+            at = up[i]
+            for first in range(0, right_count, 4):
+                some = range(first, min(first + 4, right_count))
+                sums = []
+                for j in some:
+                    for part in range(2):
+                        total = jnp.zeros((8, LANES), jnp.float32)
+                        for begin in range(0, count, 8):
+                            here = slice(begin, begin + 8)
+                            product = products[i * right_count + j, 2 * tile + part, here, :]
+                            total = total + product * weight[here, :]
+                        sums.append(total)
+                sums = sublane_sums(sums + [sums[0]] * (8 - len(sums))) * scale
+                for k, j in enumerate(some):
+                    block[at, across[j], 0, :, cut] = sums[2 * k : 2 * k + 2, :]
+        part = (slice(None),) * 4 + (cut,)
+        copies.append(pltpu.make_async_copy(block.at[part], out.at[part], sems.at[tile]))
+        copies[-1].start()
+    for copy in copies:
+        copy.wait()
+
+
+def stack(energy, products, left_count, right_count, width, channels):
+    vmem = pl.BlockSpec(memory_space=pltpu.VMEM)
+    shape = (left_count, right_count, 1, 2, width)
+    return pl.pallas_call(
+        functools.partial(stack_kernel, left_count, right_count, channels),
+        out_shape=jax.ShapeDtypeStruct(shape, jnp.float32),
+        in_specs=[vmem, vmem],
+        out_specs=pl.BlockSpec(memory_space=pltpu.HBM),
+        scratch_shapes=[
+            pltpu.VMEM(shape, jnp.float32),
+            pltpu.SemaphoreType.DMA((width // LANES,)),
+        ],
+        compiler_params=pltpu.CompilerParams(vmem_limit_bytes=CROSS_VMEM),
+        cost_estimate=pl.CostEstimate(flops=4 << 20, bytes_accessed=2 << 20, transcendentals=0),
+        name="stack",
+    )(energy, products)
 
 
 def partners(size):
@@ -281,8 +407,7 @@
 
 
 def per_device(row_size, col_size, strain, offsets, bins):
-    axes = ("x", "c", "z", "y")
-    x_size, c_size, z_size, y_size = (lax.axis_size(a) for a in axes)
+    x_size, c_size, z_size, y_size = (lax.axis_size(a) for a in AXES)
     channels = row_size * col_size
     own = transform(strain, offsets, bins)
 
@@ -290,8 +415,9 @@
     beside = fetch_all(own, "x", x_size)
     other = fetch_all(own, "y", y_size)
     soon = [fetch(w, "y", y_size, step) for w in column[3:] for step in range(1, y_size)]
-    other, beside, soon, column = lax.optimization_barrier((other, beside, soon, column))
-    near = functools.reduce(jnp.add, [energy_of(w) for w in column])
+    kept = own.astype(jnp.float32)
+    other, beside, soon, column, kept = lax.optimization_barrier((other, beside, soon, column, kept))
+    near = functools.reduce(jnp.add, [energy_of(w) for w in column[1:]], energy_of(kept))
 
     forward = [fetch(w, "y", y_size, step) for w in column[1:3] for step in range(1, y_size)]
     far = []
@@ -308,17 +434,16 @@
     energy = functools.reduce(jnp.add, [energy_of(w) for w in other + forward], near)
     energy = functools.reduce(jnp.add, far, energy)
 
+    right = [kept] + beside
+    right = right + [fetch(w, "c", c_size, step) for step in range(1, c_size) for w in [own] + beside]
+    energy, right = lax.optimization_barrier((energy, right))
     energy = functools.reduce(jnp.add, fetch_all(energy, "c", c_size), energy)
-    right = [own] + beside
-    right = right + [fetch(w, "c", c_size, step) for step in range(1, c_size) for w in right]
-    x, c, z, y = (lax.axis_index(a) for a in axes)
-    across = [f(x) * c_size + g(c) for g in partners(c_size) for f in partners(x_size)]
-    up = [f(z) * y_size + y for f in partners(z_size)]
-    up = up + [z * y_size + g(y) for g in partners(y_size)[1:]]
-    up = up + [f(z) * y_size + g(y) for f in partners(z_size)[1:] for g in partners(y_size)[1:]]
-    places = jnp.stack(across + up).astype(jnp.int32)
-    left = column + other + forward
-    return cross(places, energy, left, right, offsets.shape[0], bins.shape[0], channels)
+    left = [kept] + column[1:] + other + forward
+    count, width = offsets.shape[0], bins.shape[0]
+    if len(left) * len(right) * count * 2 * width * 4 > PRODUCT_BYTES:
+        return cross(energy, left, right, count, width, channels)
+    products = pair_products(left, right, count, width)
+    return stack(energy, products, len(left), len(right), width, channels)
 
 
 def factors(size):
@@ -328,7 +453,7 @@
 def solution(mesh):
     row_size, col_size = mesh.shape["row"], mesh.shape["col"]
     shape = factors(row_size) + factors(col_size)
-    fine = Mesh(mesh.devices.reshape(shape), ("x", "c", "z", "y"))
+    fine = Mesh(mesh.devices.reshape(shape), AXES)
     return jax.shard_map(
         functools.partial(per_device, row_size, col_size),
         mesh=fine,

time: 28.9 us -> 27.7 us (0.958)
  waiting for transfers between devices: 7.58 us -> 6.34 us
  other arithmetic: 0.12 us -> 1.01 us
  Pallas kernels: 6.38 us -> 5.64 us
    ppermute x11, waiting for transfers between devices: 6.73 us -> 5.45 us  [fetch(): return lax.ppermute(x, axis, [(source(p), p) for p in range(size)])]
    convert_element_type x0 -> x1, other arithmetic: none -> 0.89 us  [per_device(): kept = own.astype(jnp.float32)]
    pallas_call x1 -> x2, Pallas kernels: 2.32 us -> 1.62 us  [the longest x1 1.15 us: stack(): pl.pallas_call(functools.partial(stack_kernel, left_count, right_count, c...]
  transfers between devices with their start and end apart: 13 -> 13, of which waited for: 7 -> 7; matrix products, arithmetic and copies ran while one was open for 1% -> 4% of each run, Pallas kernels for 0% -> 2%
where the time goes in v4:
time: 27.7 us; the launch traced here: 27.6 us
  starting transfers between devices  14.5 us (52%)
  waiting for transfers between devices  6.34 us (23%)
  Pallas kernels  5.64 us (20%)
  other arithmetic  1.01 us (4%)
    ppermute x11, starting transfers between devices, fetch(): return lax.ppermute(x, axis, [(source(p), p) for p in range(size)])  12 us
    ppermute x11, waiting for transfers between devices, fetch(): return lax.ppermute(x, axis, [(source(p), p) for p in range(size)])  5.45 us
    pallas_call x1, Pallas kernels, transform(): pl.pallas_call(functools.partial(transform_kernel, count, rows, width), o...  4.02 us
    ppermute x2, starting transfers between devices, per_device(): far.append(lax.ppermute(near, ('x', 'y'), pairs))  2.48 us
    pallas_call x1, Pallas kernels, stack(): pl.pallas_call(functools.partial(stack_kernel, left_count, right_count, c...  1.15 us
    convert_element_type x1, other arithmetic, per_device(): kept = own.astype(jnp.float32)  0.89 us
    ppermute x2, waiting for transfers between devices, per_device(): far.append(lax.ppermute(near, ('x', 'y'), pairs))  0.88 us
  transfers between devices with their start and end apart: 13, of which 7 were waited for; matrix products, arithmetic and copies ran while one was open for 4% of the time, Pallas kernels for 2%

profile of v4, /device:TPU:0, one launch (start us, length us, event | category | flops | bytes accessed | tf_op | source)
XLA Modules:
  0.0 27.6 jit_solution(6978604510382838730)
XLA Ops:
  0.0 4.0 %transform.1 = bf16[272,128]{1,0:T(8,128)(2,1)} custom-call(s32[32]{0:T(128)} %offsets_hbm.1, bf16[1,192000]{1,0:T(2,128)(2,1)} %strain_hbm.1, s32[512]{0:T(512)} %bins_hbm.1), custom_call_target="tpu_custom_call" | custom-call | flops 419430400 | bytes 6291456 | tf_op jit(solution)/shard_map/transform/pallas_call | solution.py:198
  4.0 5.1 %collective-permute-start.2 = (bf16[272,128]{1,0:T(8,128)(2,1)}, bf16[272,128]{1,0:T(8,128)(2,1)S(1)}, u32[]{:S(2)}, u32[]{:S(2)}) collective-permute-start(bf16[272,128]{1,0:T(8,128)(2,1)} %transform.1), channel_id=1, source_target_pairs={{6,0},{4,2},{2,4},{0,6},{7,1},{5,3},{3,5},{1,7},{14,8},{12,10},{10... | collective-permute-start | bytes 208904 | tf_op jit(solution)/shard_map/ppermute | solution.py:402
  9.1 0.0 collective-permute-start.5
  9.1 0.6 %collective-permute-start.4 = (bf16[272,128]{1,0:T(8,128)(2,1)}, bf16[272,128]{1,0:T(8,128)(2,1)S(1)}, u32[]{:S(2)}, u32[]{:S(2)}) collective-permute-start(bf16[272,128]{1,0:T(8,128)(2,1)} %transform.1), channel_id=1, source_target_pairs={{2,0},{0,2},{6,4},{4,6},{3,1},{1,3},{7,5},{5,7},{10,8},{8,10},{14,... | collective-permute-start | bytes 208904 | tf_op jit(solution)/shard_map/ppermute | solution.py:402
  9.8 1.6 %collective-permute-start.1 = (bf16[272,128]{1,0:T(8,128)(2,1)}, bf16[272,128]{1,0:T(8,128)(2,1)S(1)}, u32[]{:S(2)}, u32[]{:S(2)}) collective-permute-start(bf16[272,128]{1,0:T(8,128)(2,1)} %transform.1), channel_id=1, source_target_pairs={{16,0},{0,16},{17,1},{1,17},{18,2},{2,18},{19,3},{3,19},{20,4},{4,... | collective-permute-start | bytes 208904 | tf_op jit(solution)/shard_map/ppermute | solution.py:402
  11.4 1.5 %collective-permute-start = (bf16[272,128]{1,0:T(8,128)(2,1)}, bf16[272,128]{1,0:T(8,128)(2,1)S(1)}, u32[]{:S(2)}, u32[]{:S(2)}) collective-permute-start(bf16[272,128]{1,0:T(8,128)(2,1)} %transform.1), channel_id=1, source_target_pairs={{1,0},{0,1},{3,2},{2,3},{5,4},{4,5},{7,6},{6,7},{9,8},{8,9},{11,10... | collective-permute-start | bytes 208904 | tf_op jit(solution)/shard_map/ppermute | solution.py:402
  12.9 0.0 collective-permute-done.2.refs_3_
  12.9 1.0 %collective-permute-start.3 = (bf16[272,128]{1,0:T(8,128)(2,1)S(1)}, bf16[272,128]{1,0:T(8,128)(2,1)S(1)}, u32[]{:S(2)}, u32[]{:S(2)}) collective-permute-start(bf16[272,128]{1,0:T(8,128)(2,1)S(1)} %collective-permute-done.2.refs_3_), channel_id=1, source_target_pairs={{1,0},{0,1},{3,2},{2,3},{5,4},{4,5},{7,6},{6,7},{9,8},{8,9},{11,10... | collective-permute-start | bytes 208904 | tf_op jit(solution)/shard_map/ppermute | solution.py:402
  13.9 0.9 %convert_element_type.24.refs_0_.refs_8_ = f32[272,128]{1,0:T(8,128)S(1)} convert(bf16[272,128]{1,0:T(8,128)(2,1)} %transform.1) | non-fusion elementwise | flops 34816 | bytes 208896 | tf_op jit(solution)/shard_map/convert_element_type | solution.py:418
  14.8 0.5 %collective-permute-done.5.refs_2_ = bf16[272,128]{1,0:T(8,128)(2,1)S(1)} collective-permute-done((bf16[272,128]{1,0:T(8,128)(2,1)}, bf16[272,128]{1,0:T(8,128)(2,1)S(1)}, u32[]{:S(2)}, u32[]{:S(2)}) %collective-permute-start.5) | collective-permute-done | bytes 69664 | tf_op jit(solution)/shard_map/ppermute | solution.py:402
  15.3 0.0 collective-permute-start.10
  15.3 0.0 collective-permute-done.4.refs_1_
  15.3 0.0 collective-permute-done.1.refs_9_
  15.3 0.7 %collective-permute-done.refs_4_ = bf16[272,128]{1,0:T(8,128)(2,1)S(1)} collective-permute-done((bf16[272,128]{1,0:T(8,128)(2,1)}, bf16[272,128]{1,0:T(8,128)(2,1)S(1)}, u32[]{:S(2)}, u32[]{:S(2)}) %collective-permute-start) | collective-permute-done | bytes 69664 | tf_op jit(solution)/shard_map/ppermute | solution.py:402
  15.9 1.3 %collective-permute-done.3.refs_7_ = bf16[272,128]{1,0:T(8,128)(2,1)S(1)} collective-permute-done((bf16[272,128]{1,0:T(8,128)(2,1)S(1)}, bf16[272,128]{1,0:T(8,128)(2,1)S(1)}, u32[]{:S(2)}, u32[]{:S(2)}) %collective-permute-start.3) | collective-permute-done | bytes 69664 | tf_op jit(solution)/shard_map/ppermute | solution.py:402
  17.3 2.0 %collective-permute-start.9 = (f32[1,128]{1,0:T(1,128)S(1)}, f32[1,128]{1,0:T(1,128)S(1)}, u32[]{:S(2)}, u32[]{:S(2)}) collective-permute-start(f32[1,128]{1,0:T(1,128)S(1)} %add_bitcast_fusion), channel_id=1, source_target_pairs={{17,0},{16,1},{1,16},{0,17},{19,2},{18,3},{3,18},{2,19},{21,4},{20... | collective-permute-start | bytes 1544 | tf_op jit(solution)/shard_map/ppermute | solution.py:431
  19.3 0.5 %collective-permute-start.8 = (f32[1,128]{1,0:T(1,128)S(1)}, f32[1,128]{1,0:T(1,128)S(1)}, u32[]{:S(2)}, u32[]{:S(2)}) collective-permute-start(f32[1,128]{1,0:T(1,128)S(1)} %add_bitcast_fusion), channel_id=1, source_target_pairs={{16,0},{17,1},{0,16},{1,17},{18,2},{19,3},{2,18},{3,19},{20,4},{21... | collective-permute-start | bytes 1544 | tf_op jit(solution)/shard_map/ppermute | solution.py:431
  19.8 1.1 %collective-permute-start.6 = (bf16[272,128]{1,0:T(8,128)(2,1)S(1)}, bf16[272,128]{1,0:T(8,128)(2,1)S(1)}, u32[]{:S(2)}, u32[]{:S(2)}) collective-permute-start(bf16[272,128]{1,0:T(8,128)(2,1)S(1)} %collective-permute-done.4.refs_1_), channel_id=1, source_target_pairs={{1,0},{0,1},{3,2},{2,3},{5,4},{4,5},{7,6},{6,7},{9,8},{8,9},{11,10... | collective-permute-start | bytes 208904 | tf_op jit(solution)/shard_map/ppermute | solution.py:402
  20.9 1.0 %collective-permute-start.7 = (bf16[272,128]{1,0:T(8,128)(2,1)S(1)}, bf16[272,128]{1,0:T(8,128)(2,1)S(1)}, u32[]{:S(2)}, u32[]{:S(2)}) collective-permute-start(bf16[272,128]{1,0:T(8,128)(2,1)S(1)} %collective-permute-done.5.refs_2_), channel_id=1, source_target_pairs={{1,0},{0,1},{3,2},{2,3},{5,4},{4,5},{7,6},{6,7},{9,8},{8,9},{11,10... | collective-permute-start | bytes 208904 | tf_op jit(solution)/shard_map/ppermute | solution.py:402
  21.8 0.0 collective-permute-done.9
  21.8 0.1 collective-permute-start.11
  21.9 0.9 %collective-permute-done.8 = f32[1,128]{1,0:T(1,128)S(1)} collective-permute-done((f32[1,128]{1,0:T(1,128)S(1)}, f32[1,128]{1,0:T(1,128)S(1)}, u32[]{:S(2)}, u32[]{:S(2)}) %collective-permute-start.8) | collective-permute-done | bytes 544 | tf_op jit(solution)/shard_map/ppermute | solution.py:431
  22.8 1.3 %collective-permute-done.6.refs_5_ = bf16[272,128]{1,0:T(8,128)(2,1)S(1)} collective-permute-done((bf16[272,128]{1,0:T(8,128)(2,1)S(1)}, bf16[272,128]{1,0:T(8,128)(2,1)S(1)}, u32[]{:S(2)}, u32[]{:S(2)}) %collective-permute-start.6) | collective-permute-done | bytes 69664 | tf_op jit(solution)/shard_map/ppermute | solution.py:402
  24.1 1.1 %collective-permute-done.7.refs_6_ = bf16[272,128]{1,0:T(8,128)(2,1)S(1)} collective-permute-done((bf16[272,128]{1,0:T(8,128)(2,1)S(1)}, bf16[272,128]{1,0:T(8,128)(2,1)S(1)}, u32[]{:S(2)}, u32[]{:S(2)}) %collective-permute-start.7) | collective-permute-done | bytes 69664 | tf_op jit(solution)/shard_map/ppermute | solution.py:402
  25.2 0.0 collective-permute-done.10.refs_10_
  25.2 0.0 collective-permute-done.11.refs_11_
  25.2 0.1 collective-permute-start.12
  25.3 0.5 %pair_products.1.products = f32[32,8,32,128]{3,2,1,0:T(8,128)S(1)} custom-call(f32[272,128]{1,0:T(8,128)S(1)} %convert_element_type.24.refs_0_.refs_8_, bf16[272,128]{1,0:T(8,128)(2,1)S(1)} %collective-permute-done.4.refs_1_, bf16[272,128]{1,0:T(8,128)(2,1)S(1)} %collective-permute-done.5.refs_2_, bf16[272,128]{1,0:T(8,128)(2,1)S(1)} %collective-permute-done.2.refs_3_, ...), custom_call_target="tpu_custom_call" | custom-call | flops 4194304 | bytes 2097152 | tf_op jit(solution)/shard_map/pair_products/pallas_call | solution.py:319
  25.8 0.6 %collective-permute-done.12 = f32[1,128]{1,0:T(1,128)S(1)} collective-permute-done((f32[1,128]{1,0:T(1,128)S(1)}, f32[1,128]{1,0:T(1,128)S(1)}, u32[]{:S(2)}, u32[]{:S(2)}) %collective-permute-start.12) | collective-permute-done | bytes 544 | tf_op jit(solution)/shard_map/ppermute | solution.py:402
  26.4 1.2 %stack.1 = f32[8,4,1,2,512]{4,3,2,1,0:T(2,128)} custom-call(f32[1,128]{1,0:T(1,128)S(1)} %add.69.energy, f32[32,8,32,128]{3,2,1,0:T(8,128)S(1)} %pair_products.1.products), custom_call_target="tpu_custom_call" | custom-call | flops 4194304 | bytes 2097152 | tf_op jit(solution)/shard_map/stack/pallas_call | solution.py:379
  (8 shorter events, 0.1 us)
Async XLA Ops:
  4.0 8.9 %collective-permute-start.2 = (bf16[272,128]{1,0:T(8,128)(2,1)}, bf16[272,128]{1,0:T(8,128)(2,1)S(1)}, u32[]{:S(2)}, u32[]{:S(2)}) collective-permute-start(bf16[272,128]{1,0:T(8,128)(2,1)} %transform.1), channel_id=1, source_target_pairs={{6,0},{4,2},{2,4},{0,6},{7,1},{5,3},{3,5},{1,7},{14,8},{12,10},{10... | collective-permute-start | bytes 208904 | tf_op jit(solution)/shard_map/ppermute | solution.py:402
  9.1 6.1 %collective-permute-start.5 = (bf16[272,128]{1,0:T(8,128)(2,1)}, bf16[272,128]{1,0:T(8,128)(2,1)S(1)}, u32[]{:S(2)}, u32[]{:S(2)}) collective-permute-start(bf16[272,128]{1,0:T(8,128)(2,1)} %transform.1), channel_id=1, source_target_pairs={{4,0},{6,2},{0,4},{2,6},{5,1},{7,3},{1,5},{3,7},{12,8},{14,10},{8,... | collective-permute-start | bytes 208904 | tf_op jit(solution)/shard_map/ppermute | solution.py:402
  9.1 6.1 %collective-permute-start.4 = (bf16[272,128]{1,0:T(8,128)(2,1)}, bf16[272,128]{1,0:T(8,128)(2,1)S(1)}, u32[]{:S(2)}, u32[]{:S(2)}) collective-permute-start(bf16[272,128]{1,0:T(8,128)(2,1)} %transform.1), channel_id=1, source_target_pairs={{2,0},{0,2},{6,4},{4,6},{3,1},{1,3},{7,5},{5,7},{10,8},{8,10},{14,... | collective-permute-start | bytes 208904 | tf_op jit(solution)/shard_map/ppermute | solution.py:402
  9.8 5.5 %collective-permute-start.1 = (bf16[272,128]{1,0:T(8,128)(2,1)}, bf16[272,128]{1,0:T(8,128)(2,1)S(1)}, u32[]{:S(2)}, u32[]{:S(2)}) collective-permute-start(bf16[272,128]{1,0:T(8,128)(2,1)} %transform.1), channel_id=1, source_target_pairs={{16,0},{0,16},{17,1},{1,17},{18,2},{2,18},{19,3},{3,19},{20,4},{4,... | collective-permute-start | bytes 208904 | tf_op jit(solution)/shard_map/ppermute | solution.py:402
  11.4 4.5 %collective-permute-start = (bf16[272,128]{1,0:T(8,128)(2,1)}, bf16[272,128]{1,0:T(8,128)(2,1)S(1)}, u32[]{:S(2)}, u32[]{:S(2)}) collective-permute-start(bf16[272,128]{1,0:T(8,128)(2,1)} %transform.1), channel_id=1, source_target_pairs={{1,0},{0,1},{3,2},{2,3},{5,4},{4,5},{7,6},{6,7},{9,8},{8,9},{11,10... | collective-permute-start | bytes 208904 | tf_op jit(solution)/shard_map/ppermute | solution.py:402
  12.9 4.3 %collective-permute-start.3 = (bf16[272,128]{1,0:T(8,128)(2,1)S(1)}, bf16[272,128]{1,0:T(8,128)(2,1)S(1)}, u32[]{:S(2)}, u32[]{:S(2)}) collective-permute-start(bf16[272,128]{1,0:T(8,128)(2,1)S(1)} %collective-permute-done.2.refs_3_), channel_id=1, source_target_pairs={{1,0},{0,1},{3,2},{2,3},{5,4},{4,5},{7,6},{6,7},{9,8},{8,9},{11,10... | collective-permute-start | bytes 208904 | tf_op jit(solution)/shard_map/ppermute | solution.py:402
  15.3 10.0 %collective-permute-start.10 = (bf16[272,128]{1,0:T(8,128)(2,1)}, bf16[272,128]{1,0:T(8,128)(2,1)S(1)}, u32[]{:S(2)}, u32[]{:S(2)}) collective-permute-start(bf16[272,128]{1,0:T(8,128)(2,1)} %transform.1), channel_id=1, source_target_pairs={{8,0},{0,8},{9,1},{1,9},{10,2},{2,10},{11,3},{3,11},{12,4},{4,12},... | collective-permute-start | bytes 208904 | tf_op jit(solution)/shard_map/ppermute | solution.py:402
  17.3 4.5 %collective-permute-start.9 = (f32[1,128]{1,0:T(1,128)S(1)}, f32[1,128]{1,0:T(1,128)S(1)}, u32[]{:S(2)}, u32[]{:S(2)}) collective-permute-start(f32[1,128]{1,0:T(1,128)S(1)} %add_bitcast_fusion), channel_id=1, source_target_pairs={{17,0},{16,1},{1,16},{0,17},{19,2},{18,3},{3,18},{2,19},{21,4},{20... | collective-permute-start | bytes 1544 | tf_op jit(solution)/shard_map/ppermute | solution.py:431
  19.3 3.5 %collective-permute-start.8 = (f32[1,128]{1,0:T(1,128)S(1)}, f32[1,128]{1,0:T(1,128)S(1)}, u32[]{:S(2)}, u32[]{:S(2)}) collective-permute-start(f32[1,128]{1,0:T(1,128)S(1)} %add_bitcast_fusion), channel_id=1, source_target_pairs={{16,0},{17,1},{0,16},{1,17},{18,2},{19,3},{2,18},{3,19},{20,4},{21... | collective-permute-start | bytes 1544 | tf_op jit(solution)/shard_map/ppermute | solution.py:431
  19.8 4.3 %collective-permute-start.6 = (bf16[272,128]{1,0:T(8,128)(2,1)S(1)}, bf16[272,128]{1,0:T(8,128)(2,1)S(1)}, u32[]{:S(2)}, u32[]{:S(2)}) collective-permute-start(bf16[272,128]{1,0:T(8,128)(2,1)S(1)} %collective-permute-done.4.refs_1_), channel_id=1, source_target_pairs={{1,0},{0,1},{3,2},{2,3},{5,4},{4,5},{7,6},{6,7},{9,8},{8,9},{11,10... | collective-permute-start | bytes 208904 | tf_op jit(solution)/shard_map/ppermute | solution.py:402
  20.9 4.3 %collective-permute-start.7 = (bf16[272,128]{1,0:T(8,128)(2,1)S(1)}, bf16[272,128]{1,0:T(8,128)(2,1)S(1)}, u32[]{:S(2)}, u32[]{:S(2)}) collective-permute-start(bf16[272,128]{1,0:T(8,128)(2,1)S(1)} %collective-permute-done.5.refs_2_), channel_id=1, source_target_pairs={{1,0},{0,1},{3,2},{2,3},{5,4},{4,5},{7,6},{6,7},{9,8},{8,9},{11,10... | collective-permute-start | bytes 208904 | tf_op jit(solution)/shard_map/ppermute | solution.py:402
  21.8 3.4 %collective-permute-start.11 = (bf16[272,128]{1,0:T(8,128)(2,1)S(1)}, bf16[272,128]{1,0:T(8,128)(2,1)S(1)}, u32[]{:S(2)}, u32[]{:S(2)}) collective-permute-start(bf16[272,128]{1,0:T(8,128)(2,1)S(1)} %collective-permute-done.1.refs_9_), channel_id=1, source_target_pairs={{8,0},{0,8},{9,1},{1,9},{10,2},{2,10},{11,3},{3,11},{12,4},{4,12},... | collective-permute-start | bytes 208904 | tf_op jit(solution)/shard_map/ppermute | solution.py:402
  25.2 1.2 %collective-permute-start.12 = (f32[1,128]{1,0:T(1,128)S(1)}, f32[1,128]{1,0:T(1,128)S(1)}, u32[]{:S(2)}, u32[]{:S(2)}) collective-permute-start(f32[1,128]{1,0:T(1,128)S(1)} %fusion.1), channel_id=1, source_target_pairs={{8,0},{0,8},{9,1},{1,9},{10,2},{2,10},{11,3},{3,11},{12,4},{4,12},... | collective-permute-start | bytes 1544 | tf_op jit(solution)/shard_map/ppermute | solution.py:402

commit v5 on v4

--- a/solution.py
+++ b/solution.py
@@ -20,6 +20,7 @@
 PRODUCT_BYTES = 8 << 20
 EXTRA = 16
 PIECES = 3
+GROUPS = 2
 EDGE = 16
 
 
@@ -28,7 +29,7 @@
 
 
 def transform_kernel(
-    count, rows, width, offsets_hbm, strain_hbm, bins_hbm, payload,
+    count, groups, rows, width, offsets_hbm, strain_hbm, bins_hbm, payload,
     offsets, strain, bins, trig, ramp, record, shift, blocks, sums, table, waves, sems,
 ):
     arrivals = [
@@ -101,33 +102,39 @@
         + lax.broadcasted_iota(jnp.int32, (8, LANES), 1)
     ).astype(jnp.float32)
     steps = DEPTH // LANES
-    for s in range(count):
-        first = offsets[s] // LANES
-        moved = place - shift[0, s : s + 1, :]
-        turn_cos = shift[1, s : s + 1, :]
-        turn_sin = shift[2, s : s + 1, :]
-        total = jnp.zeros((8, LANES), jnp.float32)
-        for start in range(0, rows, 8):
-            here = slice(start, start + 8)
-            for part in range(steps):
-                lanes = slice(part * LANES, (part + 1) * LANES)
-                block = record[pl.ds(first + part + steps * start, 8, stride=steps), :]
-                window = 0.5 - (trig[0, here, lanes] * turn_cos + trig[1, here, lanes] * turn_sin)
-                value = block * window
-                sample = start * DEPTH + part * LANES
-                if sample == 0:
-                    value = jnp.where(moved > -0.5, value, 0.0)
-                if (start + 7) * DEPTH + (part + 1) * LANES > SEGLEN:
-                    value = jnp.where(moved < SEGLEN - sample - 0.5, value, 0.0)
-                value = value.astype(jnp.bfloat16).astype(jnp.float32)
-                total = total + value * value
-                blocks[part, pl.ds(s + start * count, 8, stride=count), :] = value
-        sums[s : s + 1, :] = jnp.sum(total, axis=0, keepdims=True)
-    tapered = jnp.concatenate(
-        [blocks[part].astype(jnp.bfloat16) for part in range(steps)], axis=1
-    )
-
-    def window_sums(tile):
+    some = count // groups
+
+    def taper(group, segments):
+        for s in segments:
+            first = offsets[s] // LANES
+            moved = place - shift[0, s : s + 1, :]
+            turn_cos = shift[1, s : s + 1, :]
+            turn_sin = shift[2, s : s + 1, :]
+            total = jnp.zeros((8, LANES), jnp.float32)
+            for start in range(0, rows, 8):
+                here = slice(start, start + 8)
+                for part in range(steps):
+                    lanes = slice(part * LANES, (part + 1) * LANES)
+                    block = record[pl.ds(first + part + steps * start, 8, stride=steps), :]
+                    window = 0.5 - (trig[0, here, lanes] * turn_cos + trig[1, here, lanes] * turn_sin)
+                    value = block * window
+                    sample = start * DEPTH + part * LANES
+                    if sample == 0:
+                        value = jnp.where(moved > -0.5, value, 0.0)
+                    if (start + 7) * DEPTH + (part + 1) * LANES > SEGLEN:
+                        value = jnp.where(moved < SEGLEN - sample - 0.5, value, 0.0)
+                    value = value.astype(jnp.bfloat16).astype(jnp.float32)
+                    total = total + value * value
+                    at = s - group * some + start * some
+                    blocks[group, part, pl.ds(at, 8, stride=some), :] = value
+            sums[s : s + 1, :] = jnp.sum(total, axis=0, keepdims=True)
+
+    def tapered_group(group):
+        return jnp.concatenate(
+            [blocks[group, part].astype(jnp.bfloat16) for part in range(steps)], axis=1
+        )
+
+    def window_sums(powers, tile):
         above = powers[min(tile + 1, tiles - 1)]
         sums = jnp.concatenate([powers[tile], above], axis=1)
         reach = 1
@@ -136,9 +143,9 @@
             reach *= 4
         return pltpu.roll(sums[:, :LANES], SMOOTH // 2, 1)
 
-    def whiten(tile):
-        windows.append(window_sums(tile))
-        lane = lax.broadcasted_iota(jnp.int32, (count, LANES), 1)
+    def whiten(group, spectra, powers, windows, tile):
+        windows.append(window_sums(powers, tile))
+        lane = lax.broadcasted_iota(jnp.int32, (some, LANES), 1)
         begin, end = SMOOTH // 2, LANES - SMOOTH // 2
         under = windows[tile][:, begin : begin + 1] if tile == 0 else windows[tile - 1]
         power = jnp.where(lane < begin, under, windows[tile])
@@ -147,9 +154,9 @@
         cut = slice(tile * LANES, (tile + 1) * LANES)
         scale = ramp[:, cut] * lax.rsqrt(power * (1.0 / SMOOTH) + EPS)
         real, imag = spectra[tile]
-        at = 2 * tile * count
-        payload[at : at + count, :] = (real * scale).astype(jnp.bfloat16)
-        payload[at + count : at + 2 * count, :] = (imag * scale).astype(jnp.bfloat16)
+        at = 2 * tile * count + group * some
+        payload[at : at + some, :] = (real * scale).astype(jnp.bfloat16)
+        payload[at + count : at + count + some, :] = (imag * scale).astype(jnp.bfloat16)
 
     def write_energy():
         lane = lax.broadcasted_iota(jnp.int32, (count, LANES), 1)
@@ -163,40 +170,47 @@
             extra = jnp.where(place == i, piece, extra)
             rest = rest - piece
         payload[2 * tiles * count :, :] = extra.astype(jnp.bfloat16)
-    spectra, powers, windows = [], [], []
-    for tile in range(tiles):
-        cut = slice(tile * LANES, (tile + 1) * LANES)
-        to = 2 * tile * LANES
-        product = jnp.dot(
-            tapered, table[:, to : to + 2 * LANES], preferred_element_type=jnp.float32
-        )
-        real = jnp.zeros((count, LANES), jnp.float32)
-        imag = jnp.zeros((count, LANES), jnp.float32)
-        for r in range(rows):
-            part = product[r * count : (r + 1) * count, :]
-            twist_re = waves[0, twist_row + r : twist_row + r + 1, cut]
-            twist_im = -waves[1, twist_row + r : twist_row + r + 1, cut]
-            part_re, part_im = part[:, :LANES], part[:, LANES:]
-            real = real + (part_re * twist_re - part_im * twist_im)
-            imag = imag + (part_re * twist_im + part_im * twist_re)
-        spectra.append((real, imag))
-        powers.append(real * real + imag * imag)
-        if tile == 0:
-            write_energy()
-        else:
-            whiten(tile - 1)
-    whiten(tiles - 1)
+    taper(0, range(some))
+    for group in range(groups):
+        tapered = tapered_group(group)
+        spectra, powers, windows = [], [], []
+        for tile in range(tiles):
+            cut = slice(tile * LANES, (tile + 1) * LANES)
+            to = 2 * tile * LANES
+            product = jnp.dot(
+                tapered, table[:, to : to + 2 * LANES], preferred_element_type=jnp.float32
+            )
+            if group < groups - 1:
+                begin = (group + 1) * some
+                taper(group + 1, range(begin + tile * some // tiles, begin + (tile + 1) * some // tiles))
+            real = jnp.zeros((some, LANES), jnp.float32)
+            imag = jnp.zeros((some, LANES), jnp.float32)
+            for r in range(rows):
+                part = product[r * some : (r + 1) * some, :]
+                twist_re = waves[0, twist_row + r : twist_row + r + 1, cut]
+                twist_im = -waves[1, twist_row + r : twist_row + r + 1, cut]
+                part_re, part_im = part[:, :LANES], part[:, LANES:]
+                real = real + (part_re * twist_re - part_im * twist_im)
+                imag = imag + (part_re * twist_im + part_im * twist_re)
+            spectra.append((real, imag))
+            powers.append(real * real + imag * imag)
+            if tile:
+                whiten(group, spectra, powers, windows, tile - 1)
+            elif group == groups - 1:
+                write_energy()
+        whiten(group, spectra, powers, windows, tiles - 1)
 
 
 def transform(strain, offsets, bins):
     count, width = offsets.shape[0], bins.shape[0]
     samples = strain.shape[1]
     rows = -(-(SEGLEN + LANES - 1) // (8 * DEPTH)) * 8
+    groups = GROUPS if count % (16 * GROUPS) == 0 else 1
     lines = -(-(samples // LANES + DEPTH // LANES) // 8) * 8
     vmem = pl.BlockSpec(memory_space=pltpu.VMEM)
     hbm = pl.BlockSpec(memory_space=pltpu.HBM)
     return pl.pallas_call(
-        functools.partial(transform_kernel, count, rows, width),
+        functools.partial(transform_kernel, count, groups, rows, width),
         out_shape=jax.ShapeDtypeStruct((2 * width // LANES * count + EXTRA, LANES), jnp.bfloat16),
         in_specs=[hbm] * 3,
         out_specs=vmem,
@@ -208,7 +222,7 @@
             pltpu.VMEM((1, width), jnp.float32),
             pltpu.VMEM((lines, LANES), jnp.float32),
             pltpu.VMEM((3, count, LANES), jnp.float32),
-            pltpu.VMEM((DEPTH // LANES, rows * count, LANES), jnp.float32),
+            pltpu.VMEM((groups, DEPTH // LANES, rows * count // groups, LANES), jnp.float32),
             pltpu.VMEM((count, LANES), jnp.float32),
             pltpu.VMEM((DEPTH, 2 * width), jnp.bfloat16),
             pltpu.VMEM((2, EDGE + DEPTH // EDGE + rows, width), jnp.float32),

time: 27.7 us -> 27.5 us (level)
  Pallas kernels: 5.64 us -> 5.36 us
    pallas_call x1, Pallas kernels: 4.02 us -> 3.74 us  [transform(): pl.pallas_call(functools.partial(transform_kernel, count, groups, rows, w...]
where the time goes in v5:
time: 27.5 us; the launch traced here: 27.3 us
  starting transfers between devices  14.5 us (53%)
  waiting for transfers between devices  6.31 us (23%)
  Pallas kernels  5.36 us (19%)
  other arithmetic  1.01 us (4%)
    ppermute x11, starting transfers between devices, fetch(): return lax.ppermute(x, axis, [(source(p), p) for p in range(size)])  12.1 us
    ppermute x11, waiting for transfers between devices, fetch(): return lax.ppermute(x, axis, [(source(p), p) for p in range(size)])  5.44 us
    pallas_call x1, Pallas kernels, transform(): pl.pallas_call(functools.partial(transform_kernel, count, groups, rows, w...  3.74 us
    ppermute x2, starting transfers between devices, per_device(): far.append(lax.ppermute(near, ('x', 'y'), pairs))  2.49 us
    pallas_call x1, Pallas kernels, stack(): pl.pallas_call(functools.partial(stack_kernel, left_count, right_count, c...  1.15 us
    convert_element_type x1, other arithmetic, per_device(): kept = own.astype(jnp.float32)  0.89 us
    ppermute x2, waiting for transfers between devices, per_device(): far.append(lax.ppermute(near, ('x', 'y'), pairs))  0.87 us
  transfers between devices with their start and end apart: 13, of which 7 were waited for; matrix products, arithmetic and copies ran while one was open for 4% of the time, Pallas kernels for 2%

profile of v5, /device:TPU:0, one launch (start us, length us, event | category | flops | bytes accessed | tf_op | source)
XLA Modules:
  0.0 27.3 jit_solution(9364517114952329247)
XLA Ops:
  0.0 3.7 %transform.1 = bf16[272,128]{1,0:T(8,128)(2,1)} custom-call(s32[32]{0:T(128)} %offsets_hbm.1, bf16[1,192000]{1,0:T(2,128)(2,1)} %strain_hbm.1, s32[512]{0:T(512)} %bins_hbm.1), custom_call_target="tpu_custom_call" | custom-call | flops 419430400 | bytes 6291456 | tf_op jit(solution)/shard_map/transform/pallas_call | solution.py:212
  3.7 5.1 %collective-permute-start.2 = (bf16[272,128]{1,0:T(8,128)(2,1)}, bf16[272,128]{1,0:T(8,128)(2,1)S(1)}, u32[]{:S(2)}, u32[]{:S(2)}) collective-permute-start(bf16[272,128]{1,0:T(8,128)(2,1)} %transform.1), channel_id=1, source_target_pairs={{6,0},{4,2},{2,4},{0,6},{7,1},{5,3},{3,5},{1,7},{14,8},{12,10},{10... | collective-permute-start | bytes 208904 | tf_op jit(solution)/shard_map/ppermute | solution.py:416
  8.8 0.0 collective-permute-start.5
  8.9 0.6 %collective-permute-start.4 = (bf16[272,128]{1,0:T(8,128)(2,1)}, bf16[272,128]{1,0:T(8,128)(2,1)S(1)}, u32[]{:S(2)}, u32[]{:S(2)}) collective-permute-start(bf16[272,128]{1,0:T(8,128)(2,1)} %transform.1), channel_id=1, source_target_pairs={{2,0},{0,2},{6,4},{4,6},{3,1},{1,3},{7,5},{5,7},{10,8},{8,10},{14,... | collective-permute-start | bytes 208904 | tf_op jit(solution)/shard_map/ppermute | solution.py:416
  9.5 1.7 %collective-permute-start.1 = (bf16[272,128]{1,0:T(8,128)(2,1)}, bf16[272,128]{1,0:T(8,128)(2,1)S(1)}, u32[]{:S(2)}, u32[]{:S(2)}) collective-permute-start(bf16[272,128]{1,0:T(8,128)(2,1)} %transform.1), channel_id=1, source_target_pairs={{16,0},{0,16},{17,1},{1,17},{18,2},{2,18},{19,3},{3,19},{20,4},{4,... | collective-permute-start | bytes 208904 | tf_op jit(solution)/shard_map/ppermute | solution.py:416
  11.1 1.5 %collective-permute-start = (bf16[272,128]{1,0:T(8,128)(2,1)}, bf16[272,128]{1,0:T(8,128)(2,1)S(1)}, u32[]{:S(2)}, u32[]{:S(2)}) collective-permute-start(bf16[272,128]{1,0:T(8,128)(2,1)} %transform.1), channel_id=1, source_target_pairs={{1,0},{0,1},{3,2},{2,3},{5,4},{4,5},{7,6},{6,7},{9,8},{8,9},{11,10... | collective-permute-start | bytes 208904 | tf_op jit(solution)/shard_map/ppermute | solution.py:416
  12.7 0.0 collective-permute-done.2.refs_3_
  12.7 1.0 %collective-permute-start.3 = (bf16[272,128]{1,0:T(8,128)(2,1)S(1)}, bf16[272,128]{1,0:T(8,128)(2,1)S(1)}, u32[]{:S(2)}, u32[]{:S(2)}) collective-permute-start(bf16[272,128]{1,0:T(8,128)(2,1)S(1)} %collective-permute-done.2.refs_3_), channel_id=1, source_target_pairs={{1,0},{0,1},{3,2},{2,3},{5,4},{4,5},{7,6},{6,7},{9,8},{8,9},{11,10... | collective-permute-start | bytes 208904 | tf_op jit(solution)/shard_map/ppermute | solution.py:416
  13.6 0.9 %convert_element_type.24.refs_0_.refs_8_ = f32[272,128]{1,0:T(8,128)S(1)} convert(bf16[272,128]{1,0:T(8,128)(2,1)} %transform.1) | non-fusion elementwise | flops 34816 | bytes 208896 | tf_op jit(solution)/shard_map/convert_element_type | solution.py:432
  14.5 0.5 %collective-permute-done.5.refs_2_ = bf16[272,128]{1,0:T(8,128)(2,1)S(1)} collective-permute-done((bf16[272,128]{1,0:T(8,128)(2,1)}, bf16[272,128]{1,0:T(8,128)(2,1)S(1)}, u32[]{:S(2)}, u32[]{:S(2)}) %collective-permute-start.5) | collective-permute-done | bytes 69664 | tf_op jit(solution)/shard_map/ppermute | solution.py:416
  15.0 0.0 collective-permute-start.10
  15.0 0.0 collective-permute-done.4.refs_1_
  15.0 0.0 collective-permute-done.1.refs_9_
  15.0 0.7 %collective-permute-done.refs_4_ = bf16[272,128]{1,0:T(8,128)(2,1)S(1)} collective-permute-done((bf16[272,128]{1,0:T(8,128)(2,1)}, bf16[272,128]{1,0:T(8,128)(2,1)S(1)}, u32[]{:S(2)}, u32[]{:S(2)}) %collective-permute-start) | collective-permute-done | bytes 69664 | tf_op jit(solution)/shard_map/ppermute | solution.py:416
  15.7 1.3 %collective-permute-done.3.refs_7_ = bf16[272,128]{1,0:T(8,128)(2,1)S(1)} collective-permute-done((bf16[272,128]{1,0:T(8,128)(2,1)S(1)}, bf16[272,128]{1,0:T(8,128)(2,1)S(1)}, u32[]{:S(2)}, u32[]{:S(2)}) %collective-permute-start.3) | collective-permute-done | bytes 69664 | tf_op jit(solution)/shard_map/ppermute | solution.py:416
  17.0 2.0 %collective-permute-start.9 = (f32[1,128]{1,0:T(1,128)S(1)}, f32[1,128]{1,0:T(1,128)S(1)}, u32[]{:S(2)}, u32[]{:S(2)}) collective-permute-start(f32[1,128]{1,0:T(1,128)S(1)} %add_bitcast_fusion), channel_id=1, source_target_pairs={{17,0},{16,1},{1,16},{0,17},{19,2},{18,3},{3,18},{2,19},{21,4},{20... | collective-permute-start | bytes 1544 | tf_op jit(solution)/shard_map/ppermute | solution.py:445
  19.0 0.5 %collective-permute-start.8 = (f32[1,128]{1,0:T(1,128)S(1)}, f32[1,128]{1,0:T(1,128)S(1)}, u32[]{:S(2)}, u32[]{:S(2)}) collective-permute-start(f32[1,128]{1,0:T(1,128)S(1)} %add_bitcast_fusion), channel_id=1, source_target_pairs={{16,0},{17,1},{0,16},{1,17},{18,2},{19,3},{2,18},{3,19},{20,4},{21... | collective-permute-start | bytes 1544 | tf_op jit(solution)/shard_map/ppermute | solution.py:445
  19.5 1.1 %collective-permute-start.6 = (bf16[272,128]{1,0:T(8,128)(2,1)S(1)}, bf16[272,128]{1,0:T(8,128)(2,1)S(1)}, u32[]{:S(2)}, u32[]{:S(2)}) collective-permute-start(bf16[272,128]{1,0:T(8,128)(2,1)S(1)} %collective-permute-done.4.refs_1_), channel_id=1, source_target_pairs={{1,0},{0,1},{3,2},{2,3},{5,4},{4,5},{7,6},{6,7},{9,8},{8,9},{11,10... | collective-permute-start | bytes 208904 | tf_op jit(solution)/shard_map/ppermute | solution.py:416
  20.6 1.0 %collective-permute-start.7 = (bf16[272,128]{1,0:T(8,128)(2,1)S(1)}, bf16[272,128]{1,0:T(8,128)(2,1)S(1)}, u32[]{:S(2)}, u32[]{:S(2)}) collective-permute-start(bf16[272,128]{1,0:T(8,128)(2,1)S(1)} %collective-permute-done.5.refs_2_), channel_id=1, source_target_pairs={{1,0},{0,1},{3,2},{2,3},{5,4},{4,5},{7,6},{6,7},{9,8},{8,9},{11,10... | collective-permute-start | bytes 208904 | tf_op jit(solution)/shard_map/ppermute | solution.py:416
  21.6 0.0 collective-permute-done.9
  21.6 0.1 collective-permute-start.11
  21.7 0.9 %collective-permute-done.8 = f32[1,128]{1,0:T(1,128)S(1)} collective-permute-done((f32[1,128]{1,0:T(1,128)S(1)}, f32[1,128]{1,0:T(1,128)S(1)}, u32[]{:S(2)}, u32[]{:S(2)}) %collective-permute-start.8) | collective-permute-done | bytes 544 | tf_op jit(solution)/shard_map/ppermute | solution.py:445
  22.5 1.3 %collective-permute-done.6.refs_5_ = bf16[272,128]{1,0:T(8,128)(2,1)S(1)} collective-permute-done((bf16[272,128]{1,0:T(8,128)(2,1)S(1)}, bf16[272,128]{1,0:T(8,128)(2,1)S(1)}, u32[]{:S(2)}, u32[]{:S(2)}) %collective-permute-start.6) | collective-permute-done | bytes 69664 | tf_op jit(solution)/shard_map/ppermute | solution.py:416
  23.8 1.1 %collective-permute-done.7.refs_6_ = bf16[272,128]{1,0:T(8,128)(2,1)S(1)} collective-permute-done((bf16[272,128]{1,0:T(8,128)(2,1)S(1)}, bf16[272,128]{1,0:T(8,128)(2,1)S(1)}, u32[]{:S(2)}, u32[]{:S(2)}) %collective-permute-start.7) | collective-permute-done | bytes 69664 | tf_op jit(solution)/shard_map/ppermute | solution.py:416
  24.9 0.0 collective-permute-done.10.refs_10_
  25.0 0.0 collective-permute-done.11.refs_11_
  25.0 0.1 collective-permute-start.12
  25.0 0.5 %pair_products.1.products = f32[32,8,32,128]{3,2,1,0:T(8,128)S(1)} custom-call(f32[272,128]{1,0:T(8,128)S(1)} %convert_element_type.24.refs_0_.refs_8_, bf16[272,128]{1,0:T(8,128)(2,1)S(1)} %collective-permute-done.4.refs_1_, bf16[272,128]{1,0:T(8,128)(2,1)S(1)} %collective-permute-done.5.refs_2_, bf16[272,128]{1,0:T(8,128)(2,1)S(1)} %collective-permute-done.2.refs_3_, ...), custom_call_target="tpu_custom_call" | custom-call | flops 4194304 | bytes 2097152 | tf_op jit(solution)/shard_map/pair_products/pallas_call | solution.py:333
  25.5 0.6 %collective-permute-done.12 = f32[1,128]{1,0:T(1,128)S(1)} collective-permute-done((f32[1,128]{1,0:T(1,128)S(1)}, f32[1,128]{1,0:T(1,128)S(1)}, u32[]{:S(2)}, u32[]{:S(2)}) %collective-permute-start.12) | collective-permute-done | bytes 544 | tf_op jit(solution)/shard_map/ppermute | solution.py:416
  26.2 1.2 %stack.1 = f32[8,4,1,2,512]{4,3,2,1,0:T(2,128)} custom-call(f32[1,128]{1,0:T(1,128)S(1)} %add.69.energy, f32[32,8,32,128]{3,2,1,0:T(8,128)S(1)} %pair_products.1.products), custom_call_target="tpu_custom_call" | custom-call | flops 4194304 | bytes 2097152 | tf_op jit(solution)/shard_map/stack/pallas_call | solution.py:393
  (8 shorter events, 0.1 us)
Async XLA Ops:
  3.7 8.9 %collective-permute-start.2 = (bf16[272,128]{1,0:T(8,128)(2,1)}, bf16[272,128]{1,0:T(8,128)(2,1)S(1)}, u32[]{:S(2)}, u32[]{:S(2)}) collective-permute-start(bf16[272,128]{1,0:T(8,128)(2,1)} %transform.1), channel_id=1, source_target_pairs={{6,0},{4,2},{2,4},{0,6},{7,1},{5,3},{3,5},{1,7},{14,8},{12,10},{10... | collective-permute-start | bytes 208904 | tf_op jit(solution)/shard_map/ppermute | solution.py:416
  8.8 6.1 %collective-permute-start.5 = (bf16[272,128]{1,0:T(8,128)(2,1)}, bf16[272,128]{1,0:T(8,128)(2,1)S(1)}, u32[]{:S(2)}, u32[]{:S(2)}) collective-permute-start(bf16[272,128]{1,0:T(8,128)(2,1)} %transform.1), channel_id=1, source_target_pairs={{4,0},{6,2},{0,4},{2,6},{5,1},{7,3},{1,5},{3,7},{12,8},{14,10},{8,... | collective-permute-start | bytes 208904 | tf_op jit(solution)/shard_map/ppermute | solution.py:416
  8.9 6.1 %collective-permute-start.4 = (bf16[272,128]{1,0:T(8,128)(2,1)}, bf16[272,128]{1,0:T(8,128)(2,1)S(1)}, u32[]{:S(2)}, u32[]{:S(2)}) collective-permute-start(bf16[272,128]{1,0:T(8,128)(2,1)} %transform.1), channel_id=1, source_target_pairs={{2,0},{0,2},{6,4},{4,6},{3,1},{1,3},{7,5},{5,7},{10,8},{8,10},{14,... | collective-permute-start | bytes 208904 | tf_op jit(solution)/shard_map/ppermute | solution.py:416
  9.5 5.5 %collective-permute-start.1 = (bf16[272,128]{1,0:T(8,128)(2,1)}, bf16[272,128]{1,0:T(8,128)(2,1)S(1)}, u32[]{:S(2)}, u32[]{:S(2)}) collective-permute-start(bf16[272,128]{1,0:T(8,128)(2,1)} %transform.1), channel_id=1, source_target_pairs={{16,0},{0,16},{17,1},{1,17},{18,2},{2,18},{19,3},{3,19},{20,4},{4,... | collective-permute-start | bytes 208904 | tf_op jit(solution)/shard_map/ppermute | solution.py:416
  11.1 4.5 %collective-permute-start = (bf16[272,128]{1,0:T(8,128)(2,1)}, bf16[272,128]{1,0:T(8,128)(2,1)S(1)}, u32[]{:S(2)}, u32[]{:S(2)}) collective-permute-start(bf16[272,128]{1,0:T(8,128)(2,1)} %transform.1), channel_id=1, source_target_pairs={{1,0},{0,1},{3,2},{2,3},{5,4},{4,5},{7,6},{6,7},{9,8},{8,9},{11,10... | collective-permute-start | bytes 208904 | tf_op jit(solution)/shard_map/ppermute | solution.py:416
  12.7 4.3 %collective-permute-start.3 = (bf16[272,128]{1,0:T(8,128)(2,1)S(1)}, bf16[272,128]{1,0:T(8,128)(2,1)S(1)}, u32[]{:S(2)}, u32[]{:S(2)}) collective-permute-start(bf16[272,128]{1,0:T(8,128)(2,1)S(1)} %collective-permute-done.2.refs_3_), channel_id=1, source_target_pairs={{1,0},{0,1},{3,2},{2,3},{5,4},{4,5},{7,6},{6,7},{9,8},{8,9},{11,10... | collective-permute-start | bytes 208904 | tf_op jit(solution)/shard_map/ppermute | solution.py:416
  15.0 10.0 %collective-permute-start.10 = (bf16[272,128]{1,0:T(8,128)(2,1)}, bf16[272,128]{1,0:T(8,128)(2,1)S(1)}, u32[]{:S(2)}, u32[]{:S(2)}) collective-permute-start(bf16[272,128]{1,0:T(8,128)(2,1)} %transform.1), channel_id=1, source_target_pairs={{8,0},{0,8},{9,1},{1,9},{10,2},{2,10},{11,3},{3,11},{12,4},{4,12},... | collective-permute-start | bytes 208904 | tf_op jit(solution)/shard_map/ppermute | solution.py:416
  17.0 4.5 %collective-permute-start.9 = (f32[1,128]{1,0:T(1,128)S(1)}, f32[1,128]{1,0:T(1,128)S(1)}, u32[]{:S(2)}, u32[]{:S(2)}) collective-permute-start(f32[1,128]{1,0:T(1,128)S(1)} %add_bitcast_fusion), channel_id=1, source_target_pairs={{17,0},{16,1},{1,16},{0,17},{19,2},{18,3},{3,18},{2,19},{21,4},{20... | collective-permute-start | bytes 1544 | tf_op jit(solution)/shard_map/ppermute | solution.py:445
  19.0 3.5 %collective-permute-start.8 = (f32[1,128]{1,0:T(1,128)S(1)}, f32[1,128]{1,0:T(1,128)S(1)}, u32[]{:S(2)}, u32[]{:S(2)}) collective-permute-start(f32[1,128]{1,0:T(1,128)S(1)} %add_bitcast_fusion), channel_id=1, source_target_pairs={{16,0},{17,1},{0,16},{1,17},{18,2},{19,3},{2,18},{3,19},{20,4},{21... | collective-permute-start | bytes 1544 | tf_op jit(solution)/shard_map/ppermute | solution.py:445
  19.5 4.3 %collective-permute-start.6 = (bf16[272,128]{1,0:T(8,128)(2,1)S(1)}, bf16[272,128]{1,0:T(8,128)(2,1)S(1)}, u32[]{:S(2)}, u32[]{:S(2)}) collective-permute-start(bf16[272,128]{1,0:T(8,128)(2,1)S(1)} %collective-permute-done.4.refs_1_), channel_id=1, source_target_pairs={{1,0},{0,1},{3,2},{2,3},{5,4},{4,5},{7,6},{6,7},{9,8},{8,9},{11,10... | collective-permute-start | bytes 208904 | tf_op jit(solution)/shard_map/ppermute | solution.py:416
  20.6 4.3 %collective-permute-start.7 = (bf16[272,128]{1,0:T(8,128)(2,1)S(1)}, bf16[272,128]{1,0:T(8,128)(2,1)S(1)}, u32[]{:S(2)}, u32[]{:S(2)}) collective-permute-start(bf16[272,128]{1,0:T(8,128)(2,1)S(1)} %collective-permute-done.5.refs_2_), channel_id=1, source_target_pairs={{1,0},{0,1},{3,2},{2,3},{5,4},{4,5},{7,6},{6,7},{9,8},{8,9},{11,10... | collective-permute-start | bytes 208904 | tf_op jit(solution)/shard_map/ppermute | solution.py:416
  21.6 3.4 %collective-permute-start.11 = (bf16[272,128]{1,0:T(8,128)(2,1)S(1)}, bf16[272,128]{1,0:T(8,128)(2,1)S(1)}, u32[]{:S(2)}, u32[]{:S(2)}) collective-permute-start(bf16[272,128]{1,0:T(8,128)(2,1)S(1)} %collective-permute-done.1.refs_9_), channel_id=1, source_target_pairs={{8,0},{0,8},{9,1},{1,9},{10,2},{2,10},{11,3},{3,11},{12,4},{4,12},... | collective-permute-start | bytes 208904 | tf_op jit(solution)/shard_map/ppermute | solution.py:416
  25.0 1.2 %collective-permute-start.12 = (f32[1,128]{1,0:T(1,128)S(1)}, f32[1,128]{1,0:T(1,128)S(1)}, u32[]{:S(2)}, u32[]{:S(2)}) collective-permute-start(f32[1,128]{1,0:T(1,128)S(1)} %fusion.1), channel_id=1, source_target_pairs={{8,0},{0,8},{9,1},{1,9},{10,2},{2,10},{11,3},{3,11},{12,4},{4,12},... | collective-permute-start | bytes 1544 | tf_op jit(solution)/shard_map/ppermute | solution.py:416

commit v6 on v5

--- a/solution.py
+++ b/solution.py
@@ -428,28 +428,15 @@
     column = [own] + fetch_all(own, "z", z_size)
     beside = fetch_all(own, "x", x_size)
     other = fetch_all(own, "y", y_size)
-    soon = [fetch(w, "y", y_size, step) for w in column[3:] for step in range(1, y_size)]
+    forward = [fetch(w, "y", y_size, step) for w in column[1:] for step in range(1, y_size)]
     kept = own.astype(jnp.float32)
-    other, beside, soon, column, kept = lax.optimization_barrier((other, beside, soon, column, kept))
-    near = functools.reduce(jnp.add, [energy_of(w) for w in column[1:]], energy_of(kept))
-
-    forward = [fetch(w, "y", y_size, step) for w in column[1:3] for step in range(1, y_size)]
-    far = []
-    for i in range(1, x_size):
-        for j in range(y_size):
-            pairs = [
-                (partners(x_size)[i](x) * y_size + partners(y_size)[j](y), x * y_size + y)
-                for x in range(x_size)
-                for y in range(y_size)
-            ]
-            far.append(lax.ppermute(near, ("x", "y"), pairs))
-    forward, far, near = lax.optimization_barrier((forward, far, near))
-    forward = forward + soon
-    energy = functools.reduce(jnp.add, [energy_of(w) for w in other + forward], near)
-    energy = functools.reduce(jnp.add, far, energy)
+    other, forward, beside, column, kept = lax.optimization_barrier((other, forward, beside, column, kept))
+    column_energy = [energy_of(w) for w in [kept] + column[1:] + other + forward]
+    energy = functools.reduce(jnp.add, column_energy)
 
     right = [kept] + beside
     right = right + [fetch(w, "c", c_size, step) for step in range(1, c_size) for w in [own] + beside]
+    energy = functools.reduce(jnp.add, fetch_all(energy, "x", x_size), energy)
     energy, right = lax.optimization_barrier((energy, right))
     energy = functools.reduce(jnp.add, fetch_all(energy, "c", c_size), energy)
     left = [kept] + column[1:] + other + forward

time: 27.5 us -> 27.1 us (0.985)
  starting transfers between devices: 14.5 us -> 13.6 us
  waiting for transfers between devices: 6.31 us -> 6.84 us
    ppermute x2 -> x0, starting transfers between devices: 2.49 us -> none  [per_device(): far.append(lax.ppermute(near, ('x', 'y'), pairs))]
    ppermute x11 -> x12, starting transfers between devices: 12.1 us -> 13.6 us  [fetch(): return lax.ppermute(x, axis, [(source(p), p) for p in range(size)])]
    ppermute x11 -> x12, waiting for transfers between devices: 5.44 us -> 6.84 us  [fetch(): return lax.ppermute(x, axis, [(source(p), p) for p in range(size)])]
    ppermute x2 -> x0, waiting for transfers between devices: 0.87 us -> none  [per_device(): far.append(lax.ppermute(near, ('x', 'y'), pairs))]
  transfers between devices with their start and end apart: 13 -> 12, of which waited for: 7 -> 5; matrix products, arithmetic and copies ran while one was open for 4% -> 4% of each run, Pallas kernels for 2% -> 2%
where the time goes in v6:
time: 27.1 us; the launch traced here: 26.9 us
  starting transfers between devices  13.6 us (50%)
  waiting for transfers between devices  6.84 us (25%)
  Pallas kernels  5.37 us (20%)
  other arithmetic  0.99 us (4%)
    ppermute x12, starting transfers between devices, fetch(): return lax.ppermute(x, axis, [(source(p), p) for p in range(size)])  13.6 us
    ppermute x12, waiting for transfers between devices, fetch(): return lax.ppermute(x, axis, [(source(p), p) for p in range(size)])  6.84 us
    pallas_call x1, Pallas kernels, transform(): pl.pallas_call(functools.partial(transform_kernel, count, groups, rows, w...  3.74 us
    pallas_call x1, Pallas kernels, stack(): pl.pallas_call(functools.partial(stack_kernel, left_count, right_count, c...  1.15 us
    convert_element_type x1, other arithmetic, per_device(): kept = own.astype(jnp.float32)  0.89 us
  transfers between devices with their start and end apart: 12, of which 5 were waited for; matrix products, arithmetic and copies ran while one was open for 4% of the time, Pallas kernels for 2%

profile of v6, /device:TPU:0, one launch (start us, length us, event | category | flops | bytes accessed | tf_op | source)
XLA Modules:
  0.0 26.9 jit_solution(12220888293518334144)
XLA Ops:
  0.0 3.7 %transform.1 = bf16[272,128]{1,0:T(8,128)(2,1)} custom-call(s32[32]{0:T(128)} %offsets_hbm.1, bf16[1,192000]{1,0:T(2,128)(2,1)} %strain_hbm.1, s32[512]{0:T(512)} %bins_hbm.1), custom_call_target="tpu_custom_call" | custom-call | flops 419430400 | bytes 6291456 | tf_op jit(solution)/shard_map/transform/pallas_call | solution.py:212
  3.8 5.1 %collective-permute-start.5 = (bf16[272,128]{1,0:T(8,128)(2,1)}, bf16[272,128]{1,0:T(8,128)(2,1)S(1)}, u32[]{:S(2)}, u32[]{:S(2)}) collective-permute-start(bf16[272,128]{1,0:T(8,128)(2,1)} %transform.1), channel_id=1, source_target_pairs={{6,0},{4,2},{2,4},{0,6},{7,1},{5,3},{3,5},{1,7},{14,8},{12,10},{10... | collective-permute-start | bytes 208904 | tf_op jit(solution)/shard_map/ppermute | solution.py:416
  8.9 0.0 collective-permute-start.3
  8.9 0.6 %collective-permute-start.1 = (bf16[272,128]{1,0:T(8,128)(2,1)}, bf16[272,128]{1,0:T(8,128)(2,1)S(1)}, u32[]{:S(2)}, u32[]{:S(2)}) collective-permute-start(bf16[272,128]{1,0:T(8,128)(2,1)} %transform.1), channel_id=1, source_target_pairs={{2,0},{0,2},{6,4},{4,6},{3,1},{1,3},{7,5},{5,7},{10,8},{8,10},{14,... | collective-permute-start | bytes 208904 | tf_op jit(solution)/shard_map/ppermute | solution.py:416
  9.5 1.6 %collective-permute-start.7 = (bf16[272,128]{1,0:T(8,128)(2,1)}, bf16[272,128]{1,0:T(8,128)(2,1)S(1)}, u32[]{:S(2)}, u32[]{:S(2)}) collective-permute-start(bf16[272,128]{1,0:T(8,128)(2,1)} %transform.1), channel_id=1, source_target_pairs={{16,0},{0,16},{17,1},{1,17},{18,2},{2,18},{19,3},{3,19},{20,4},{4,... | collective-permute-start | bytes 208904 | tf_op jit(solution)/shard_map/ppermute | solution.py:416
  11.1 1.5 %collective-permute-start = (bf16[272,128]{1,0:T(8,128)(2,1)}, bf16[272,128]{1,0:T(8,128)(2,1)S(1)}, u32[]{:S(2)}, u32[]{:S(2)}) collective-permute-start(bf16[272,128]{1,0:T(8,128)(2,1)} %transform.1), channel_id=1, source_target_pairs={{1,0},{0,1},{3,2},{2,3},{5,4},{4,5},{7,6},{6,7},{9,8},{8,9},{11,10... | collective-permute-start | bytes 208904 | tf_op jit(solution)/shard_map/ppermute | solution.py:416
  12.6 0.0 collective-permute-done.5.refs_3_
  12.6 1.0 %collective-permute-start.6 = (bf16[272,128]{1,0:T(8,128)(2,1)S(1)}, bf16[272,128]{1,0:T(8,128)(2,1)S(1)}, u32[]{:S(2)}, u32[]{:S(2)}) collective-permute-start(bf16[272,128]{1,0:T(8,128)(2,1)S(1)} %collective-permute-done.5.refs_3_), channel_id=1, source_target_pairs={{1,0},{0,1},{3,2},{2,3},{5,4},{4,5},{7,6},{6,7},{9,8},{8,9},{11,10... | collective-permute-start | bytes 208904 | tf_op jit(solution)/shard_map/ppermute | solution.py:416
  13.6 1.3 %collective-permute-done.3.refs_2_ = bf16[272,128]{1,0:T(8,128)(2,1)S(1)} collective-permute-done((bf16[272,128]{1,0:T(8,128)(2,1)}, bf16[272,128]{1,0:T(8,128)(2,1)S(1)}, u32[]{:S(2)}, u32[]{:S(2)}) %collective-permute-start.3) | collective-permute-done | bytes 69664 | tf_op jit(solution)/shard_map/ppermute | solution.py:416
  15.0 1.5 %collective-permute-start.4 = (bf16[272,128]{1,0:T(8,128)(2,1)S(1)}, bf16[272,128]{1,0:T(8,128)(2,1)S(1)}, u32[]{:S(2)}, u32[]{:S(2)}) collective-permute-start(bf16[272,128]{1,0:T(8,128)(2,1)S(1)} %collective-permute-done.3.refs_2_), channel_id=1, source_target_pairs={{1,0},{0,1},{3,2},{2,3},{5,4},{4,5},{7,6},{6,7},{9,8},{8,9},{11,10... | collective-permute-start | bytes 208904 | tf_op jit(solution)/shard_map/ppermute | solution.py:416
  16.5 0.0 collective-permute-done.1.refs_1_
  16.5 0.5 %collective-permute-start.2 = (bf16[272,128]{1,0:T(8,128)(2,1)S(1)}, bf16[272,128]{1,0:T(8,128)(2,1)S(1)}, u32[]{:S(2)}, u32[]{:S(2)}) collective-permute-start(bf16[272,128]{1,0:T(8,128)(2,1)S(1)} %collective-permute-done.1.refs_1_), channel_id=1, source_target_pairs={{1,0},{0,1},{3,2},{2,3},{5,4},{4,5},{7,6},{6,7},{9,8},{8,9},{11,10... | collective-permute-start | bytes 208904 | tf_op jit(solution)/shard_map/ppermute | solution.py:416
  17.0 0.9 %convert_element_type.24.refs_0_.refs_8_ = f32[272,128]{1,0:T(8,128)S(1)} convert(bf16[272,128]{1,0:T(8,128)(2,1)} %transform.1) | non-fusion elementwise | flops 34816 | bytes 208896 | tf_op jit(solution)/shard_map/convert_element_type | solution.py:432
  17.9 0.0 collective-permute-done.7.refs_9_
  17.9 0.1 collective-permute-start.9
  18.0 0.0 collective-permute-done.refs_4_
  18.0 0.0 collective-permute-done.6.refs_7_
  18.0 1.9 %collective-permute-done.4.refs_6_ = bf16[272,128]{1,0:T(8,128)(2,1)S(1)} collective-permute-done((bf16[272,128]{1,0:T(8,128)(2,1)S(1)}, bf16[272,128]{1,0:T(8,128)(2,1)S(1)}, u32[]{:S(2)}, u32[]{:S(2)}) %collective-permute-start.4) | collective-permute-done | bytes 69664 | tf_op jit(solution)/shard_map/ppermute | solution.py:416
  19.9 0.9 %collective-permute-done.2.refs_5_ = bf16[272,128]{1,0:T(8,128)(2,1)S(1)} collective-permute-done((bf16[272,128]{1,0:T(8,128)(2,1)S(1)}, bf16[272,128]{1,0:T(8,128)(2,1)S(1)}, u32[]{:S(2)}, u32[]{:S(2)}) %collective-permute-start.2) | collective-permute-done | bytes 69664 | tf_op jit(solution)/shard_map/ppermute | solution.py:416
  20.8 0.0 collective-permute-start.10
  20.9 1.6 %collective-permute-start.8 = (f32[1,128]{1,0:T(1,128)S(1)}, f32[1,128]{1,0:T(1,128)S(1)}, u32[]{:S(2)}, u32[]{:S(2)}) collective-permute-start(f32[1,128]{1,0:T(1,128)S(1)} %add_bitcast_fusion), channel_id=1, source_target_pairs={{16,0},{0,16},{17,1},{1,17},{18,2},{2,18},{19,3},{3,19},{20,4},{4,... | collective-permute-start | bytes 1544 | tf_op jit(solution)/shard_map/ppermute | solution.py:416
  22.5 2.0 %collective-permute-done.8 = f32[1,128]{1,0:T(1,128)S(1)} collective-permute-done((f32[1,128]{1,0:T(1,128)S(1)}, f32[1,128]{1,0:T(1,128)S(1)}, u32[]{:S(2)}, u32[]{:S(2)}) %collective-permute-start.8) | collective-permute-done | bytes 544 | tf_op jit(solution)/shard_map/ppermute | solution.py:416
  24.5 0.0 collective-permute-done.9.refs_10_
  24.5 0.0 collective-permute-done.10.refs_11_
  24.5 0.1 collective-permute-start.11
  24.6 0.5 %pair_products.1.products = f32[32,8,32,128]{3,2,1,0:T(8,128)S(1)} custom-call(f32[272,128]{1,0:T(8,128)S(1)} %convert_element_type.24.refs_0_.refs_8_, bf16[272,128]{1,0:T(8,128)(2,1)S(1)} %collective-permute-done.1.refs_1_, bf16[272,128]{1,0:T(8,128)(2,1)S(1)} %collective-permute-done.3.refs_2_, bf16[272,128]{1,0:T(8,128)(2,1)S(1)} %collective-permute-done.5.refs_3_, ...), custom_call_target="tpu_custom_call" | custom-call | flops 4194304 | bytes 2097152 | tf_op jit(solution)/shard_map/pair_products/pallas_call | solution.py:333
  25.1 0.6 %collective-permute-done.11 = f32[1,128]{1,0:T(1,128)S(1)} collective-permute-done((f32[1,128]{1,0:T(1,128)S(1)}, f32[1,128]{1,0:T(1,128)S(1)}, u32[]{:S(2)}, u32[]{:S(2)}) %collective-permute-start.11) | collective-permute-done | bytes 544 | tf_op jit(solution)/shard_map/ppermute | solution.py:416
  25.7 1.2 %stack.1 = f32[8,4,1,2,512]{4,3,2,1,0:T(2,128)} custom-call(f32[1,128]{1,0:T(1,128)S(1)} %add.98.energy, f32[32,8,32,128]{3,2,1,0:T(8,128)S(1)} %pair_products.1.products), custom_call_target="tpu_custom_call" | custom-call | flops 4194304 | bytes 2097152 | tf_op jit(solution)/shard_map/stack/pallas_call | solution.py:393
  (7 shorter events, 0.1 us)
Async XLA Ops:
  3.8 8.9 %collective-permute-start.5 = (bf16[272,128]{1,0:T(8,128)(2,1)}, bf16[272,128]{1,0:T(8,128)(2,1)S(1)}, u32[]{:S(2)}, u32[]{:S(2)}) collective-permute-start(bf16[272,128]{1,0:T(8,128)(2,1)} %transform.1), channel_id=1, source_target_pairs={{6,0},{4,2},{2,4},{0,6},{7,1},{5,3},{3,5},{1,7},{14,8},{12,10},{10... | collective-permute-start | bytes 208904 | tf_op jit(solution)/shard_map/ppermute | solution.py:416
  8.9 6.1 %collective-permute-start.3 = (bf16[272,128]{1,0:T(8,128)(2,1)}, bf16[272,128]{1,0:T(8,128)(2,1)S(1)}, u32[]{:S(2)}, u32[]{:S(2)}) collective-permute-start(bf16[272,128]{1,0:T(8,128)(2,1)} %transform.1), channel_id=1, source_target_pairs={{4,0},{6,2},{0,4},{2,6},{5,1},{7,3},{1,5},{3,7},{12,8},{14,10},{8,... | collective-permute-start | bytes 208904 | tf_op jit(solution)/shard_map/ppermute | solution.py:416
  8.9 7.6 %collective-permute-start.1 = (bf16[272,128]{1,0:T(8,128)(2,1)}, bf16[272,128]{1,0:T(8,128)(2,1)S(1)}, u32[]{:S(2)}, u32[]{:S(2)}) collective-permute-start(bf16[272,128]{1,0:T(8,128)(2,1)} %transform.1), channel_id=1, source_target_pairs={{2,0},{0,2},{6,4},{4,6},{3,1},{1,3},{7,5},{5,7},{10,8},{8,10},{14,... | collective-permute-start | bytes 208904 | tf_op jit(solution)/shard_map/ppermute | solution.py:416
  9.5 8.4 %collective-permute-start.7 = (bf16[272,128]{1,0:T(8,128)(2,1)}, bf16[272,128]{1,0:T(8,128)(2,1)S(1)}, u32[]{:S(2)}, u32[]{:S(2)}) collective-permute-start(bf16[272,128]{1,0:T(8,128)(2,1)} %transform.1), channel_id=1, source_target_pairs={{16,0},{0,16},{17,1},{1,17},{18,2},{2,18},{19,3},{3,19},{20,4},{4,... | collective-permute-start | bytes 208904 | tf_op jit(solution)/shard_map/ppermute | solution.py:416
  11.1 6.8 %collective-permute-start = (bf16[272,128]{1,0:T(8,128)(2,1)}, bf16[272,128]{1,0:T(8,128)(2,1)S(1)}, u32[]{:S(2)}, u32[]{:S(2)}) collective-permute-start(bf16[272,128]{1,0:T(8,128)(2,1)} %transform.1), channel_id=1, source_target_pairs={{1,0},{0,1},{3,2},{2,3},{5,4},{4,5},{7,6},{6,7},{9,8},{8,9},{11,10... | collective-permute-start | bytes 208904 | tf_op jit(solution)/shard_map/ppermute | solution.py:416
  12.6 5.3 %collective-permute-start.6 = (bf16[272,128]{1,0:T(8,128)(2,1)S(1)}, bf16[272,128]{1,0:T(8,128)(2,1)S(1)}, u32[]{:S(2)}, u32[]{:S(2)}) collective-permute-start(bf16[272,128]{1,0:T(8,128)(2,1)S(1)} %collective-permute-done.5.refs_3_), channel_id=1, source_target_pairs={{1,0},{0,1},{3,2},{2,3},{5,4},{4,5},{7,6},{6,7},{9,8},{8,9},{11,10... | collective-permute-start | bytes 208904 | tf_op jit(solution)/shard_map/ppermute | solution.py:416
  15.0 5.0 %collective-permute-start.4 = (bf16[272,128]{1,0:T(8,128)(2,1)S(1)}, bf16[272,128]{1,0:T(8,128)(2,1)S(1)}, u32[]{:S(2)}, u32[]{:S(2)}) collective-permute-start(bf16[272,128]{1,0:T(8,128)(2,1)S(1)} %collective-permute-done.3.refs_2_), channel_id=1, source_target_pairs={{1,0},{0,1},{3,2},{2,3},{5,4},{4,5},{7,6},{6,7},{9,8},{8,9},{11,10... | collective-permute-start | bytes 208904 | tf_op jit(solution)/shard_map/ppermute | solution.py:416
  16.5 4.3 %collective-permute-start.2 = (bf16[272,128]{1,0:T(8,128)(2,1)S(1)}, bf16[272,128]{1,0:T(8,128)(2,1)S(1)}, u32[]{:S(2)}, u32[]{:S(2)}) collective-permute-start(bf16[272,128]{1,0:T(8,128)(2,1)S(1)} %collective-permute-done.1.refs_1_), channel_id=1, source_target_pairs={{1,0},{0,1},{3,2},{2,3},{5,4},{4,5},{7,6},{6,7},{9,8},{8,9},{11,10... | collective-permute-start | bytes 208904 | tf_op jit(solution)/shard_map/ppermute | solution.py:416
  17.9 6.6 %collective-permute-start.9 = (bf16[272,128]{1,0:T(8,128)(2,1)}, bf16[272,128]{1,0:T(8,128)(2,1)S(1)}, u32[]{:S(2)}, u32[]{:S(2)}) collective-permute-start(bf16[272,128]{1,0:T(8,128)(2,1)} %transform.1), channel_id=1, source_target_pairs={{8,0},{0,8},{9,1},{1,9},{10,2},{2,10},{11,3},{3,11},{12,4},{4,12},... | collective-permute-start | bytes 208904 | tf_op jit(solution)/shard_map/ppermute | solution.py:416
  20.8 3.7 %collective-permute-start.10 = (bf16[272,128]{1,0:T(8,128)(2,1)S(1)}, bf16[272,128]{1,0:T(8,128)(2,1)S(1)}, u32[]{:S(2)}, u32[]{:S(2)}) collective-permute-start(bf16[272,128]{1,0:T(8,128)(2,1)S(1)} %collective-permute-done.7.refs_9_), channel_id=1, source_target_pairs={{8,0},{0,8},{9,1},{1,9},{10,2},{2,10},{11,3},{3,11},{12,4},{4,12},... | collective-permute-start | bytes 208904 | tf_op jit(solution)/shard_map/ppermute | solution.py:416
  20.9 3.6 %collective-permute-start.8 = (f32[1,128]{1,0:T(1,128)S(1)}, f32[1,128]{1,0:T(1,128)S(1)}, u32[]{:S(2)}, u32[]{:S(2)}) collective-permute-start(f32[1,128]{1,0:T(1,128)S(1)} %add_bitcast_fusion), channel_id=1, source_target_pairs={{16,0},{0,16},{17,1},{1,17},{18,2},{2,18},{19,3},{3,19},{20,4},{4,... | collective-permute-start | bytes 1544 | tf_op jit(solution)/shard_map/ppermute | solution.py:416
  24.5 1.2 %collective-permute-start.11 = (f32[1,128]{1,0:T(1,128)S(1)}, f32[1,128]{1,0:T(1,128)S(1)}, u32[]{:S(2)}, u32[]{:S(2)}) collective-permute-start(f32[1,128]{1,0:T(1,128)S(1)} %add.97), channel_id=1, source_target_pairs={{8,0},{0,8},{9,1},{1,9},{10,2},{2,10},{11,3},{3,11},{12,4},{4,12},... | collective-permute-start | bytes 1544 | tf_op jit(solution)/shard_map/ppermute | solution.py:416

commit v7 on v6

--- a/solution.py
+++ b/solution.py
@@ -131,7 +131,8 @@
 
     def tapered_group(group):
         return jnp.concatenate(
-            [blocks[group, part].astype(jnp.bfloat16) for part in range(steps)], axis=1
+            [blocks[group, part, : rows * some].astype(jnp.bfloat16) for part in range(steps)],
+            axis=1,
         )
 
     def window_sums(powers, tile):
@@ -222,7 +223,7 @@
             pltpu.VMEM((1, width), jnp.float32),
             pltpu.VMEM((lines, LANES), jnp.float32),
             pltpu.VMEM((3, count, LANES), jnp.float32),
-            pltpu.VMEM((groups, DEPTH // LANES, rows * count // groups, LANES), jnp.float32),
+            pltpu.VMEM((groups, DEPTH // LANES, (rows + 1) * count // groups, LANES), jnp.float32),
             pltpu.VMEM((count, LANES), jnp.float32),
             pltpu.VMEM((DEPTH, 2 * width), jnp.bfloat16),
             pltpu.VMEM((2, EDGE + DEPTH // EDGE + rows, width), jnp.float32),

time: 27.1 us -> 27.1 us (level)
  no operation moved by 1% of the time
where the time goes in v7:
time: 27.1 us; the launch traced here: 26.9 us
  starting transfers between devices  13.6 us (50%)
  waiting for transfers between devices  6.81 us (25%)
  Pallas kernels  5.37 us (20%)
  other arithmetic  0.99 us (4%)
    ppermute x12, starting transfers between devices, fetch(): return lax.ppermute(x, axis, [(source(p), p) for p in range(size)])  13.6 us
    ppermute x12, waiting for transfers between devices, fetch(): return lax.ppermute(x, axis, [(source(p), p) for p in range(size)])  6.81 us
    pallas_call x1, Pallas kernels, transform(): pl.pallas_call(functools.partial(transform_kernel, count, groups, rows, w...  3.75 us
    pallas_call x1, Pallas kernels, stack(): pl.pallas_call(functools.partial(stack_kernel, left_count, right_count, c...  1.15 us
    convert_element_type x1, other arithmetic, per_device(): kept = own.astype(jnp.float32)  0.89 us
  transfers between devices with their start and end apart: 12, of which 5 were waited for; matrix products, arithmetic and copies ran while one was open for 4% of the time, Pallas kernels for 2%

profile of v7, /device:TPU:0, one launch (start us, length us, event | category | flops | bytes accessed | tf_op | source)
XLA Modules:
  0.0 26.9 jit_solution(10099123881430579012)
XLA Ops:
  0.0 3.7 %transform.1 = bf16[272,128]{1,0:T(8,128)(2,1)} custom-call(s32[32]{0:T(128)} %offsets_hbm.1, bf16[1,192000]{1,0:T(2,128)(2,1)} %strain_hbm.1, s32[512]{0:T(512)} %bins_hbm.1), custom_call_target="tpu_custom_call" | custom-call | flops 419430400 | bytes 6291456 | tf_op jit(solution)/shard_map/transform/pallas_call | solution.py:213
  3.8 5.1 %collective-permute-start.5 = (bf16[272,128]{1,0:T(8,128)(2,1)}, bf16[272,128]{1,0:T(8,128)(2,1)S(1)}, u32[]{:S(2)}, u32[]{:S(2)}) collective-permute-start(bf16[272,128]{1,0:T(8,128)(2,1)} %transform.1), channel_id=1, source_target_pairs={{6,0},{4,2},{2,4},{0,6},{7,1},{5,3},{3,5},{1,7},{14,8},{12,10},{10... | collective-permute-start | bytes 208904 | tf_op jit(solution)/shard_map/ppermute | solution.py:417
  8.9 0.0 collective-permute-start.3
  8.9 0.6 %collective-permute-start.1 = (bf16[272,128]{1,0:T(8,128)(2,1)}, bf16[272,128]{1,0:T(8,128)(2,1)S(1)}, u32[]{:S(2)}, u32[]{:S(2)}) collective-permute-start(bf16[272,128]{1,0:T(8,128)(2,1)} %transform.1), channel_id=1, source_target_pairs={{2,0},{0,2},{6,4},{4,6},{3,1},{1,3},{7,5},{5,7},{10,8},{8,10},{14,... | collective-permute-start | bytes 208904 | tf_op jit(solution)/shard_map/ppermute | solution.py:417
  9.5 1.6 %collective-permute-start.7 = (bf16[272,128]{1,0:T(8,128)(2,1)}, bf16[272,128]{1,0:T(8,128)(2,1)S(1)}, u32[]{:S(2)}, u32[]{:S(2)}) collective-permute-start(bf16[272,128]{1,0:T(8,128)(2,1)} %transform.1), channel_id=1, source_target_pairs={{16,0},{0,16},{17,1},{1,17},{18,2},{2,18},{19,3},{3,19},{20,4},{4,... | collective-permute-start | bytes 208904 | tf_op jit(solution)/shard_map/ppermute | solution.py:417
  11.1 1.5 %collective-permute-start = (bf16[272,128]{1,0:T(8,128)(2,1)}, bf16[272,128]{1,0:T(8,128)(2,1)S(1)}, u32[]{:S(2)}, u32[]{:S(2)}) collective-permute-start(bf16[272,128]{1,0:T(8,128)(2,1)} %transform.1), channel_id=1, source_target_pairs={{1,0},{0,1},{3,2},{2,3},{5,4},{4,5},{7,6},{6,7},{9,8},{8,9},{11,10... | collective-permute-start | bytes 208904 | tf_op jit(solution)/shard_map/ppermute | solution.py:417
  12.7 0.0 collective-permute-done.5.refs_3_
  12.7 1.0 %collective-permute-start.6 = (bf16[272,128]{1,0:T(8,128)(2,1)S(1)}, bf16[272,128]{1,0:T(8,128)(2,1)S(1)}, u32[]{:S(2)}, u32[]{:S(2)}) collective-permute-start(bf16[272,128]{1,0:T(8,128)(2,1)S(1)} %collective-permute-done.5.refs_3_), channel_id=1, source_target_pairs={{1,0},{0,1},{3,2},{2,3},{5,4},{4,5},{7,6},{6,7},{9,8},{8,9},{11,10... | collective-permute-start | bytes 208904 | tf_op jit(solution)/shard_map/ppermute | solution.py:417
  13.6 1.3 %collective-permute-done.3.refs_2_ = bf16[272,128]{1,0:T(8,128)(2,1)S(1)} collective-permute-done((bf16[272,128]{1,0:T(8,128)(2,1)}, bf16[272,128]{1,0:T(8,128)(2,1)S(1)}, u32[]{:S(2)}, u32[]{:S(2)}) %collective-permute-start.3) | collective-permute-done | bytes 69664 | tf_op jit(solution)/shard_map/ppermute | solution.py:417
  15.0 1.5 %collective-permute-start.4 = (bf16[272,128]{1,0:T(8,128)(2,1)S(1)}, bf16[272,128]{1,0:T(8,128)(2,1)S(1)}, u32[]{:S(2)}, u32[]{:S(2)}) collective-permute-start(bf16[272,128]{1,0:T(8,128)(2,1)S(1)} %collective-permute-done.3.refs_2_), channel_id=1, source_target_pairs={{1,0},{0,1},{3,2},{2,3},{5,4},{4,5},{7,6},{6,7},{9,8},{8,9},{11,10... | collective-permute-start | bytes 208904 | tf_op jit(solution)/shard_map/ppermute | solution.py:417
  16.5 0.0 collective-permute-done.1.refs_1_
  16.5 0.5 %collective-permute-start.2 = (bf16[272,128]{1,0:T(8,128)(2,1)S(1)}, bf16[272,128]{1,0:T(8,128)(2,1)S(1)}, u32[]{:S(2)}, u32[]{:S(2)}) collective-permute-start(bf16[272,128]{1,0:T(8,128)(2,1)S(1)} %collective-permute-done.1.refs_1_), channel_id=1, source_target_pairs={{1,0},{0,1},{3,2},{2,3},{5,4},{4,5},{7,6},{6,7},{9,8},{8,9},{11,10... | collective-permute-start | bytes 208904 | tf_op jit(solution)/shard_map/ppermute | solution.py:417
  17.0 0.9 %convert_element_type.24.refs_0_.refs_8_ = f32[272,128]{1,0:T(8,128)S(1)} convert(bf16[272,128]{1,0:T(8,128)(2,1)} %transform.1) | non-fusion elementwise | flops 34816 | bytes 208896 | tf_op jit(solution)/shard_map/convert_element_type | solution.py:433
  17.9 0.0 collective-permute-done.7.refs_9_
  17.9 0.1 collective-permute-start.9
  18.0 0.0 collective-permute-done.refs_4_
  18.0 0.0 collective-permute-done.6.refs_7_
  18.0 1.9 %collective-permute-done.4.refs_6_ = bf16[272,128]{1,0:T(8,128)(2,1)S(1)} collective-permute-done((bf16[272,128]{1,0:T(8,128)(2,1)S(1)}, bf16[272,128]{1,0:T(8,128)(2,1)S(1)}, u32[]{:S(2)}, u32[]{:S(2)}) %collective-permute-start.4) | collective-permute-done | bytes 69664 | tf_op jit(solution)/shard_map/ppermute | solution.py:417
  19.9 0.9 %collective-permute-done.2.refs_5_ = bf16[272,128]{1,0:T(8,128)(2,1)S(1)} collective-permute-done((bf16[272,128]{1,0:T(8,128)(2,1)S(1)}, bf16[272,128]{1,0:T(8,128)(2,1)S(1)}, u32[]{:S(2)}, u32[]{:S(2)}) %collective-permute-start.2) | collective-permute-done | bytes 69664 | tf_op jit(solution)/shard_map/ppermute | solution.py:417
  20.8 0.0 collective-permute-start.10
  20.9 1.6 %collective-permute-start.8 = (f32[1,128]{1,0:T(1,128)S(1)}, f32[1,128]{1,0:T(1,128)S(1)}, u32[]{:S(2)}, u32[]{:S(2)}) collective-permute-start(f32[1,128]{1,0:T(1,128)S(1)} %add_bitcast_fusion), channel_id=1, source_target_pairs={{16,0},{0,16},{17,1},{1,17},{18,2},{2,18},{19,3},{3,19},{20,4},{4,... | collective-permute-start | bytes 1544 | tf_op jit(solution)/shard_map/ppermute | solution.py:417
  22.5 2.0 %collective-permute-done.8 = f32[1,128]{1,0:T(1,128)S(1)} collective-permute-done((f32[1,128]{1,0:T(1,128)S(1)}, f32[1,128]{1,0:T(1,128)S(1)}, u32[]{:S(2)}, u32[]{:S(2)}) %collective-permute-start.8) | collective-permute-done | bytes 544 | tf_op jit(solution)/shard_map/ppermute | solution.py:417
  24.5 0.0 collective-permute-done.9.refs_10_
  24.5 0.0 collective-permute-done.10.refs_11_
  24.5 0.1 collective-permute-start.11
  24.6 0.5 %pair_products.1.products = f32[32,8,32,128]{3,2,1,0:T(8,128)S(1)} custom-call(f32[272,128]{1,0:T(8,128)S(1)} %convert_element_type.24.refs_0_.refs_8_, bf16[272,128]{1,0:T(8,128)(2,1)S(1)} %collective-permute-done.1.refs_1_, bf16[272,128]{1,0:T(8,128)(2,1)S(1)} %collective-permute-done.3.refs_2_, bf16[272,128]{1,0:T(8,128)(2,1)S(1)} %collective-permute-done.5.refs_3_, ...), custom_call_target="tpu_custom_call" | custom-call | flops 4194304 | bytes 2097152 | tf_op jit(solution)/shard_map/pair_products/pallas_call | solution.py:334
  25.1 0.6 %collective-permute-done.11 = f32[1,128]{1,0:T(1,128)S(1)} collective-permute-done((f32[1,128]{1,0:T(1,128)S(1)}, f32[1,128]{1,0:T(1,128)S(1)}, u32[]{:S(2)}, u32[]{:S(2)}) %collective-permute-start.11) | collective-permute-done | bytes 544 | tf_op jit(solution)/shard_map/ppermute | solution.py:417
  25.7 1.2 %stack.1 = f32[8,4,1,2,512]{4,3,2,1,0:T(2,128)} custom-call(f32[1,128]{1,0:T(1,128)S(1)} %add.98.energy, f32[32,8,32,128]{3,2,1,0:T(8,128)S(1)} %pair_products.1.products), custom_call_target="tpu_custom_call" | custom-call | flops 4194304 | bytes 2097152 | tf_op jit(solution)/shard_map/stack/pallas_call | solution.py:394
  (7 shorter events, 0.1 us)
Async XLA Ops:
  3.8 8.9 %collective-permute-start.5 = (bf16[272,128]{1,0:T(8,128)(2,1)}, bf16[272,128]{1,0:T(8,128)(2,1)S(1)}, u32[]{:S(2)}, u32[]{:S(2)}) collective-permute-start(bf16[272,128]{1,0:T(8,128)(2,1)} %transform.1), channel_id=1, source_target_pairs={{6,0},{4,2},{2,4},{0,6},{7,1},{5,3},{3,5},{1,7},{14,8},{12,10},{10... | collective-permute-start | bytes 208904 | tf_op jit(solution)/shard_map/ppermute | solution.py:417
  8.9 6.1 %collective-permute-start.3 = (bf16[272,128]{1,0:T(8,128)(2,1)}, bf16[272,128]{1,0:T(8,128)(2,1)S(1)}, u32[]{:S(2)}, u32[]{:S(2)}) collective-permute-start(bf16[272,128]{1,0:T(8,128)(2,1)} %transform.1), channel_id=1, source_target_pairs={{4,0},{6,2},{0,4},{2,6},{5,1},{7,3},{1,5},{3,7},{12,8},{14,10},{8,... | collective-permute-start | bytes 208904 | tf_op jit(solution)/shard_map/ppermute | solution.py:417
  8.9 7.6 %collective-permute-start.1 = (bf16[272,128]{1,0:T(8,128)(2,1)}, bf16[272,128]{1,0:T(8,128)(2,1)S(1)}, u32[]{:S(2)}, u32[]{:S(2)}) collective-permute-start(bf16[272,128]{1,0:T(8,128)(2,1)} %transform.1), channel_id=1, source_target_pairs={{2,0},{0,2},{6,4},{4,6},{3,1},{1,3},{7,5},{5,7},{10,8},{8,10},{14,... | collective-permute-start | bytes 208904 | tf_op jit(solution)/shard_map/ppermute | solution.py:417
  9.5 8.4 %collective-permute-start.7 = (bf16[272,128]{1,0:T(8,128)(2,1)}, bf16[272,128]{1,0:T(8,128)(2,1)S(1)}, u32[]{:S(2)}, u32[]{:S(2)}) collective-permute-start(bf16[272,128]{1,0:T(8,128)(2,1)} %transform.1), channel_id=1, source_target_pairs={{16,0},{0,16},{17,1},{1,17},{18,2},{2,18},{19,3},{3,19},{20,4},{4,... | collective-permute-start | bytes 208904 | tf_op jit(solution)/shard_map/ppermute | solution.py:417
  11.1 6.9 %collective-permute-start = (bf16[272,128]{1,0:T(8,128)(2,1)}, bf16[272,128]{1,0:T(8,128)(2,1)S(1)}, u32[]{:S(2)}, u32[]{:S(2)}) collective-permute-start(bf16[272,128]{1,0:T(8,128)(2,1)} %transform.1), channel_id=1, source_target_pairs={{1,0},{0,1},{3,2},{2,3},{5,4},{4,5},{7,6},{6,7},{9,8},{8,9},{11,10... | collective-permute-start | bytes 208904 | tf_op jit(solution)/shard_map/ppermute | solution.py:417
  12.7 5.3 %collective-permute-start.6 = (bf16[272,128]{1,0:T(8,128)(2,1)S(1)}, bf16[272,128]{1,0:T(8,128)(2,1)S(1)}, u32[]{:S(2)}, u32[]{:S(2)}) collective-permute-start(bf16[272,128]{1,0:T(8,128)(2,1)S(1)} %collective-permute-done.5.refs_3_), channel_id=1, source_target_pairs={{1,0},{0,1},{3,2},{2,3},{5,4},{4,5},{7,6},{6,7},{9,8},{8,9},{11,10... | collective-permute-start | bytes 208904 | tf_op jit(solution)/shard_map/ppermute | solution.py:417
  15.0 5.0 %collective-permute-start.4 = (bf16[272,128]{1,0:T(8,128)(2,1)S(1)}, bf16[272,128]{1,0:T(8,128)(2,1)S(1)}, u32[]{:S(2)}, u32[]{:S(2)}) collective-permute-start(bf16[272,128]{1,0:T(8,128)(2,1)S(1)} %collective-permute-done.3.refs_2_), channel_id=1, source_target_pairs={{1,0},{0,1},{3,2},{2,3},{5,4},{4,5},{7,6},{6,7},{9,8},{8,9},{11,10... | collective-permute-start | bytes 208904 | tf_op jit(solution)/shard_map/ppermute | solution.py:417
  16.5 4.3 %collective-permute-start.2 = (bf16[272,128]{1,0:T(8,128)(2,1)S(1)}, bf16[272,128]{1,0:T(8,128)(2,1)S(1)}, u32[]{:S(2)}, u32[]{:S(2)}) collective-permute-start(bf16[272,128]{1,0:T(8,128)(2,1)S(1)} %collective-permute-done.1.refs_1_), channel_id=1, source_target_pairs={{1,0},{0,1},{3,2},{2,3},{5,4},{4,5},{7,6},{6,7},{9,8},{8,9},{11,10... | collective-permute-start | bytes 208904 | tf_op jit(solution)/shard_map/ppermute | solution.py:417
  17.9 6.6 %collective-permute-start.9 = (bf16[272,128]{1,0:T(8,128)(2,1)}, bf16[272,128]{1,0:T(8,128)(2,1)S(1)}, u32[]{:S(2)}, u32[]{:S(2)}) collective-permute-start(bf16[272,128]{1,0:T(8,128)(2,1)} %transform.1), channel_id=1, source_target_pairs={{8,0},{0,8},{9,1},{1,9},{10,2},{2,10},{11,3},{3,11},{12,4},{4,12},... | collective-permute-start | bytes 208904 | tf_op jit(solution)/shard_map/ppermute | solution.py:417
  20.8 3.7 %collective-permute-start.10 = (bf16[272,128]{1,0:T(8,128)(2,1)S(1)}, bf16[272,128]{1,0:T(8,128)(2,1)S(1)}, u32[]{:S(2)}, u32[]{:S(2)}) collective-permute-start(bf16[272,128]{1,0:T(8,128)(2,1)S(1)} %collective-permute-done.7.refs_9_), channel_id=1, source_target_pairs={{8,0},{0,8},{9,1},{1,9},{10,2},{2,10},{11,3},{3,11},{12,4},{4,12},... | collective-permute-start | bytes 208904 | tf_op jit(solution)/shard_map/ppermute | solution.py:417
  20.9 3.6 %collective-permute-start.8 = (f32[1,128]{1,0:T(1,128)S(1)}, f32[1,128]{1,0:T(1,128)S(1)}, u32[]{:S(2)}, u32[]{:S(2)}) collective-permute-start(f32[1,128]{1,0:T(1,128)S(1)} %add_bitcast_fusion), channel_id=1, source_target_pairs={{16,0},{0,16},{17,1},{1,17},{18,2},{2,18},{19,3},{3,19},{20,4},{4,... | collective-permute-start | bytes 1544 | tf_op jit(solution)/shard_map/ppermute | solution.py:417
  24.5 1.2 %collective-permute-start.11 = (f32[1,128]{1,0:T(1,128)S(1)}, f32[1,128]{1,0:T(1,128)S(1)}, u32[]{:S(2)}, u32[]{:S(2)}) collective-permute-start(f32[1,128]{1,0:T(1,128)S(1)} %add.97), channel_id=1, source_target_pairs={{8,0},{0,8},{9,1},{1,9},{10,2},{2,10},{11,3},{3,11},{12,4},{4,12},... | collective-permute-start | bytes 1544 | tf_op jit(solution)/shard_map/ppermute | solution.py:417

commit v8 on v7

--- a/solution.py
+++ b/solution.py
@@ -435,11 +435,20 @@
     column_energy = [energy_of(w) for w in [kept] + column[1:] + other + forward]
     energy = functools.reduce(jnp.add, column_energy)
 
+    energy, beside, column = lax.optimization_barrier((energy, beside, column))
+    parts = []
+    for i in range(x_size):
+        for j in range(c_size):
+            f, g = partners(x_size)[i], partners(c_size)[j]
+            pairs = [
+                (f(x) * c_size + g(c), x * c_size + c) for x in range(x_size) for c in range(c_size)
+            ]
+            if i or j:
+                parts.append(lax.ppermute(energy, ("x", "c"), pairs))
+    energy = functools.reduce(jnp.add, parts, energy)
+    swapped = [column[0]] + beside
     right = [kept] + beside
-    right = right + [fetch(w, "c", c_size, step) for step in range(1, c_size) for w in [own] + beside]
-    energy = functools.reduce(jnp.add, fetch_all(energy, "x", x_size), energy)
-    energy, right = lax.optimization_barrier((energy, right))
-    energy = functools.reduce(jnp.add, fetch_all(energy, "c", c_size), energy)
+    right = right + [fetch(w, "c", c_size, step) for step in range(1, c_size) for w in swapped]
     left = [kept] + column[1:] + other + forward
     count, width = offsets.shape[0], bins.shape[0]
     if len(left) * len(right) * count * 2 * width * 4 > PRODUCT_BYTES:

time: 27.1 us -> 26.7 us (0.985)
  waiting for transfers between devices: 6.81 us -> 5.72 us
  starting transfers between devices: 13.6 us -> 14.3 us
    ppermute x12 -> x10, waiting for transfers between devices: 6.81 us -> 4.22 us  [fetch(): return lax.ppermute(x, axis, [(source(p), p) for p in range(size)])]
    ppermute x0 -> x3, starting transfers between devices: none -> 1.93 us  [per_device(): parts.append(lax.ppermute(energy, ('x', 'c'), pairs))]
    ppermute x0 -> x3, waiting for transfers between devices: none -> 1.5 us  [per_device(): parts.append(lax.ppermute(energy, ('x', 'c'), pairs))]
    ppermute x12 -> x10, starting transfers between devices: 13.6 us -> 12.4 us  [fetch(): return lax.ppermute(x, axis, [(source(p), p) for p in range(size)])]
  transfers between devices with their start and end apart: 12 -> 13, of which waited for: 5 -> 5; matrix products, arithmetic and copies ran while one was open for 4% -> 3% of each run, Pallas kernels for 2% -> 0%
where the time goes in v8:
time: 26.7 us; the launch traced here: 26.5 us
  starting transfers between devices  14.3 us (54%)
  waiting for transfers between devices  5.72 us (21%)
  Pallas kernels  5.36 us (20%)
  other arithmetic  0.99 us (4%)
    ppermute x10, starting transfers between devices, fetch(): return lax.ppermute(x, axis, [(source(p), p) for p in range(size)])  12.4 us
    ppermute x10, waiting for transfers between devices, fetch(): return lax.ppermute(x, axis, [(source(p), p) for p in range(size)])  4.22 us
    pallas_call x1, Pallas kernels, transform(): pl.pallas_call(functools.partial(transform_kernel, count, groups, rows, w...  3.74 us
    ppermute x3, starting transfers between devices, per_device(): parts.append(lax.ppermute(energy, ('x', 'c'), pairs))  1.93 us
    ppermute x3, waiting for transfers between devices, per_device(): parts.append(lax.ppermute(energy, ('x', 'c'), pairs))  1.5 us
    pallas_call x1, Pallas kernels, stack(): pl.pallas_call(functools.partial(stack_kernel, left_count, right_count, c...  1.15 us
    convert_element_type x1, other arithmetic, per_device(): kept = own.astype(jnp.float32)  0.89 us
  transfers between devices with their start and end apart: 13, of which 5 were waited for; matrix products, arithmetic and copies ran while one was open for 3% of the time, Pallas kernels for 0%

profile of v8, /device:TPU:0, one launch (start us, length us, event | category | flops | bytes accessed | tf_op | source)
XLA Modules:
  0.0 26.5 jit_solution(107912501154633465)
XLA Ops:
  0.0 3.7 %transform.1 = bf16[272,128]{1,0:T(8,128)(2,1)} custom-call(s32[32]{0:T(128)} %offsets_hbm.1, bf16[1,192000]{1,0:T(2,128)(2,1)} %strain_hbm.1, s32[512]{0:T(512)} %bins_hbm.1), custom_call_target="tpu_custom_call" | custom-call | flops 419430400 | bytes 6291456 | tf_op jit(solution)/shard_map/transform/pallas_call | solution.py:213
  3.7 5.1 %collective-permute-start.5 = (bf16[272,128]{1,0:T(8,128)(2,1)}, bf16[272,128]{1,0:T(8,128)(2,1)S(1)}, u32[]{:S(2)}, u32[]{:S(2)}) collective-permute-start(bf16[272,128]{1,0:T(8,128)(2,1)} %transform.1), channel_id=1, source_target_pairs={{6,0},{4,2},{2,4},{0,6},{7,1},{5,3},{3,5},{1,7},{14,8},{12,10},{10... | collective-permute-start | bytes 208904 | tf_op jit(solution)/shard_map/ppermute | solution.py:417
  8.8 0.0 collective-permute-start.3
  8.8 0.6 %collective-permute-start.1 = (bf16[272,128]{1,0:T(8,128)(2,1)}, bf16[272,128]{1,0:T(8,128)(2,1)S(1)}, u32[]{:S(2)}, u32[]{:S(2)}) collective-permute-start(bf16[272,128]{1,0:T(8,128)(2,1)} %transform.1), channel_id=1, source_target_pairs={{2,0},{0,2},{6,4},{4,6},{3,1},{1,3},{7,5},{5,7},{10,8},{8,10},{14,... | collective-permute-start | bytes 208904 | tf_op jit(solution)/shard_map/ppermute | solution.py:417
  9.5 1.7 %collective-permute-start.7 = (bf16[272,128]{1,0:T(8,128)(2,1)}, bf16[272,128]{1,0:T(8,128)(2,1)S(1)}, u32[]{:S(2)}, u32[]{:S(2)}) collective-permute-start(bf16[272,128]{1,0:T(8,128)(2,1)} %transform.1), channel_id=1, source_target_pairs={{16,0},{0,16},{17,1},{1,17},{18,2},{2,18},{19,3},{3,19},{20,4},{4,... | collective-permute-start | bytes 208904 | tf_op jit(solution)/shard_map/ppermute | solution.py:417
  11.1 1.5 %collective-permute-start = (bf16[272,128]{1,0:T(8,128)(2,1)}, bf16[272,128]{1,0:T(8,128)(2,1)S(1)}, u32[]{:S(2)}, u32[]{:S(2)}) collective-permute-start(bf16[272,128]{1,0:T(8,128)(2,1)} %transform.1), channel_id=1, source_target_pairs={{1,0},{0,1},{3,2},{2,3},{5,4},{4,5},{7,6},{6,7},{9,8},{8,9},{11,10... | collective-permute-start | bytes 208904 | tf_op jit(solution)/shard_map/ppermute | solution.py:417
  12.7 0.0 collective-permute-done.5.refs_3_
  12.7 1.0 %collective-permute-start.6 = (bf16[272,128]{1,0:T(8,128)(2,1)S(1)}, bf16[272,128]{1,0:T(8,128)(2,1)S(1)}, u32[]{:S(2)}, u32[]{:S(2)}) collective-permute-start(bf16[272,128]{1,0:T(8,128)(2,1)S(1)} %collective-permute-done.5.refs_3_), channel_id=1, source_target_pairs={{1,0},{0,1},{3,2},{2,3},{5,4},{4,5},{7,6},{6,7},{9,8},{8,9},{11,10... | collective-permute-start | bytes 208904 | tf_op jit(solution)/shard_map/ppermute | solution.py:417
  13.6 1.3 %collective-permute-done.3.refs_2_ = bf16[272,128]{1,0:T(8,128)(2,1)S(1)} collective-permute-done((bf16[272,128]{1,0:T(8,128)(2,1)}, bf16[272,128]{1,0:T(8,128)(2,1)S(1)}, u32[]{:S(2)}, u32[]{:S(2)}) %collective-permute-start.3) | collective-permute-done | bytes 69664 | tf_op jit(solution)/shard_map/ppermute | solution.py:417
  15.0 1.5 %collective-permute-start.4 = (bf16[272,128]{1,0:T(8,128)(2,1)S(1)}, bf16[272,128]{1,0:T(8,128)(2,1)S(1)}, u32[]{:S(2)}, u32[]{:S(2)}) collective-permute-start(bf16[272,128]{1,0:T(8,128)(2,1)S(1)} %collective-permute-done.3.refs_2_), channel_id=1, source_target_pairs={{1,0},{0,1},{3,2},{2,3},{5,4},{4,5},{7,6},{6,7},{9,8},{8,9},{11,10... | collective-permute-start | bytes 208904 | tf_op jit(solution)/shard_map/ppermute | solution.py:417
  16.5 0.0 collective-permute-done.1.refs_1_
  16.5 0.5 %collective-permute-start.2 = (bf16[272,128]{1,0:T(8,128)(2,1)S(1)}, bf16[272,128]{1,0:T(8,128)(2,1)S(1)}, u32[]{:S(2)}, u32[]{:S(2)}) collective-permute-start(bf16[272,128]{1,0:T(8,128)(2,1)S(1)} %collective-permute-done.1.refs_1_), channel_id=1, source_target_pairs={{1,0},{0,1},{3,2},{2,3},{5,4},{4,5},{7,6},{6,7},{9,8},{8,9},{11,10... | collective-permute-start | bytes 208904 | tf_op jit(solution)/shard_map/ppermute | solution.py:417
  17.0 0.9 %convert_element_type.24.refs_0_.refs_8_ = f32[272,128]{1,0:T(8,128)S(1)} convert(bf16[272,128]{1,0:T(8,128)(2,1)} %transform.1) | non-fusion elementwise | flops 34816 | bytes 208896 | tf_op jit(solution)/shard_map/convert_element_type | solution.py:433
  17.9 0.0 collective-permute-done.7.refs_9_
  17.9 0.0 collective-permute-done.refs_4_
  17.9 0.0 collective-permute-done.6.refs_7_
  17.9 2.0 %collective-permute-done.4.refs_6_ = bf16[272,128]{1,0:T(8,128)(2,1)S(1)} collective-permute-done((bf16[272,128]{1,0:T(8,128)(2,1)S(1)}, bf16[272,128]{1,0:T(8,128)(2,1)S(1)}, u32[]{:S(2)}, u32[]{:S(2)}) %collective-permute-start.4) | collective-permute-done | bytes 69664 | tf_op jit(solution)/shard_map/ppermute | solution.py:417
  19.9 0.8 %collective-permute-done.2.refs_5_ = bf16[272,128]{1,0:T(8,128)(2,1)S(1)} collective-permute-done((bf16[272,128]{1,0:T(8,128)(2,1)S(1)}, bf16[272,128]{1,0:T(8,128)(2,1)S(1)}, u32[]{:S(2)}, u32[]{:S(2)}) %collective-permute-start.2) | collective-permute-done | bytes 69664 | tf_op jit(solution)/shard_map/ppermute | solution.py:417
  20.9 0.4 %collective-permute-start.10 = (f32[1,128]{1,0:T(1,128)S(1)}, f32[1,128]{1,0:T(1,128)S(1)}, u32[]{:S(2)}, u32[]{:S(2)}) collective-permute-start(f32[1,128]{1,0:T(1,128)S(1)} %add_bitcast_fusion), channel_id=1, source_target_pairs={{24,0},{16,8},{8,16},{0,24},{25,1},{17,9},{9,17},{1,25},{26,2},{18... | collective-permute-start | bytes 1544 | tf_op jit(solution)/shard_map/ppermute | solution.py:447
  21.3 1.3 %collective-permute-start.9 = (f32[1,128]{1,0:T(1,128)S(1)}, f32[1,128]{1,0:T(1,128)S(1)}, u32[]{:S(2)}, u32[]{:S(2)}) collective-permute-start(f32[1,128]{1,0:T(1,128)S(1)} %add_bitcast_fusion), channel_id=1, source_target_pairs={{16,0},{24,8},{0,16},{8,24},{17,1},{25,9},{1,17},{9,25},{18,2},{26... | collective-permute-start | bytes 1544 | tf_op jit(solution)/shard_map/ppermute | solution.py:447
  22.6 0.3 %collective-permute-start.8 = (f32[1,128]{1,0:T(1,128)S(1)}, f32[1,128]{1,0:T(1,128)S(1)}, u32[]{:S(2)}, u32[]{:S(2)}) collective-permute-start(f32[1,128]{1,0:T(1,128)S(1)} %add_bitcast_fusion), channel_id=1, source_target_pairs={{8,0},{0,8},{24,16},{16,24},{9,1},{1,9},{25,17},{17,25},{10,2},{2,... | collective-permute-start | bytes 1544 | tf_op jit(solution)/shard_map/ppermute | solution.py:447
  22.8 0.2 collective-permute-start.11
  23.1 0.3 %collective-permute-start.12 = (bf16[272,128]{1,0:T(8,128)(2,1)S(1)}, bf16[272,128]{1,0:T(8,128)(2,1)S(1)}, u32[]{:S(2)}, u32[]{:S(2)}) collective-permute-start(bf16[272,128]{1,0:T(8,128)(2,1)S(1)} %collective-permute-done.7.refs_9_), channel_id=1, source_target_pairs={{8,0},{0,8},{9,1},{1,9},{10,2},{2,10},{11,3},{3,11},{12,4},{4,12},... | collective-permute-start | bytes 208904 | tf_op jit(solution)/shard_map/ppermute | solution.py:417
  23.3 0.6 %collective-permute-done.10 = f32[1,128]{1,0:T(1,128)S(1)} collective-permute-done((f32[1,128]{1,0:T(1,128)S(1)}, f32[1,128]{1,0:T(1,128)S(1)}, u32[]{:S(2)}, u32[]{:S(2)}) %collective-permute-start.10) | collective-permute-done | bytes 544 | tf_op jit(solution)/shard_map/ppermute | solution.py:447
  23.9 0.9 %collective-permute-done.9 = f32[1,128]{1,0:T(1,128)S(1)} collective-permute-done((f32[1,128]{1,0:T(1,128)S(1)}, f32[1,128]{1,0:T(1,128)S(1)}, u32[]{:S(2)}, u32[]{:S(2)}) %collective-permute-start.9) | collective-permute-done | bytes 544 | tf_op jit(solution)/shard_map/ppermute | solution.py:447
  24.8 0.0 collective-permute-done.8
  24.9 0.0 collective-permute-done.11.refs_10_
  24.9 0.0 collective-permute-done.12.refs_11_
  24.9 0.5 %pair_products.1.products = f32[32,8,32,128]{3,2,1,0:T(8,128)S(1)} custom-call(f32[272,128]{1,0:T(8,128)S(1)} %convert_element_type.24.refs_0_.refs_8_, bf16[272,128]{1,0:T(8,128)(2,1)S(1)} %collective-permute-done.1.refs_1_, bf16[272,128]{1,0:T(8,128)(2,1)S(1)} %collective-permute-done.3.refs_2_, bf16[272,128]{1,0:T(8,128)(2,1)S(1)} %collective-permute-done.5.refs_3_, ...), custom_call_target="tpu_custom_call" | custom-call | flops 4194304 | bytes 2097152 | tf_op jit(solution)/shard_map/pair_products/pallas_call | solution.py:334
  25.3 1.2 %stack.1 = f32[8,4,1,2,512]{4,3,2,1,0:T(2,128)} custom-call(f32[1,128]{1,0:T(1,128)S(1)} %add_add_fusion.energy, f32[32,8,32,128]{3,2,1,0:T(8,128)S(1)} %pair_products.1.products), custom_call_target="tpu_custom_call" | custom-call | flops 4194304 | bytes 2097152 | tf_op jit(solution)/shard_map/stack/pallas_call | solution.py:394
  (6 shorter events, 0.1 us)
Async XLA Ops:
  3.7 8.9 %collective-permute-start.5 = (bf16[272,128]{1,0:T(8,128)(2,1)}, bf16[272,128]{1,0:T(8,128)(2,1)S(1)}, u32[]{:S(2)}, u32[]{:S(2)}) collective-permute-start(bf16[272,128]{1,0:T(8,128)(2,1)} %transform.1), channel_id=1, source_target_pairs={{6,0},{4,2},{2,4},{0,6},{7,1},{5,3},{3,5},{1,7},{14,8},{12,10},{10... | collective-permute-start | bytes 208904 | tf_op jit(solution)/shard_map/ppermute | solution.py:417
  8.8 6.1 %collective-permute-start.3 = (bf16[272,128]{1,0:T(8,128)(2,1)}, bf16[272,128]{1,0:T(8,128)(2,1)S(1)}, u32[]{:S(2)}, u32[]{:S(2)}) collective-permute-start(bf16[272,128]{1,0:T(8,128)(2,1)} %transform.1), channel_id=1, source_target_pairs={{4,0},{6,2},{0,4},{2,6},{5,1},{7,3},{1,5},{3,7},{12,8},{14,10},{8,... | collective-permute-start | bytes 208904 | tf_op jit(solution)/shard_map/ppermute | solution.py:417
  8.8 7.6 %collective-permute-start.1 = (bf16[272,128]{1,0:T(8,128)(2,1)}, bf16[272,128]{1,0:T(8,128)(2,1)S(1)}, u32[]{:S(2)}, u32[]{:S(2)}) collective-permute-start(bf16[272,128]{1,0:T(8,128)(2,1)} %transform.1), channel_id=1, source_target_pairs={{2,0},{0,2},{6,4},{4,6},{3,1},{1,3},{7,5},{5,7},{10,8},{8,10},{14,... | collective-permute-start | bytes 208904 | tf_op jit(solution)/shard_map/ppermute | solution.py:417
  9.5 8.4 %collective-permute-start.7 = (bf16[272,128]{1,0:T(8,128)(2,1)}, bf16[272,128]{1,0:T(8,128)(2,1)S(1)}, u32[]{:S(2)}, u32[]{:S(2)}) collective-permute-start(bf16[272,128]{1,0:T(8,128)(2,1)} %transform.1), channel_id=1, source_target_pairs={{16,0},{0,16},{17,1},{1,17},{18,2},{2,18},{19,3},{3,19},{20,4},{4,... | collective-permute-start | bytes 208904 | tf_op jit(solution)/shard_map/ppermute | solution.py:417
  11.1 6.8 %collective-permute-start = (bf16[272,128]{1,0:T(8,128)(2,1)}, bf16[272,128]{1,0:T(8,128)(2,1)S(1)}, u32[]{:S(2)}, u32[]{:S(2)}) collective-permute-start(bf16[272,128]{1,0:T(8,128)(2,1)} %transform.1), channel_id=1, source_target_pairs={{1,0},{0,1},{3,2},{2,3},{5,4},{4,5},{7,6},{6,7},{9,8},{8,9},{11,10... | collective-permute-start | bytes 208904 | tf_op jit(solution)/shard_map/ppermute | solution.py:417
  12.7 5.3 %collective-permute-start.6 = (bf16[272,128]{1,0:T(8,128)(2,1)S(1)}, bf16[272,128]{1,0:T(8,128)(2,1)S(1)}, u32[]{:S(2)}, u32[]{:S(2)}) collective-permute-start(bf16[272,128]{1,0:T(8,128)(2,1)S(1)} %collective-permute-done.5.refs_3_), channel_id=1, source_target_pairs={{1,0},{0,1},{3,2},{2,3},{5,4},{4,5},{7,6},{6,7},{9,8},{8,9},{11,10... | collective-permute-start | bytes 208904 | tf_op jit(solution)/shard_map/ppermute | solution.py:417
  15.0 5.0 %collective-permute-start.4 = (bf16[272,128]{1,0:T(8,128)(2,1)S(1)}, bf16[272,128]{1,0:T(8,128)(2,1)S(1)}, u32[]{:S(2)}, u32[]{:S(2)}) collective-permute-start(bf16[272,128]{1,0:T(8,128)(2,1)S(1)} %collective-permute-done.3.refs_2_), channel_id=1, source_target_pairs={{1,0},{0,1},{3,2},{2,3},{5,4},{4,5},{7,6},{6,7},{9,8},{8,9},{11,10... | collective-permute-start | bytes 208904 | tf_op jit(solution)/shard_map/ppermute | solution.py:417
  16.5 4.3 %collective-permute-start.2 = (bf16[272,128]{1,0:T(8,128)(2,1)S(1)}, bf16[272,128]{1,0:T(8,128)(2,1)S(1)}, u32[]{:S(2)}, u32[]{:S(2)}) collective-permute-start(bf16[272,128]{1,0:T(8,128)(2,1)S(1)} %collective-permute-done.1.refs_1_), channel_id=1, source_target_pairs={{1,0},{0,1},{3,2},{2,3},{5,4},{4,5},{7,6},{6,7},{9,8},{8,9},{11,10... | collective-permute-start | bytes 208904 | tf_op jit(solution)/shard_map/ppermute | solution.py:417
  20.9 3.0 %collective-permute-start.10 = (f32[1,128]{1,0:T(1,128)S(1)}, f32[1,128]{1,0:T(1,128)S(1)}, u32[]{:S(2)}, u32[]{:S(2)}) collective-permute-start(f32[1,128]{1,0:T(1,128)S(1)} %add_bitcast_fusion), channel_id=1, source_target_pairs={{24,0},{16,8},{8,16},{0,24},{25,1},{17,9},{9,17},{1,25},{26,2},{18... | collective-permute-start | bytes 1544 | tf_op jit(solution)/shard_map/ppermute | solution.py:447
  21.3 3.5 %collective-permute-start.9 = (f32[1,128]{1,0:T(1,128)S(1)}, f32[1,128]{1,0:T(1,128)S(1)}, u32[]{:S(2)}, u32[]{:S(2)}) collective-permute-start(f32[1,128]{1,0:T(1,128)S(1)} %add_bitcast_fusion), channel_id=1, source_target_pairs={{16,0},{24,8},{0,16},{8,24},{17,1},{25,9},{1,17},{9,25},{18,2},{26... | collective-permute-start | bytes 1544 | tf_op jit(solution)/shard_map/ppermute | solution.py:447
  22.6 2.3 %collective-permute-start.8 = (f32[1,128]{1,0:T(1,128)S(1)}, f32[1,128]{1,0:T(1,128)S(1)}, u32[]{:S(2)}, u32[]{:S(2)}) collective-permute-start(f32[1,128]{1,0:T(1,128)S(1)} %add_bitcast_fusion), channel_id=1, source_target_pairs={{8,0},{0,8},{24,16},{16,24},{9,1},{1,9},{25,17},{17,25},{10,2},{2,... | collective-permute-start | bytes 1544 | tf_op jit(solution)/shard_map/ppermute | solution.py:447
  22.8 2.0 %collective-permute-start.11 = (bf16[272,128]{1,0:T(8,128)(2,1)}, bf16[272,128]{1,0:T(8,128)(2,1)S(1)}, u32[]{:S(2)}, u32[]{:S(2)}) collective-permute-start(bf16[272,128]{1,0:T(8,128)(2,1)} %transform.1), channel_id=1, source_target_pairs={{8,0},{0,8},{9,1},{1,9},{10,2},{2,10},{11,3},{3,11},{12,4},{4,12},... | collective-permute-start | bytes 208904 | tf_op jit(solution)/shard_map/ppermute | solution.py:417
  23.1 1.8 %collective-permute-start.12 = (bf16[272,128]{1,0:T(8,128)(2,1)S(1)}, bf16[272,128]{1,0:T(8,128)(2,1)S(1)}, u32[]{:S(2)}, u32[]{:S(2)}) collective-permute-start(bf16[272,128]{1,0:T(8,128)(2,1)S(1)} %collective-permute-done.7.refs_9_), channel_id=1, source_target_pairs={{8,0},{0,8},{9,1},{1,9},{10,2},{2,10},{11,3},{3,11},{12,4},{4,12},... | collective-permute-start | bytes 208904 | tf_op jit(solution)/shard_map/ppermute | solution.py:417
